TPU v7x, 32 devices: a whole 2x2x4 slice. The times are simulated.
32 devices in a mesh: ctx: 4 (over y, x), fsdp: 8 (over z, core).
Axes of the slice: x: 2, y: 2, z: 4, core: 2. Of those that a mesh axis runs over, the one named last changes fastest.
Arguments:
- inputs: bfloat16 [8, 1024, 2304], P('fsdp', 'ctx'), may hold values from -5 to 5
- positions: int32 [8, 1024], P('fsdp', 'ctx'), may hold values from 0 to 1023, as said below
- pre_attn_gain: bfloat16 [2304], P('fsdp'), may hold values from 0.099609375 to 1.8984375
- post_attn_gain: bfloat16 [2304], P('fsdp'), may hold values from 0.099609375 to 1.8984375
- pre_mlp_gain: bfloat16 [2304], P('fsdp'), may hold values from 0.099609375 to 1.8984375
- post_mlp_gain: bfloat16 [2304], P('fsdp'), may hold values from 0.099609375 to 1.8984375
- query_weight: bfloat16 [2304, 2048], P('fsdp'), may hold values from -1 to 1
- key_weight: bfloat16 [2304, 1024], P('fsdp'), may hold values from -1 to 1
- value_weight: bfloat16 [2304, 1024], P('fsdp'), may hold values from -0.125 to 0.125
- out_weight: bfloat16 [2048, 2304], P('fsdp'), may hold values from -0.125 to 0.125
- gate_weight: bfloat16 [2304, 9216], P('fsdp'), may hold values from -0.125 to 0.125
- up_weight: bfloat16 [2304, 9216], P('fsdp'), may hold values from -0.125 to 0.125
- down_weight: bfloat16 [9216, 2304], P('fsdp'), may hold values from -0.0625 to 0.0625
- cotangent: bfloat16 [8, 1024, 2304], P('fsdp', 'ctx'), may hold values from -6 to 6
Outputs:
- output: bfloat16 [8, 1024, 2304], P('fsdp', 'ctx')
- input_grad: bfloat16 [8, 1024, 2304], P('fsdp', 'ctx')
- pre_attn_gain_grad: float32 [2304], P('fsdp')
- post_attn_gain_grad: float32 [2304], P('fsdp')
- pre_mlp_gain_grad: float32 [2304], P('fsdp')
- post_mlp_gain_grad: float32 [2304], P('fsdp')
- query_weight_grad: float32 [2304, 2048], P('fsdp')
- key_weight_grad: float32 [2304, 1024], P('fsdp')
- value_weight_grad: float32 [2304, 1024], P('fsdp')
- out_weight_grad: float32 [2048, 2304], P('fsdp')
- gate_weight_grad: float32 [2304, 9216], P('fsdp')
- up_weight_grad: float32 [2304, 9216], P('fsdp')
- down_weight_grad: float32 [9216, 2304], P('fsdp')
Inputs may be any that keep to these rules, and one draw needn't show every extreme that they name: Each row is a permutation of the positions of one sequence. The 256 tokens held by one index c of ctx are two runs of 128 consecutive positions, blocks b and 2 n - 1 - b of the sequence (n the number of ctx indices), with b a permutation of the ctx indices drawn for each sequence.
All inputs are finite; a program needn't handle non-finite values.
Results may differ from a plain program's by a relative error of at most 0.029.
Values may be sent and summed in bfloat16 or wider, within the bound.
No kernel may reach another device: no remote copies, remote signals or barrier semaphores. Data moves between devices by JAX's collectives and lax.ppermute only.
A program may use at most 576 MiB of HBM per device.

v0:
```python
from functools import partial

import jax
import jax.numpy as jnp
from jax import lax
from jax.sharding import PartitionSpec as P

HQ = 8
KV = 4
HD = 256


soft_cap = 50.0
epsilon = 1e-06
rope_base = 10000.0
masked_fill = -1e30
highest = lax.Precision.HIGHEST


def shifted(shard, axis, by):
    size = lax.axis_size(axis)
    return lax.ppermute(shard, axis, [(i, (i + by) % size) for i in range(size)])


def frequencies(half, head_dim):
    return rope_base ** (-(jnp.arange(half, dtype=jnp.float32) * 2.0) / head_dim)


def rotate(vectors, angles):
    half = vectors.shape[-1] // 2
    first = vectors[..., :half]
    second = vectors[..., half:]
    cosine = jnp.cos(angles)[..., None, :]
    sine = jnp.sin(angles)[..., None, :]
    return jnp.concatenate(
        [first * cosine - second * sine, second * cosine + first * sine], axis=-1
    )


def unrotate(grads, angles):
    half = grads.shape[-1] // 2
    first = grads[..., :half]
    second = grads[..., half:]
    cosine = jnp.cos(angles)[..., None, :]
    sine = jnp.sin(angles)[..., None, :]
    return jnp.concatenate(
        [first * cosine + second * sine, second * cosine - first * sine], axis=-1
    )


def inverse_rms(vectors):
    return lax.rsqrt(jnp.mean(vectors * vectors, axis=-1, keepdims=True) + epsilon)


def norm_back(vectors, inverse, gain, upstream):
    scaled = upstream * gain
    unit = vectors * inverse
    grad_vectors = inverse * (scaled - unit * jnp.mean(unit * scaled, axis=-1, keepdims=True))
    return (grad_vectors, jnp.sum(upstream * unit, axis=0))


def contract_last(left, right):
    return lax.dot_general(
        left, right, (((1,), (1,)), ((), ())), preferred_element_type=jnp.float32
    )


def contract_first(left, right):
    return lax.dot_general(
        left, right, (((0,), (0,)), ((), ())), preferred_element_type=jnp.float32
    )


def per_device(
    inputs,
    positions,
    pre_attn_gain,
    post_attn_gain,
    pre_mlp_gain,
    post_mlp_gain,
    query_weight,
    key_weight,
    value_weight,
    out_weight,
    gate_weight,
    up_weight,
    down_weight,
    cotangent,
):
    rows = inputs[0].astype(jnp.float32)
    query_pos = positions[0]
    tokens = rows.shape[0]
    head_dim = HD
    query_heads = HQ
    kv_heads = KV
    groups = query_heads // kv_heads
    scale = head_dim ** (-0.5)
    cycle_size = lax.axis_size("ctx")
    angles = query_pos.astype(jnp.float32)[:, None] * frequencies(head_dim // 2, head_dim)
    gathered = (
        lax.all_gather(pre_attn_gain, "fsdp", axis=0, tiled=True),
        lax.all_gather(post_attn_gain, "fsdp", axis=0, tiled=True),
        lax.all_gather(pre_mlp_gain, "fsdp", axis=0, tiled=True),
        lax.all_gather(post_mlp_gain, "fsdp", axis=0, tiled=True),
        lax.all_gather(query_weight, "fsdp", axis=0, tiled=True),
        lax.all_gather(key_weight, "fsdp", axis=0, tiled=True),
        lax.all_gather(value_weight, "fsdp", axis=0, tiled=True),
        lax.all_gather(out_weight, "fsdp", axis=0, tiled=True),
    )
    gain_a = gathered[0].astype(jnp.float32)
    gain_b = gathered[1].astype(jnp.float32)
    gain_c = gathered[2].astype(jnp.float32)
    gain_d = gathered[3].astype(jnp.float32)
    full_query, full_key, full_value, full_out = (
        gathered[4],
        gathered[5],
        gathered[6],
        gathered[7],
    )
    inverse_a = inverse_rms(rows)
    normed = (rows * inverse_a * gain_a).astype(jnp.bfloat16)
    query_lin = jnp.dot(normed, full_query, preferred_element_type=jnp.float32)
    key_lin = jnp.dot(normed, full_key, preferred_element_type=jnp.float32)
    value_lin = jnp.dot(normed, full_value, preferred_element_type=jnp.float32)
    queries = (rotate(query_lin.reshape(tokens, query_heads, head_dim), angles) * scale).astype(
        jnp.bfloat16
    )
    keys = rotate(key_lin.reshape(tokens, kv_heads, head_dim), angles).astype(jnp.bfloat16)
    values = value_lin.reshape(tokens, kv_heads, head_dim).astype(jnp.bfloat16)
    query_groups = queries.reshape(tokens, kv_heads, groups, head_dim)
    top = jnp.full((kv_heads, groups, tokens), masked_fill, jnp.float32)
    piece_keys = lax.all_gather(keys, "ctx", axis=0, tiled=True)
    piece_values = lax.all_gather(values, "ctx", axis=0, tiled=True)
    piece_pos = lax.all_gather(query_pos, "ctx", axis=0, tiled=True)
    raw = jnp.einsum("tkgd,rkd->kgtr", query_groups, piece_keys, preferred_element_type=jnp.float32)
    capped = soft_cap * jnp.tanh(raw / soft_cap)
    allowed = piece_pos[None, :] <= query_pos[:, None]
    capped = jnp.where(allowed, capped, masked_fill)
    new_top = jnp.maximum(top, jnp.max(capped, axis=-1))
    probs = jnp.where(allowed, jnp.exp(capped - new_top[..., None]), 0.0)
    total = jnp.sum(probs, axis=-1)
    accum = jnp.einsum("kgtr,rkd->kgtd", probs, piece_values.astype(jnp.float32), precision=highest)
    top, total, accum = (new_top, total, accum)
    log_total = top + jnp.log(total)
    attn_groups = jnp.transpose(accum / total[..., None], (2, 0, 1, 3))
    attn_low = attn_groups.reshape(tokens, query_heads * head_dim).astype(jnp.bfloat16)
    branch = jnp.dot(attn_low, full_out, preferred_element_type=jnp.float32)
    inverse_b = inverse_rms(branch)
    middle = rows + branch * inverse_b * gain_b
    inverse_c = inverse_rms(middle)
    normed_mlp = (middle * inverse_c * gain_c).astype(jnp.bfloat16)
    full_gate, full_up, full_down = (
        lax.all_gather(gate_weight, "fsdp", axis=0, tiled=True),
        lax.all_gather(up_weight, "fsdp", axis=0, tiled=True),
        lax.all_gather(down_weight, "fsdp", axis=0, tiled=True),
    )
    gate = jnp.dot(normed_mlp, full_gate, preferred_element_type=jnp.float32)
    up = jnp.dot(normed_mlp, full_up, preferred_element_type=jnp.float32)
    activated = jax.nn.gelu(gate, approximate=True)
    hidden = (activated * up).astype(jnp.bfloat16)
    down = jnp.dot(hidden, full_down, preferred_element_type=jnp.float32)
    inverse_d = inverse_rms(down)
    result = middle + down * inverse_d * gain_d
    output = result.astype(jnp.bfloat16)[None]
    grad_result = cotangent[0].astype(jnp.float32)
    grad_down, grad_gain_d = norm_back(down, inverse_d, gain_d, grad_result)
    grad_down_low = grad_down.astype(jnp.bfloat16)
    grad_hidden = contract_last(grad_down_low, full_down)
    grad_gate = jax.vjp(partial(jax.nn.gelu, approximate=True), gate)[1](grad_hidden * up)[0]
    grad_mlp = jnp.concatenate([grad_gate, grad_hidden * activated], axis=1).astype(jnp.bfloat16)
    hidden_units = gate.shape[1]
    grad_normed_mlp = contract_last(grad_mlp[:, :hidden_units], full_gate) + contract_last(
        grad_mlp[:, hidden_units:], full_up
    )
    grad_middle_mlp, grad_gain_c = norm_back(middle, inverse_c, gain_c, grad_normed_mlp)
    grad_middle = grad_result + grad_middle_mlp
    grad_branch, grad_gain_b = norm_back(branch, inverse_b, gain_b, grad_middle)
    grad_branch_low = grad_branch.astype(jnp.bfloat16)
    grad_attn_low = (
        contract_last(grad_branch_low, full_out)
        .astype(jnp.bfloat16)
        .reshape(tokens, kv_heads, groups, head_dim)
    )
    grad_attn_wide = grad_attn_low.astype(jnp.float32)
    delta = jnp.transpose(jnp.sum(grad_attn_wide * attn_groups, axis=-1), (1, 2, 0))

    def block_back(piece_keys, piece_values, piece_pos):
        raw = jnp.einsum(
            "tkgd,rkd->kgtr", query_groups, piece_keys, preferred_element_type=jnp.float32
        )
        bent = jnp.tanh(raw / soft_cap)
        allowed = piece_pos[None, :] <= query_pos[:, None]
        probs = jnp.where(allowed, jnp.exp(soft_cap * bent - log_total[..., None]), 0.0)
        grad_probs = jnp.einsum(
            "tkgd,rkd->kgtr", grad_attn_low, piece_values, preferred_element_type=jnp.float32
        )
        grad_raw = (probs * (grad_probs - delta[..., None]) * (1.0 - bent * bent)).astype(
            jnp.bfloat16
        )
        query_add = jnp.einsum(
            "kgtr,rkd->tkgd", grad_raw, piece_keys, preferred_element_type=jnp.float32
        )
        key_add = jnp.einsum(
            "kgtr,tkgd->rkd", grad_raw, query_groups, preferred_element_type=jnp.float32
        )
        value_add = jnp.einsum("kgtr,tkgd->rkd", probs, grad_attn_wide, precision=highest)
        return (query_add, key_add, value_add)

    zero_query = jnp.zeros((tokens, kv_heads, groups, head_dim), jnp.float32)

    def cycle_turn(turn, state):
        grad_query, piece_keys, piece_values, piece_pos, grad_keys, grad_values = state
        query_add, key_add, value_add = block_back(piece_keys, piece_values, piece_pos)
        grad_keys, grad_values = (
            shifted((grad_keys + key_add).astype(jnp.bfloat16), "ctx", 1).astype(jnp.float32),
            shifted((grad_values + value_add).astype(jnp.bfloat16), "ctx", 1).astype(jnp.float32),
        )
        piece_keys, piece_values, piece_pos = shifted(
            (piece_keys, piece_values, piece_pos), "ctx", 1
        )
        return (grad_query + query_add, piece_keys, piece_values, piece_pos, grad_keys, grad_values)

    zero_keys = jnp.zeros((tokens, kv_heads, head_dim), jnp.float32)
    state = lax.fori_loop(
        0, cycle_size, cycle_turn, (zero_query, keys, values, query_pos, zero_keys, zero_keys)
    )
    grad_query, grad_keys, grad_values = (state[0], state[4], state[5])
    grad_query_lin = (
        unrotate(grad_query.reshape(tokens, query_heads, head_dim) * scale, angles)
        .reshape(tokens, query_heads * head_dim)
        .astype(jnp.bfloat16)
    )
    grad_key_lin = (
        unrotate(grad_keys, angles).reshape(tokens, kv_heads * head_dim).astype(jnp.bfloat16)
    )
    grad_value_lin = grad_values.reshape(tokens, kv_heads * head_dim).astype(jnp.bfloat16)
    grad_normed = (
        contract_last(grad_query_lin, full_query)
        + contract_last(grad_key_lin, full_key)
        + contract_last(grad_value_lin, full_value)
    )
    grad_rows, grad_gain_a = norm_back(rows, inverse_a, gain_a, grad_normed)
    input_grad = (grad_middle + grad_rows).astype(jnp.bfloat16)[None]
    projections = jnp.concatenate([grad_query_lin, grad_key_lin, grad_value_lin], axis=1)
    down_shard = lax.psum_scatter(
        contract_first(hidden, grad_down_low).astype(jnp.bfloat16),
        "fsdp",
        scatter_dimension=0,
        tiled=True,
    )
    projection_sums = lax.psum_scatter(
        contract_first(normed, projections).astype(jnp.bfloat16),
        "fsdp",
        scatter_dimension=0,
        tiled=True,
    )
    feed_sums = lax.psum_scatter(
        contract_first(normed_mlp, grad_mlp).astype(jnp.bfloat16),
        "fsdp",
        scatter_dimension=0,
        tiled=True,
    )
    out_term = contract_first(attn_low, grad_branch_low)
    out_shard, gain_a_shard, gain_b_shard, gain_c_shard, gain_d_shard = (
        lax.psum_scatter(
            out_term.astype(jnp.bfloat16), "fsdp", scatter_dimension=0, tiled=True
        ).astype(jnp.float32),
        lax.psum_scatter(
            grad_gain_a.astype(jnp.bfloat16), "fsdp", scatter_dimension=0, tiled=True
        ).astype(jnp.float32),
        lax.psum_scatter(
            grad_gain_b.astype(jnp.bfloat16), "fsdp", scatter_dimension=0, tiled=True
        ).astype(jnp.float32),
        lax.psum_scatter(
            grad_gain_c.astype(jnp.bfloat16), "fsdp", scatter_dimension=0, tiled=True
        ).astype(jnp.float32),
        lax.psum_scatter(
            grad_gain_d.astype(jnp.bfloat16), "fsdp", scatter_dimension=0, tiled=True
        ).astype(jnp.float32),
    )
    totals = (
        lax.psum(projection_sums, "ctx").astype(jnp.float32),
        lax.psum(feed_sums, "ctx").astype(jnp.float32),
        lax.psum(out_shard.astype(jnp.bfloat16), "ctx").astype(jnp.float32),
        lax.psum(down_shard, "ctx").astype(jnp.float32),
        lax.psum(gain_a_shard.astype(jnp.bfloat16), "ctx").astype(jnp.float32),
        lax.psum(gain_b_shard.astype(jnp.bfloat16), "ctx").astype(jnp.float32),
        lax.psum(gain_c_shard.astype(jnp.bfloat16), "ctx").astype(jnp.float32),
        lax.psum(gain_d_shard.astype(jnp.bfloat16), "ctx").astype(jnp.float32),
    )
    query_columns = query_heads * head_dim
    key_columns = kv_heads * head_dim
    projection_total = totals[0]
    feed_total = totals[1]
    return (
        output,
        input_grad,
        totals[4],
        totals[5],
        totals[6],
        totals[7],
        projection_total[:, :query_columns],
        projection_total[:, query_columns : query_columns + key_columns],
        projection_total[:, query_columns + key_columns :],
        totals[2],
        feed_total[:, :hidden_units],
        feed_total[:, hidden_units:],
        totals[3],
    )


def solution(mesh):
    return jax.shard_map(
        per_device,
        mesh=mesh,
        in_specs=(
            P("fsdp", "ctx", None),
            P("fsdp", "ctx"),
            P("fsdp"),
            P("fsdp"),
            P("fsdp"),
            P("fsdp"),
            P("fsdp", None),
            P("fsdp", None),
            P("fsdp", None),
            P("fsdp", None),
            P("fsdp", None),
            P("fsdp", None),
            P("fsdp", None),
            P("fsdp", "ctx", None),
        ),
        out_specs=(
            P("fsdp", "ctx", None),
            P("fsdp", "ctx", None),
            P("fsdp"),
            P("fsdp"),
            P("fsdp"),
            P("fsdp"),
            P("fsdp", None),
            P("fsdp", None),
            P("fsdp", None),
            P("fsdp", None),
            P("fsdp", None),
            P("fsdp", None),
            P("fsdp", None),
        ),
        check_vma=False,
    )
```

profile of v0, /device:TPU:0, one launch (start us, length us, event | category | flops | bytes accessed | tf_op | source)
XLA Modules:
  0.0 3614.6 jit_solution(7156684153204010968)
XLA Ops:
  11.8 31.5 all-reduce.10
  44.2 20.3 all-gather.11.cloned.1.call-done
  64.6 6.6 copy.61
  76.4 40.3 %all-gather.17.cloned.1.call-done = bf16[2304,1024]{1,0:T(8,128)(2,1)} async-done(((bf16[288,1024]{1,0:T(8,128)(2,1)}), bf16[2304,1024]{1,0:T(8,128)(2,1)}) %all-gather.17.cloned.1.call-update) | async-done | bytes 4718608 | tf_op jit(solution)/shard_map/all_gather | solution.py:107
  116.7 6.6 copy.66
  123.3 5.1 convolution_convert_fusion.5
  132.6 8.0 all-gather
  140.8 67.2 %all-gather.15.cloned.1.call-done = bf16[2304,2048]{1,0:T(8,128)(2,1)} async-done(((bf16[288,2048]{1,0:T(8,128)(2,1)}), bf16[2304,2048]{1,0:T(8,128)(2,1)}) %all-gather.15.cloned.1.call-update) | async-done | bytes 9437200 | tf_op jit(solution)/shard_map/all_gather | solution.py:105
  207.9 12.7 copy.62
  220.6 5.4 fusion.95
  231.6 11.7 all-gather.13.cloned.1.call-done
  253.5 26.8 all-gather.19.cloned.1.call-done
  280.3 12.2 fusion.103
  292.5 80.1 %all-gather.21.cloned.1.call-done = bf16[2048,2304]{1,0:T(8,128)(2,1)} async-done(((bf16[256,2304]{1,0:T(8,128)(2,1)}), bf16[2048,2304]{1,0:T(8,128)(2,1)}) %all-gather.21.cloned.1.call-update) | async-done | bytes 9437200 | tf_op jit(solution)/shard_map/all_gather | solution.py:108
  372.6 6.4 multiply_reduce_fusion.6
  381.3 354.6 %all-gather.23.cloned.1.call-done = bf16[2304,9216]{1,0:T(8,128)(2,1)} async-done(((bf16[288,9216]{1,0:T(8,128)(2,1)}), bf16[2304,9216]{1,0:T(8,128)(2,1)}) %all-gather.23.cloned.1.call-update) | async-done | bytes 42467344 | tf_op jit(solution)/shard_map/all_gather | solution.py:153
  735.9 26.0 fusion.104
  761.9 337.4 %all-gather.25.cloned.1.call-done = bf16[2304,9216]{1,0:T(8,128)(2,1)} async-done(((bf16[288,9216]{1,0:T(8,128)(2,1)}), bf16[2304,9216]{1,0:T(8,128)(2,1)}) %all-gather.25.cloned.1.call-update) | async-done | bytes 42467344 | tf_op jit(solution)/shard_map/all_gather | solution.py:154
  1099.3 30.9 multiply_convert_fusion.1
  1130.2 332.5 %all-gather.27.cloned.1.call-done = bf16[9216,2304]{1,0:T(8,128)(2,1)} async-done(((bf16[1152,2304]{1,0:T(8,128)(2,1)}), bf16[9216,2304]{1,0:T(8,128)(2,1)}) %all-gather.27.cloned.1.call-update) | async-done | bytes 42467344 | tf_op jit(solution)/shard_map/all_gather | solution.py:155
  1462.7 19.4 multiply_reduce_fusion.4
  1485.9 27.6 multiply_convert_fusion
  1513.5 20.3 fusion.105
  1533.7 21.8 multiply_reduce_fusion
  1563.3 5.1 convolution_convert_fusion.3
  1569.7 7.6 convolution_convert_fusion.4
  1583.9 219.1 %while.21 = (s32[]{:T(128)}, f32[256,4,2,256]{3,0,2,1:T(8,128)}, bf16[256,4,256]{2,0,1:T(8,128)(2,1)S(1)}, bf16[256,4,256]{2,0,1:T(8,128)(2,1)S(1)}, s32[256]{0:...) while((s32[]{:T(128)}, f32[256,4,2,256]{3,0,2,1:T(8,128)}, ...), condition=%wide.region_11.12_spmd.clone, body=%wide.region_10.11_spmd.clone.sunk | while | flops 2694905856 | bytes 54231476 | solution.py:224
  1609.2 9.0 collective-permute-done.4
  1619.2 20.7 collective-permute-done.2
  1665.3 9.0 collective-permute-done.4
  1675.4 19.9 collective-permute-done.2
  1720.6 9.0 collective-permute-done.4
  1730.7 18.9 collective-permute-done.2
  1774.9 9.0 collective-permute-done.4
  1785.0 18.0 collective-permute-done.2
  1814.2 10.7 convolution_convert_fusion.2
  1826.2 21.4 convolution_convert_fusion.1
  1848.8 35.3 convolution_convert_fusion
  1884.3 126.1 %reduce-scatter.7.cloned.1.call-done = bf16[288,4096]{1,0:T(8,128)(2,1)} async-done(((bf16[2304,4096]{1,0:T(8,128)(2,1)}), bf16[288,4096]{1,0:T(8,128)(2,1)}) %reduce-scatter.7.cloned.1.call-update) | async-done | bytes 2359312 | tf_op jit(solution)/shard_map/reduce_scatter | solution.py:251
  2010.5 409.9 %reduce-scatter.11.cloned.1.call-done = bf16[1152,2304]{1,0:T(8,128)(2,1)} async-done(((bf16[9216,2304]{1,0:T(8,128)(2,1)}), bf16[1152,2304]{1,0:T(8,128)(2,1)}) %reduce-scatter.11.cloned.1.call-update) | async-done | bytes 5308432 | tf_op jit(solution)/shard_map/reduce_scatter | solution.py:245
  2420.3 808.3 %reduce-scatter.13.cloned.1.call-done = bf16[288,18432]{1,0:T(8,128)(2,1)} async-done(((bf16[2304,18432]{1,0:T(8,128)(2,1)}), bf16[288,18432]{1,0:T(8,128)(2,1)}) %reduce-scatter.13.cloned.1.call-update) | async-done | bytes 10616848
  3229.9 6.3 fusion.106
  3240.7 6.4 fusion.65
  3247.1 27.1 all-reduce.9
  3279.6 11.1 all-reduce.11
  3299.7 285.3 %all-reduce.15.cloned.1.call-done = (bf16[288,4096]{1,0:T(8,128)(2,1)}, bf16[256,2304]{1,0:T(8,128)(2,1)}, bf16[288,18432]{1,0:T(8,128)(2,1)}, bf16[1152,2304]{1,0:T(8,128)(2,1)}) async-done(((bf16[288,4096]{1,0:T(8,128)(2,1)}, bf16[256,2304]{1,0:T(8,128)(2,1)}, bf16[288,18432]{1,0:T(8,128)(2,1)}, bf16[1152,2304]{1,0:T(8,128)(2,1)}), (bf16[288,4096]{1,0:T(8,128)(2,1)}, bf16[256,2304]{1,0:T(8,128)(2,1)}, ...) | async-done | bytes 19464208 | tf_op jit(solution)/shard_map/psum | solution.py:282
  3594.8 8.1 fusion.100
  3602.9 4.9 convert_element_type.217
  (309 shorter events, 199.6 us)
Async XLA Ops:
  7.2 36.1 copy-start.40
  7.2 36.1 copy-start.10
  7.3 57.3 %all-gather.11.cloned.1.call-start = ((), (), s32[]{:S(2)}) async-start(), calls=%async_computation.4 | async-start | bytes 5308416 | tf_op jit(solution)/shard_map/all_gather | solution.py:106
  8.0 108.7 %all-gather.17.cloned.1.call-start = ((), (), s32[]{:S(2)}) async-start(), calls=%async_computation.7 | async-start | bytes 5308416 | tf_op jit(solution)/shard_map/all_gather | solution.py:107
  8.7 199.2 %all-gather.15.cloned.1.call-start = ((), (), s32[]{:S(2)}) async-start(), calls=%async_computation.6 | async-start | bytes 10616832 | tf_op jit(solution)/shard_map/all_gather | solution.py:105
  9.5 233.8 %all-gather.13.cloned.1.call-start = ((), (), s32[]{:S(2)}) async-start(), calls=%async_computation.5 | async-start | bytes 2621440 | tf_op jit(solution)/shard_map/all_gather | solution.py:132
  43.3 177.3 %copy-start.32 = (f32[2304]{0:T(1024)}, f32[2304]{0:T(1024)S(1)}, u32[]{:S(2)}) copy-start(f32[2304]{0:T(1024)S(1)} %convert_element_type.176) | copy-start | bytes 27652
  43.7 176.9 %copy-start.38 = (f32[256]{0:T(256)}, f32[256]{0:T(256)S(1)}, u32[]{:S(2)}) copy-start(f32[256]{0:T(256)S(1)} %add_rsqrt_fusion.3) | copy-start | bytes 3076
  44.2 181.8 %copy-start.28 = (f32[256,128]{0,1:T(8,128)}, f32[256,128]{0,1:T(8,128)S(1)}, u32[]{:S(2)}) copy-start(f32[256,128]{0,1:T(8,128)S(1)} %get-tuple-element.235) | copy-start | bytes 393220
  44.2 181.8 %copy-start.30 = (f32[256,128]{0,1:T(8,128)}, f32[256,128]{0,1:T(8,128)S(1)}, u32[]{:S(2)}) copy-start(f32[256,128]{0,1:T(8,128)S(1)} %get-tuple-element.236) | copy-start | bytes 393220
  76.4 204.0 %all-gather.19.cloned.1.call-start = ((), (), s32[]{:S(2)}) async-start(), calls=%async_computation.8 | async-start | bytes 2621440 | tf_op jit(solution)/shard_map/all_gather | solution.py:133
  128.5 244.1 %all-gather.21.cloned.1.call-start = ((), (), s32[]{:S(2)}) async-start(), calls=%async_computation.9 | async-start | bytes 10616832 | tf_op jit(solution)/shard_map/all_gather | solution.py:108
  129.1 606.8 %all-gather.23.cloned.1.call-start = ((), (), s32[]{:S(2)}) async-start(), calls=%async_computation.10 | async-start | bytes 47775744 | tf_op jit(solution)/shard_map/all_gather | solution.py:153
  129.8 969.5 %all-gather.25.cloned.1.call-start = ((), (), s32[]{:S(2)}) async-start(), calls=%async_computation.11 | async-start | bytes 47775744 | tf_op jit(solution)/shard_map/all_gather | solution.py:154
  130.6 1332.1 %all-gather.27.cloned.1.call-start = ((), (), s32[]{:S(2)}) async-start(), calls=%async_computation.12 | async-start | bytes 47775744 | tf_op jit(solution)/shard_map/all_gather | solution.py:155
  131.3 1753.0 %reduce-scatter.9.cloned.1.call-start = ((), (), s32[]{:S(2)}) async-start(), calls=%async_computation.14 | async-start | bytes 10616832 | tf_op jit(solution)/shard_map/reduce_scatter | solution.py:265
  131.4 247.7 %copy-start.34 = (f32[2304]{0:T(1024)}, f32[2304]{0:T(1024)S(1)}, u32[]{:S(2)}) copy-start(f32[2304]{0:T(1024)S(1)} %convert_element_type.184) | copy-start | bytes 27652
  253.5 39.0 %copy-start.44 = (f32[4,2,256]{2,1,0:T(2,128)}, f32[4,2,256]{2,1,0:T(2,128)S(1)}, u32[]{:S(2)}) copy-start(f32[4,2,256]{2,1,0:T(2,128)S(1)} %fusion.39) | copy-start | bytes 24580
  292.5 86.5 %copy-start.18 = (bf16[256,4,2,256]{0,3,2,1:T(8,128)(2,1)}, bf16[256,4,2,256]{0,3,2,1:T(8,128)(2,1)S(1)}, u32[]{:S(2)}) copy-start(bf16[256,4,2,256]{0,3,2,1:T(8,128)(2,1)S(1)} %get-tuple-element.241) | copy-start | bytes 3145732
  381.3 718.0 %copy-start.24 = (bf16[256,2304]{1,0:T(8,128)(2,1)}, bf16[256,2304]{1,0:T(8,128)(2,1)S(1)}, u32[]{:S(2)}) copy-start(bf16[256,2304]{1,0:T(8,128)(2,1)S(1)} %multiply_convert_fusion.3) | copy-start | bytes 3538948
  1462.7 19.4 copy-start.37
  1533.7 22.5 copy-start.35
  1533.7 22.5 copy-start.47
  1568.5 442.0 %reduce-scatter.7.cloned.1.call-start = ((), (), s32[]{:S(2)}) async-start(), calls=%async_computation.13 | async-start | bytes 21233664 | tf_op jit(solution)/shard_map/reduce_scatter | solution.py:251
  1591.1 16.0 collective-permute-start.3
  1595.8 22.4 collective-permute-start.4
  1597.2 42.7 %collective-permute-start = (bf16[256,4,256]{2,0,1:T(8,128)(2,1)}, bf16[256,4,256]{2,0,1:T(8,128)(2,1)S(1)}, u32[]{:S(2)}, u32[]{:S(2)}) collective-permute-start(bf16[256,4,256]{2,0,1:T(8,128)(2,1)} %copy.102), channel_id=1, source_target_pairs={{0,8},{8,16},{16,24},{24,0},{1,9},{9,17},{17,25},{25,1},{2,10},{10... | collective-permute-start | bytes 1572872 | tf_op jit(solution)/shard_map/while/body/eval_jaxpr/ppermute | solution.py:22
  1598.8 41.2 %collective-permute-start.1 = (bf16[256,4,256]{2,0,1:T(8,128)(2,1)}, bf16[256,4,256]{2,0,1:T(8,128)(2,1)S(1)}, u32[]{:S(2)}, u32[]{:S(2)}) collective-permute-start(bf16[256,4,256]{2,0,1:T(8,128)(2,1)} %copy.103), channel_id=1, source_target_pairs={{0,8},{8,16},{16,24},{24,0},{1,9},{9,17},{17,25},{25,1},{2,10},{10... | collective-permute-start | bytes 1572872 | tf_op jit(solution)/shard_map/while/body/eval_jaxpr/ppermute | solution.py:22
  1599.6 40.4 %collective-permute-start.2 = (s32[256]{0:T(256)S(1)}, s32[256]{0:T(256)S(1)}, u32[]{:S(2)}, u32[]{:S(2)}) collective-permute-start(s32[256]{0:T(256)S(1)} %copy.104), channel_id=1, source_target_pairs={{0,8},{8,16},{16,24},{24,0},{1,9},{9,17},{17,25},{25,1},{2,10},{10... | collective-permute-start | bytes 3080 | tf_op jit(solution)/shard_map/while/body/eval_jaxpr/ppermute | solution.py:22
  1647.1 16.1 collective-permute-start.3
  1651.4 22.9 collective-permute-start.4
  1653.4 41.9 %collective-permute-start = (bf16[256,4,256]{2,0,1:T(8,128)(2,1)}, bf16[256,4,256]{2,0,1:T(8,128)(2,1)S(1)}, u32[]{:S(2)}, u32[]{:S(2)}) collective-permute-start(bf16[256,4,256]{2,0,1:T(8,128)(2,1)} %copy.102), channel_id=1, source_target_pairs={{0,8},{8,16},{16,24},{24,0},{1,9},{9,17},{17,25},{25,1},{2,10},{10... | collective-permute-start | bytes 1572872 | tf_op jit(solution)/shard_map/while/body/eval_jaxpr/ppermute | solution.py:22
  1654.1 41.2 %collective-permute-start.1 = (bf16[256,4,256]{2,0,1:T(8,128)(2,1)}, bf16[256,4,256]{2,0,1:T(8,128)(2,1)S(1)}, u32[]{:S(2)}, u32[]{:S(2)}) collective-permute-start(bf16[256,4,256]{2,0,1:T(8,128)(2,1)} %copy.103), channel_id=1, source_target_pairs={{0,8},{8,16},{16,24},{24,0},{1,9},{9,17},{17,25},{25,1},{2,10},{10... | collective-permute-start | bytes 1572872 | tf_op jit(solution)/shard_map/while/body/eval_jaxpr/ppermute | solution.py:22
  1655.6 39.7 %collective-permute-start.2 = (s32[256]{0:T(256)S(1)}, s32[256]{0:T(256)S(1)}, u32[]{:S(2)}, u32[]{:S(2)}) collective-permute-start(s32[256]{0:T(256)S(1)} %copy.104), channel_id=1, source_target_pairs={{0,8},{8,16},{16,24},{24,0},{1,9},{9,17},{17,25},{25,1},{2,10},{10... | collective-permute-start | bytes 3080 | tf_op jit(solution)/shard_map/while/body/eval_jaxpr/ppermute | solution.py:22
  1702.4 16.1 collective-permute-start.3
  1706.7 22.9 collective-permute-start.4
  1708.8 40.8 %collective-permute-start = (bf16[256,4,256]{2,0,1:T(8,128)(2,1)}, bf16[256,4,256]{2,0,1:T(8,128)(2,1)S(1)}, u32[]{:S(2)}, u32[]{:S(2)}) collective-permute-start(bf16[256,4,256]{2,0,1:T(8,128)(2,1)} %copy.102), channel_id=1, source_target_pairs={{0,8},{8,16},{16,24},{24,0},{1,9},{9,17},{17,25},{25,1},{2,10},{10... | collective-permute-start | bytes 1572872 | tf_op jit(solution)/shard_map/while/body/eval_jaxpr/ppermute | solution.py:22
  1709.5 40.1 %collective-permute-start.1 = (bf16[256,4,256]{2,0,1:T(8,128)(2,1)}, bf16[256,4,256]{2,0,1:T(8,128)(2,1)S(1)}, u32[]{:S(2)}, u32[]{:S(2)}) collective-permute-start(bf16[256,4,256]{2,0,1:T(8,128)(2,1)} %copy.103), channel_id=1, source_target_pairs={{0,8},{8,16},{16,24},{24,0},{1,9},{9,17},{17,25},{25,1},{2,10},{10... | collective-permute-start | bytes 1572872 | tf_op jit(solution)/shard_map/while/body/eval_jaxpr/ppermute | solution.py:22
  1710.9 38.7 %collective-permute-start.2 = (s32[256]{0:T(256)S(1)}, s32[256]{0:T(256)S(1)}, u32[]{:S(2)}, u32[]{:S(2)}) collective-permute-start(s32[256]{0:T(256)S(1)} %copy.104), channel_id=1, source_target_pairs={{0,8},{8,16},{16,24},{24,0},{1,9},{9,17},{17,25},{25,1},{2,10},{10... | collective-permute-start | bytes 3080 | tf_op jit(solution)/shard_map/while/body/eval_jaxpr/ppermute | solution.py:22
  1756.7 16.1 collective-permute-start.3
  1761.0 22.9 collective-permute-start.4
  1763.2 39.7 %collective-permute-start = (bf16[256,4,256]{2,0,1:T(8,128)(2,1)}, bf16[256,4,256]{2,0,1:T(8,128)(2,1)S(1)}, u32[]{:S(2)}, u32[]{:S(2)}) collective-permute-start(bf16[256,4,256]{2,0,1:T(8,128)(2,1)} %copy.102), channel_id=1, source_target_pairs={{0,8},{8,16},{16,24},{24,0},{1,9},{9,17},{17,25},{25,1},{2,10},{10... | collective-permute-start | bytes 1572872 | tf_op jit(solution)/shard_map/while/body/eval_jaxpr/ppermute | solution.py:22
  1764.0 39.0 %collective-permute-start.1 = (bf16[256,4,256]{2,0,1:T(8,128)(2,1)}, bf16[256,4,256]{2,0,1:T(8,128)(2,1)S(1)}, u32[]{:S(2)}, u32[]{:S(2)}) collective-permute-start(bf16[256,4,256]{2,0,1:T(8,128)(2,1)} %copy.103), channel_id=1, source_target_pairs={{0,8},{8,16},{16,24},{24,0},{1,9},{9,17},{17,25},{25,1},{2,10},{10... | collective-permute-start | bytes 1572872 | tf_op jit(solution)/shard_map/while/body/eval_jaxpr/ppermute | solution.py:22
  1765.2 37.8 %collective-permute-start.2 = (s32[256]{0:T(256)S(1)}, s32[256]{0:T(256)S(1)}, u32[]{:S(2)}, u32[]{:S(2)}) collective-permute-start(s32[256]{0:T(256)S(1)} %copy.104), channel_id=1, source_target_pairs={{0,8},{8,16},{16,24},{24,0},{1,9},{9,17},{17,25},{25,1},{2,10},{10... | collective-permute-start | bytes 3080 | tf_op jit(solution)/shard_map/while/body/eval_jaxpr/ppermute | solution.py:22
  1824.9 595.4 %reduce-scatter.11.cloned.1.call-start = ((), (), s32[]{:S(2)}) async-start(), calls=%async_computation.15 | async-start | bytes 47775744 | tf_op jit(solution)/shard_map/reduce_scatter | solution.py:245
  1847.6 1381.1 %reduce-scatter.13.cloned.1.call-start = ((), (), s32[]{:S(2)}) async-start(), calls=%async_computation.16 | async-start | bytes 95551488
  1884.1 1700.9 %all-reduce.15.cloned.1.call-start = ((), (), s32[]{:S(2)}) async-start(), calls=%async_computation.17 | async-start | bytes 38928384 | tf_op jit(solution)/shard_map/psum | solution.py:282
  3240.7 55.7 %copy-start.13 = (f32[256,2304]{1,0:T(8,128)S(1)}, f32[256,2304]{1,0:T(8,128)}, u32[]{:S(2)}) copy-start(f32[256,2304]{1,0:T(8,128)} %copy-done.12) | copy-start | bytes 7077892
  (51 other events, 169.2 us)
Sparse Core Ops, SparseCore 0:
  9.7 54.7 all-gather.10
  66.2 50.4 all-gather.16
  118.4 89.5 all-gather.14
  209.6 33.6 all-gather.12
  245.0 35.3 all-gather.18
  281.8 90.7 all-gather.20
  374.2 361.6 all-gather.22
  737.5 361.6 all-gather.24
  1100.9 361.6 all-gather.26
  1568.6 98.0 reduce-scatter.8
  1825.0 185.3 reduce-scatter.6
  2012.7 407.5 reduce-scatter.10
  2422.9 805.7 reduce-scatter.12
  3232.5 352.4 all-reduce.14
where the time goes:
time: 3630 us; the launch traced here: 3610 us
  waiting for transfers between devices  3030 us (83%)
  matrix products  330 us (9%)
  local copies, waits for them, and re-layouts  80.6 us (2%)
  blocking collectives  77.7 us (2%)
  other arithmetic  56.2 us (2%)
    unnamed x15, waiting for transfers between devices  813 us
    reduce_scatter x1, waiting for transfers between devices, per_device(): lax.psum_scatter(contract_first(hidden, grad_down_low).astype(jnp.bfloat1...  410 us
    all_gather x1, waiting for transfers between devices, per_device(): lax.all_gather(gate_weight, 'fsdp', axis=0, tiled=True)  355 us
    all_gather x1, waiting for transfers between devices, per_device(): lax.all_gather(up_weight, 'fsdp', axis=0, tiled=True)  337 us
    all_gather x1, waiting for transfers between devices, per_device(): lax.all_gather(down_weight, 'fsdp', axis=0, tiled=True)  333 us
    psum x1, waiting for transfers between devices, per_device(): lax.psum(projection_sums, 'ctx').astype(jnp.float32)  285 us
    ppermute x20, waiting for transfers between devices, shifted(): lax.ppermute(shard, axis, [(i, (i + by) % size) for i in range(size)])  127 us
    reduce_scatter x1, waiting for transfers between devices, per_device(): lax.psum_scatter(contract_first(normed, projections).astype(jnp.bfloat16)...  126 us
  transfers between devices with their start and end apart: 34, of which 25 were waited for; matrix products, arithmetic and copies ran while one was open for 9% of the time, Pallas kernels for 0%

commit v1 on v0

v1 whole, which is shorter than its diff:
```python
import functools

import jax
import jax.numpy as jnp
from jax import lax
from jax.experimental import pallas as pl
from jax.experimental.pallas import tpu as pltpu
from jax.sharding import PartitionSpec as P

HQ = 8
KV = 4
HD = 256

soft_cap = 50.0
epsilon = 1e-06
rope_base = 10000.0
low = jnp.bfloat16
wide = jnp.float32


def swap(shard, axis, mask):
    size = lax.axis_size(axis)
    return lax.ppermute(shard, axis, [(i, i ^ mask) for i in range(size)])


def after(value, *others):
    return lax.optimization_barrier((value, *others))[0]


def chip_groups():
    size = lax.axis_size("fsdp")
    return [list(range(core, size, 2)) for core in (0, 1)]


def cut_at(width):
    return (width // 512) * 256 if width >= 512 else width // 2


def gather_pieces(block, halves=True):
    width = block.shape[-1]
    got, pieces = {0: block}, [(block, 0, 0)]
    for k in range(1, lax.axis_size("ctx")):
        low_bit, high_bit = k & -k, 1 << (k.bit_length() - 1)
        if low_bit == high_bit or not halves:
            got[k] = swap(got[k ^ high_bit], "ctx", high_bit)
            pieces.append((got[k], k, 0))
        else:
            cut = cut_at(width)
            first = swap(got[k ^ high_bit][..., :cut], "ctx", high_bit)
            second = swap(got[k ^ low_bit][..., cut:], "ctx", low_bit)
            pieces += [(first, k, 0), (second, k, cut)]
            if k + 1 < lax.axis_size("ctx"):
                got[k] = jnp.concatenate([first, second], axis=-1)
    return pieces


def gather_blocks(block, halves=True):
    return as_blocks(gather_pieces(block, halves))


def as_blocks(pieces):
    blocks = [[] for _ in range(lax.axis_size("ctx"))]
    for array, k, _ in pieces:
        blocks[k].append(array)
    return [b[0] if len(b) == 1 else jnp.concatenate(b, axis=-1) for b in blocks]


def halved(parts):
    cut = cut_at(parts[0].shape[-1])
    return [(part[..., :cut], part[..., cut:]) for part in parts]


def scatter_sum(terms):
    terms = list(terms)
    for k in range(len(terms) - 1, 0, -1):
        low_bit, high_bit = k & -k, 1 << (k.bit_length() - 1)
        first = swap(terms[k][0], "ctx", high_bit).astype(wide)
        second = swap(terms[k][1], "ctx", low_bit).astype(wide)
        to_first, to_second = k ^ high_bit, k ^ low_bit
        first = terms[to_first][0].astype(wide) + first
        terms[to_first] = (first.astype(low) if to_first else first, terms[to_first][1])
        second = terms[to_second][1].astype(wide) + second
        terms[to_second] = (terms[to_second][0], second.astype(low) if to_second else second)
    return jnp.concatenate(terms[0], axis=-1)


def exchange(parts):
    return [parts[0]] + [swap(part, "ctx", k) for k, part in enumerate(parts) if k]


def chip_sum(term):
    count = lax.axis_size("fsdp")
    core = lax.axis_index("fsdp") & 1
    halves = term.reshape(count // 2, 2, term.shape[0] // count, term.shape[1])
    theirs = swap(lax.dynamic_index_in_dim(halves, 1 - core, 1, keepdims=False), "fsdp", 1)
    mine = lax.dynamic_index_in_dim(halves, core, 1, keepdims=False)
    total = (mine.astype(wide) + theirs.astype(wide)).astype(low)
    return total.reshape(-1, term.shape[1])


def fsdp_sum(arr):
    return lax.psum_scatter(
        arr,
        "fsdp",
        scatter_dimension=0,
        tiled=True,
        axis_index_groups=chip_groups(),
    )


def row_tile(rows):
    return next(t for t in (48, 32, 16, rows) if rows % t == 0)


def unit_place(block, count, main, rest):
    return block % 2 * (count // 2) * (main + rest) + block // 2 * main


def rest_place(core, count, main, rest):
    return core * (count // 2) * (main + rest) + count // 2 * main


def take_units_kernel(count, cols, main, rest, c_ref, weight_ref, pick_ref, out_ref):
    c = c_ref[0]
    for b in range(count):
        start = pl.multiple_of(b * cols + c * main, 128)
        to = unit_place(b, count, main, rest)
        out_ref[:, to : to + main] = weight_ref[:, pl.ds(start, main)]
    last = jnp.concatenate(
        [weight_ref[:, (b + 1) * cols - 128 : (b + 1) * cols] for b in range(count)], axis=1
    )
    picked = jnp.dot(last, pick_ref[...], preferred_element_type=jnp.float32)
    size = count // 2 * rest
    for core in (0, 1):
        to = rest_place(core, count, main, rest)
        out_ref[:, to : to + size] = picked[:, core * size : (core + 1) * size].astype(out_ref.dtype)


def take_units(weight, c, count, main, rest):
    rows, cols = weight.shape
    source = jnp.arange(count * 128)[:, None]
    target = jnp.arange(count * rest)[None, :]
    block = target // rest % (count // 2) * 2 + target // (count // 2 * rest)
    pick = (source == block * 128 + c * rest + target % rest).astype(weight.dtype)
    tile = row_tile(rows)
    return pl.pallas_call(
        functools.partial(take_units_kernel, count, cols // count, main, rest),
        out_shape=jax.ShapeDtypeStruct((rows, count * (main + rest)), weight.dtype),
        grid=(rows // tile,),
        in_specs=[
            pl.BlockSpec(memory_space=pltpu.SMEM),
            pl.BlockSpec((tile, cols), lambda i: (i, 0)),
            pl.BlockSpec(pick.shape, lambda i: (0, 0)),
        ],
        out_specs=pl.BlockSpec((tile, count * (main + rest)), lambda i: (i, 0)),
        compiler_params=pltpu.CompilerParams(vmem_limit_bytes=32 * 2**20),
        cost_estimate=pl.CostEstimate(
            flops=2 * rows * count * 128 * count * rest,
            bytes_accessed=3 * rows * cols,
            transcendentals=0,
        ),
    )(c.reshape(1), weight, pick)


def place_kernel(plan, fixed, axis, i_ref, *refs):
    out = refs[-1]
    index = i_ref[0]
    for ref, (k, moves) in zip(refs, plan):
        for start, size, base, stride in moves:
            to = base + (index ^ k) * stride
            if stride:
                to = pl.multiple_of(to, 16 if axis == 0 else 128)
            if axis == 0:
                out[pl.ds(to, size), :] = ref[start : start + size, :].astype(out.dtype)
            else:
                out[:, pl.ds(to, size)] = ref[:, start : start + size].astype(out.dtype)
    for start, size, base in fixed:
        out[:, base : base + size] = refs[len(plan)][:, start : start + size]


def place(pieces, index, shape, axis, dtype, extra=None, fixed=(), blocks=0):
    arrays = [array for array, _, _ in pieces]
    plan = [(k, moves) for _, k, moves in pieces]
    if axis == 1:
        tile = shape[0] // blocks if blocks else row_tile(shape[0])
        grid = shape[0] // tile
        block = lambda array: (tile, array.shape[1])
        at = lambda i: (i, 0)
        out_block = (tile, shape[1])
    else:
        tile = next(t for t in (384, 256, 128, shape[1]) if shape[1] % t == 0)
        grid = shape[1] // tile
        block = lambda array: (array.shape[0], tile)
        at = lambda i: (0, i)
        out_block = (shape[0], tile)
    ats = [at] * len(plan)
    if blocks:
        ats = [lambda i, k=k: (i ^ k, 0) for k, _ in plan]
    if extra is not None:
        arrays.append(extra)
        ats.append(at)
    return pl.pallas_call(
        functools.partial(place_kernel, plan, fixed, axis),
        out_shape=jax.ShapeDtypeStruct(shape, dtype),
        grid=(grid,),
        in_specs=[pl.BlockSpec(memory_space=pltpu.SMEM)]
        + [pl.BlockSpec(block(array), place_) for array, place_ in zip(arrays, ats)],
        out_specs=pl.BlockSpec(out_block, at),
        compiler_params=pltpu.CompilerParams(vmem_limit_bytes=32 * 2**20),
        cost_estimate=pl.CostEstimate(
            flops=0, bytes_accessed=6 * shape[0] * shape[1], transcendentals=0
        ),
    )(index.reshape(1), *arrays)


def add_rows_kernel(moves, first_ref, second_ref, out_ref):
    for start, size, to in moves:
        total = first_ref[start : start + size, :].astype(wide)
        total += second_ref[start : start + size, :].astype(wide)
        out_ref[to : to + size, :] = total.astype(out_ref.dtype)


def add_rows(first, second, moves):
    rows, cols = first.shape
    tile = next(t for t in (384, 256, 128) if cols % t == 0)
    spec = pl.BlockSpec((rows, tile), lambda i: (0, i))
    return pl.pallas_call(
        functools.partial(add_rows_kernel, moves),
        out_shape=jax.ShapeDtypeStruct((rows, cols), first.dtype),
        grid=(cols // tile,),
        in_specs=[spec, spec],
        out_specs=spec,
        compiler_params=pltpu.CompilerParams(vmem_limit_bytes=32 * 2**20),
        cost_estimate=pl.CostEstimate(
            flops=rows * cols, bytes_accessed=6 * rows * cols, transcendentals=0
        ),
    )(first, second)


def split_columns_kernel(size, cut, c_ref, ref, *outs):
    c = c_ref[0]
    for k in range(len(outs) // 2):
        start = pl.multiple_of((c ^ k) * size, 128)
        outs[2 * k][...] = ref[:, pl.ds(start, cut)]
        outs[2 * k + 1][...] = ref[:, pl.ds(start + cut, size - cut)]


def split_columns(array, c, count, cut):
    rows, cols = array.shape
    tile, size = rows // count, cols // count
    shapes = [(rows, cut), (rows, size - cut)] * count
    return pl.pallas_call(
        functools.partial(split_columns_kernel, size, cut),
        out_shape=[jax.ShapeDtypeStruct(shape, array.dtype) for shape in shapes],
        grid=(count,),
        in_specs=[
            pl.BlockSpec(memory_space=pltpu.SMEM),
            pl.BlockSpec((tile, cols), lambda i: (i, 0)),
        ],
        out_specs=[
            pl.BlockSpec((tile, shape[1]), lambda i, k=n // 2: (i ^ k, 0))
            for n, shape in enumerate(shapes)
        ],
        compiler_params=pltpu.CompilerParams(vmem_limit_bytes=32 * 2**20),
        cost_estimate=pl.CostEstimate(
            flops=0, bytes_accessed=4 * rows * cols, transcendentals=0
        ),
    )(c.reshape(1), array)


def join_kernel(plan, *refs):
    out = refs[-1]
    for ref, (k, first) in zip(refs, plan):
        out[k, :, first : first + ref.shape[1]] = ref[...]


def join(pieces):
    rows, width = pieces[0][0].shape
    count = 1 + max(k for _, k, _ in pieces)
    if any(array.shape[1] % 128 for array, _, _ in pieces) or rows % 64:
        blocks = [[] for _ in range(count)]
        for array, k, _ in pieces:
            blocks[k].append(array)
        return jnp.concatenate([jnp.concatenate(b, axis=1) for b in blocks], axis=0)
    joined = pl.pallas_call(
        functools.partial(join_kernel, [(k, first) for _, k, first in pieces]),
        out_shape=jax.ShapeDtypeStruct((count, rows, width), pieces[0][0].dtype),
        grid=(rows // 64,),
        in_specs=[pl.BlockSpec((64, array.shape[1]), lambda i: (i, 0)) for array, _, _ in pieces],
        out_specs=pl.BlockSpec((count, 64, width), lambda i: (0, i, 0)),
        compiler_params=pltpu.CompilerParams(vmem_limit_bytes=32 * 2**20),
        cost_estimate=pl.CostEstimate(
            flops=0, bytes_accessed=4 * count * rows * width, transcendentals=0
        ),
    )(*[array for array, _, _ in pieces])
    return joined.reshape(count * rows, width)


def turn(vectors, cosine, sine):
    half = cosine.shape[1]
    parts = []
    for start in range(0, vectors.shape[1], 2 * half):
        first = vectors[:, start : start + half]
        second = vectors[:, start + half : start + 2 * half]
        parts += [first * cosine - second * sine, second * cosine + first * sine]
    return jnp.concatenate(parts, axis=1)


def attention_back_kernel(
    heads, scale, grad_ref, query_ref, key_ref, value_ref, row_ref, column_ref,
    cosine_ref, sine_ref, all_cosine_ref, all_sine_ref, out_ref, sums_ref,
):
    step = pl.program_id(0)
    keys, values = key_ref[...], value_ref[...]
    width = keys.shape[1]

    @pl.when(step == 0)
    def _():
        sums_ref[...] = jnp.zeros_like(sums_ref)

    allowed = column_ref[...] <= row_ref[...]
    grads = []
    for head in range(heads):
        at = slice(head * width, (head + 1) * width)
        query, grad = query_ref[:, at], grad_ref[:, at]
        bent = jnp.tanh(contract_last(query, keys) * (1.0 / soft_cap))
        weights = jnp.where(allowed, jnp.exp(soft_cap * bent), 0.0)
        probs = weights * (1.0 / jnp.sum(weights, axis=1, keepdims=True))
        grad_probs = contract_last(grad, values)
        delta = jnp.sum(probs * grad_probs, axis=1, keepdims=True)
        grad_raw = (probs * (grad_probs - delta) * (1.0 - bent * bent)).astype(low)
        grads.append(dot(grad_raw, keys))
        sums_ref[0] += contract_first(grad_raw, query)
        sums_ref[1] += contract_first(probs.astype(low), grad)
    grads = jnp.concatenate(grads, axis=1) * scale
    here = pl.ds(pl.multiple_of(step * grads.shape[0], grads.shape[0]), grads.shape[0])
    split = grads.shape[1]
    out_ref[here, :split] = turn(grads, cosine_ref[...], -sine_ref[...]).astype(low)

    @pl.when(step == pl.num_programs(0) - 1)
    def _():
        turned = turn(sums_ref[0], all_cosine_ref[...], -all_sine_ref[...])
        out_ref[:, split : split + width] = turned.astype(low)
        out_ref[:, split + width :] = sums_ref[1].astype(low)


def attention_back(grad, queries, keys, values, places, cosine, sine, scale):
    length, width = keys.shape
    heads = queries.shape[1] // width
    tile = 256
    rows = lambda cols: pl.BlockSpec((tile, cols), lambda i: (i, 0))
    whole = lambda *shape: pl.BlockSpec(shape, lambda i: (0, 0))
    half = cosine.shape[1]
    return pl.pallas_call(
        functools.partial(attention_back_kernel, heads, scale),
        out_shape=jax.ShapeDtypeStruct((length, (heads + 2) * width), low),
        grid=(length // tile,),
        in_specs=[
            rows(heads * width),
            rows(heads * width),
            whole(length, width),
            whole(length, width),
            rows(1),
            whole(1, length),
            rows(half),
            rows(half),
            whole(length, half),
            whole(length, half),
        ],
        out_specs=whole(length, (heads + 2) * width),
        scratch_shapes=[pltpu.VMEM((2, length, width), wide)],
        compiler_params=pltpu.CompilerParams(vmem_limit_bytes=48 * 2**20),
        cost_estimate=pl.CostEstimate(
            flops=20 * heads * length * length * width,
            bytes_accessed=16 * length * width,
            transcendentals=2 * heads * length * length,
        ),
    )(
        grad,
        queries,
        keys,
        values,
        places[:, None],
        places[None, :],
        cosine,
        sine,
        cosine,
        sine,
    )


def column_tile(cols):
    return next(t for t in (256, 128, cols) if cols % t == 0)


def row_chunks(rows, body):
    size = next(t for t in (512, 256, 128, rows) if rows % t == 0)

    def step(i, carry):
        body(pl.ds(pl.multiple_of(i * size, size), size))
        return carry

    lax.fori_loop(0, rows // size, step, 0)


def units_kernel(x_ref, gate_ref, up_ref, hidden_ref, gate_slope_ref, up_slope_ref):
    root = (2.0 / jnp.pi) ** 0.5

    def body(at):
        x = x_ref[at, :]
        gate = dot(x, gate_ref[...])
        up = dot(x, up_ref[...])
        square = gate * gate
        bend = jnp.tanh(root * gate * (1.0 + 0.044715 * square))
        half = 0.5 * (1.0 + bend)
        activated = gate * half
        slope = half + 0.5 * gate * (1.0 - bend * bend) * root * (1.0 + 3.0 * 0.044715 * square)
        hidden_ref[at, :] = (activated * up).astype(low)
        gate_slope_ref[at, :] = (up * slope).astype(low)
        up_slope_ref[at, :] = activated.astype(low)

    row_chunks(x_ref.shape[0], body)


def units_forward(x, weights):
    rows, depth = x.shape
    cols = weights.shape[1] // 2
    tile = column_tile(cols)
    steps = cols // tile
    out = jax.ShapeDtypeStruct((rows, cols), low)
    out_spec = pl.BlockSpec((rows, tile), lambda j: (0, j))
    return pl.pallas_call(
        units_kernel,
        out_shape=[out] * 3,
        grid=(steps,),
        in_specs=[
            pl.BlockSpec((rows, depth), lambda j: (0, 0)),
            pl.BlockSpec((depth, tile), lambda j: (0, j)),
            pl.BlockSpec((depth, tile), lambda j: (0, j + steps)),
        ],
        out_specs=[out_spec] * 3,
        compiler_params=pltpu.CompilerParams(vmem_limit_bytes=48 * 2**20),
        cost_estimate=pl.CostEstimate(
            flops=4 * rows * depth * cols,
            bytes_accessed=4 * depth * cols + 2 * rows * depth + 6 * rows * cols,
            transcendentals=rows * cols,
        ),
    )(x, weights, weights)


def units_back_kernel(count, *refs):
    grads, weights = refs[:count], refs[count : 2 * count]
    gate_slope_ref, up_slope_ref, gate_ref, up_ref = refs[2 * count :]
    cols = gate_slope_ref.shape[1]
    tile = column_tile(cols)

    def step(j, carry):
        at = pl.ds(pl.multiple_of(j * tile, tile), tile)
        grad = sum(contract_last(g[...], w[at, :]) for g, w in zip(grads, weights))
        gate_ref[:, at] = (grad * gate_slope_ref[:, at].astype(wide)).astype(low)
        up_ref[:, at] = (grad * up_slope_ref[:, at].astype(wide)).astype(low)
        return carry

    lax.fori_loop(0, cols // tile, step, 0)


def units_back(grads, weights, gate_slope, up_slope):
    rows, cols = gate_slope.shape
    tile = next(t for t in (512, 256, 128, rows) if rows % t == 0)
    width = sum(g.shape[1] for g in grads)
    return pl.pallas_call(
        functools.partial(units_back_kernel, len(grads)),
        out_shape=[jax.ShapeDtypeStruct((rows, cols), low)] * 2,
        grid=(rows // tile,),
        in_specs=[pl.BlockSpec((tile, g.shape[1]), lambda i: (i, 0)) for g in grads]
        + [pl.BlockSpec(w.shape, lambda i: (0, 0)) for w in weights]
        + [pl.BlockSpec((tile, cols), lambda i: (i, 0))] * 2,
        out_specs=[pl.BlockSpec((tile, cols), lambda i: (i, 0))] * 2,
        compiler_params=pltpu.CompilerParams(vmem_limit_bytes=56 * 2**20),
        cost_estimate=pl.CostEstimate(
            flops=2 * rows * width * cols,
            bytes_accessed=2 * width * cols + 2 * rows * width + 8 * rows * cols,
            transcendentals=0,
        ),
    )(*grads, *weights, gate_slope, up_slope)


def product_kernel(*refs):
    *lefts, right_ref, out_ref = refs
    depth = lefts[0].shape[1]

    def body(at):
        total = sum(
            contract_last(left[at, :], right_ref[:, i * depth : (i + 1) * depth])
            for i, left in enumerate(lefts)
        )
        out_ref[at, :] = total.astype(out_ref.dtype)

    row_chunks(lefts[0].shape[0], body)


def product_last(lefts, right):
    rows, depth = lefts[0].shape
    cols, width = right.shape
    tile = column_tile(cols)
    return pl.pallas_call(
        product_kernel,
        out_shape=jax.ShapeDtypeStruct((rows, cols), low),
        grid=(cols // tile,),
        in_specs=[pl.BlockSpec((rows, depth), lambda j: (0, 0)) for _ in lefts]
        + [pl.BlockSpec((tile, width), lambda j: (j, 0))],
        out_specs=pl.BlockSpec((rows, tile), lambda j: (0, j)),
        compiler_params=pltpu.CompilerParams(vmem_limit_bytes=48 * 2**20),
        cost_estimate=pl.CostEstimate(
            flops=2 * rows * width * cols,
            bytes_accessed=2 * (rows * width + width * cols + rows * cols),
            transcendentals=0,
        ),
    )(*lefts, right)


def cores_apart_kernel(count, x_ref, out_ref):
    part = x_ref.shape[1] // count
    order = [*range(0, count, 2), *range(1, count, 2)]
    out_ref[...] = jnp.concatenate(
        [x_ref[:, b * part : (b + 1) * part] for b in order], axis=1
    )


def cores_apart(x, count):
    rows, cols = x.shape
    return pl.pallas_call(
        functools.partial(cores_apart_kernel, count),
        out_shape=jax.ShapeDtypeStruct(x.shape, x.dtype),
        grid=(rows // 128,),
        in_specs=[pl.BlockSpec((128, cols), lambda i: (i, 0))],
        out_specs=pl.BlockSpec((128, cols), lambda i: (i, 0)),
        compiler_params=pltpu.CompilerParams(vmem_limit_bytes=32 * 2**20),
        cost_estimate=pl.CostEstimate(
            flops=0, bytes_accessed=4 * rows * cols, transcendentals=0
        ),
    )(x)


def frequencies(half, head_dim):
    return rope_base ** (-(jnp.arange(half, dtype=wide) * 2.0) / head_dim)


def rotate(vectors, cosine, sine):
    half = vectors.shape[-1] // 2
    first = vectors[..., :half]
    second = vectors[..., half:]
    return jnp.concatenate(
        [first * cosine - second * sine, second * cosine + first * sine], axis=-1
    )


def inverse_rms(vectors):
    return lax.rsqrt(jnp.mean(vectors * vectors, axis=-1, keepdims=True) + epsilon)


def norm_back(vectors, inverse, gain, upstream):
    scaled = upstream * gain
    unit = vectors * inverse
    grad_vectors = inverse * (scaled - unit * jnp.mean(unit * scaled, axis=-1, keepdims=True))
    return (grad_vectors, jnp.sum(upstream * unit, axis=0))


def dot(left, right):
    return jnp.dot(left, right, preferred_element_type=wide)


def contract_last(left, right):
    return lax.dot_general(left, right, (((1,), (1,)), ((), ())), preferred_element_type=wide)


def contract_first(left, right):
    return lax.dot_general(left, right, (((0,), (0,)), ((), ())), preferred_element_type=wide)


def per_device(
    inputs,
    positions,
    pre_attn_gain,
    post_attn_gain,
    pre_mlp_gain,
    post_mlp_gain,
    query_weight,
    key_weight,
    value_weight,
    out_weight,
    gate_weight,
    up_weight,
    down_weight,
    cotangent,
):
    n_ctx, n_fsdp = lax.axis_size("ctx"), lax.axis_size("fsdp")
    c, f = lax.axis_index("ctx"), lax.axis_index("fsdp")
    rows = inputs[0].astype(wide)
    tokens, width = rows.shape
    length = n_ctx * tokens
    scale = HD ** (-0.5)
    my_heads = HQ // n_ctx
    my_kv = max(KV // n_ctx, 1)
    share = max(n_ctx // KV, 1)
    groups = my_heads // my_kv
    kv_start = (c // share) * my_kv * HD
    query_cols, kv_cols = my_heads * HD, my_kv * HD
    out_cols = width // n_ctx
    ff_rows = down_weight.shape[0]
    part = ff_rows // n_ctx
    main = ff_rows // 128 // n_ctx * 128
    rest = part - main
    chips = n_fsdp // 2
    tiled = ff_rows % 128 == 0 and main > 0 and rest * n_ctx == 128 and rest % 16 == 0
    tiled = tiled and chips * rest % 128 == 0 and query_cols % 256 == 0
    last_cols = width // 384 * 128

    def gathered(shard):
        return lax.all_gather(shard, "fsdp", axis=0, tiled=True)

    def units_together(full):
        if not tiled:
            return full
        moves = []
        for block in range(n_fsdp):
            to = unit_place(block, n_fsdp, main, rest)
            moves.append((block * part, main, to, 0))
            to = rest_place(block % 2, n_fsdp, main, rest) + block // 2 * rest
            moves.append((block * part + main, rest, to, 0))
        return place([(full, 0, moves)], jnp.zeros((), jnp.int32), full.shape, 0, full.dtype)

    def chip_term(term):
        return chip_sum(term.astype(low))

    def unit_term(left, right):
        if not tiled:
            return chip_term(contract_first(left, right))
        half, core = chips * part, f & 1
        theirs = lax.dynamic_slice_in_dim(left, (1 - core) * half, half, 1)
        theirs = swap(contract_first(theirs, right).astype(low), "fsdp", 1)
        mine = contract_first(lax.dynamic_slice_in_dim(left, core * half, half, 1), right)
        moves = [(chip * main, main, chip * part) for chip in range(chips)]
        moves += [
            (chips * main + chip * rest, rest, chip * part + main) for chip in range(chips)
        ]
        return add_rows(mine.astype(low), theirs, moves)

    def weight_term(left, right):
        if not tiled:
            return chip_term(contract_first(left, right))
        half, core = left.shape[1] // 2, f & 1
        theirs = lax.dynamic_slice_in_dim(left, (1 - core) * half, half, 1)
        theirs = swap(contract_first(theirs, right).astype(low), "fsdp", 1)
        mine = contract_first(lax.dynamic_slice_in_dim(left, core * half, half, 1), right)
        return (mine + theirs.astype(wide)).astype(low)

    def my_units(weight):
        if tiled:
            return take_units(weight, c, n_fsdp, main, rest)
        split = weight.reshape(weight.shape[0], n_fsdp, n_ctx, part)
        return lax.dynamic_index_in_dim(split, c, 2, keepdims=False).reshape(
            weight.shape[0], n_fsdp * part
        )

    def in_order(blocks):
        blocks = list(blocks)
        for bit in range(n_ctx.bit_length() - 1):
            mask = 1 << bit
            odd = (c & mask) != 0
            blocks = [jnp.where(odd, blocks[k ^ mask], blocks[k]) for k in range(n_ctx)]
        return blocks

    def token_blocks(array):
        return [array[k * tokens : (k + 1) * tokens] for k in range(n_ctx)]

    def block_order(blocks, k):
        pieces = blocks.reshape(n_ctx, tokens, blocks.shape[-1])
        return jnp.concatenate([pieces[k ^ m] for m in range(n_ctx)], axis=0)

    def from_columns(array):
        got = jnp.stack(exchange(token_blocks(array)))
        return jnp.transpose(jnp.take(got, jnp.arange(n_ctx) ^ c, axis=0), (1, 0, 2)).reshape(
            tokens, width
        )

    def to_columns(array):
        split = array.reshape(tokens, n_ctx, out_cols)
        split = jnp.take(split, jnp.arange(n_ctx) ^ c, axis=1)
        return jnp.concatenate(exchange([split[:, k] for k in range(n_ctx)]), axis=0)

    my_qkv = jnp.concatenate(
        [
            lax.dynamic_slice_in_dim(query_weight, c * query_cols, query_cols, 1),
            lax.dynamic_slice_in_dim(key_weight, kv_start, kv_cols, 1),
            lax.dynamic_slice_in_dim(value_weight, kv_start, kv_cols, 1),
        ],
        axis=1,
    )
    full_qkv = gathered(my_qkv)
    full_out = gathered(lax.dynamic_slice_in_dim(out_weight, c * out_cols, out_cols, 1))
    full_units = gathered(jnp.concatenate([my_units(gate_weight), my_units(up_weight)], axis=1))
    if tiled:
        my_down = jnp.concatenate(
            [
                lax.dynamic_slice_in_dim(down_weight, c * main, main, 0),
                lax.dynamic_slice_in_dim(down_weight, n_ctx * main + c * rest, rest, 0),
            ],
            axis=0,
        )
    else:
        my_down = lax.dynamic_slice_in_dim(down_weight, c * part, part, 0)
    gains = jnp.stack([pre_attn_gain, post_attn_gain, pre_mlp_gain, post_mlp_gain])
    gains = jnp.stack([gains if k == 0 else swap(gains, "fsdp", k) for k in range(n_fsdp)])
    gains = jnp.take(gains, jnp.arange(n_fsdp) ^ f, axis=0)
    gains = jnp.transpose(gains, (1, 0, 2)).reshape(4, width).astype(wide)
    gain_a, gain_b, gain_c, gain_d = gains[0], gains[1], gains[2], gains[3]

    inverse_a = inverse_rms(rows)
    normed = join(gather_pieces((rows * inverse_a * gain_a).astype(low)))
    normed_apart = cores_apart(normed, n_fsdp) if tiled else normed
    places = jnp.concatenate(gather_blocks(positions[0], halves=False), axis=0)
    angles = places.astype(wide)[:, None] * frequencies(HD // 2, HD)
    cosine, sine = jnp.cos(angles), jnp.sin(angles)
    projected = dot(normed, full_qkv)
    query_lin = projected[:, :query_cols].reshape(length, my_heads, HD)
    key_lin = projected[:, query_cols : query_cols + kv_cols].reshape(length, my_kv, HD)
    values = projected[:, query_cols + kv_cols :].astype(low).reshape(length, my_kv, HD)
    queries = (rotate(query_lin, cosine[:, None], sine[:, None]) * scale).astype(low)
    keys = rotate(key_lin, cosine[:, None], sine[:, None]).astype(low)
    queries = queries.reshape(length, my_kv, groups, HD)
    allowed = places[None, :] <= places[:, None]
    raw = jnp.einsum("tkgd,rkd->kgtr", queries, keys, preferred_element_type=wide)
    bent = jnp.tanh(raw / soft_cap)
    weights = jnp.where(allowed, jnp.exp(soft_cap * bent), 0.0)
    total = jnp.sum(weights, axis=-1)
    mixed = jnp.einsum("kgtr,rkd->kgtd", weights.astype(low), values, preferred_element_type=wide)
    mixed = mixed / total[..., None]
    attn = jnp.transpose(mixed, (2, 0, 1, 3)).reshape(length, query_cols).astype(low)

    if tiled:
        pieces = [
            (array, k, [(0, array.shape[1], first, query_cols)])
            for array, k, first in gather_pieces(attn)
        ]
        attn_all = place(pieces, c, (length, HQ * HD), 1, low, blocks=n_ctx)
    else:
        attn_blocks = [block_order(block, k) for k, block in enumerate(gather_blocks(attn))]
        attn_all = jnp.concatenate(in_order(attn_blocks), axis=1)
    branch = from_columns(dot(attn_all, full_out).astype(low)).astype(wide)
    inverse_b = inverse_rms(branch)
    middle = rows + branch * inverse_b * gain_b
    inverse_c = inverse_rms(middle)

    normed_mlp = join(gather_pieces((middle * inverse_c * gain_c).astype(low)))
    normed_mlp_apart = cores_apart(normed_mlp, n_fsdp) if tiled else normed_mlp
    my_down = after(my_down, full_units, normed_mlp_apart)
    first_down, last_down = gathered(my_down[:, :-last_cols]), my_down[:, -last_cols:]
    hidden, gate_slope, up_slope = units_forward(normed_mlp, full_units)
    last_down = gathered(after(last_down, first_down, hidden))
    full_downs = [units_together(first_down), units_together(last_down)]
    first_terms, last_terms = (
        token_blocks(dot(hidden, full).astype(low)) for full in full_downs
    )
    last_terms = sum(term.astype(wide) for term in exchange(last_terms))
    down = jnp.concatenate([scatter_sum(halved(first_terms)), last_terms], axis=1)
    inverse_d = inverse_rms(down)
    output = (middle + down * inverse_d * gain_d).astype(low)[None]

    grad_result = cotangent[0].astype(wide)
    grad_down, grad_gain_d = norm_back(down, inverse_d, gain_d, grad_result)
    grad_down = grad_down.astype(low)
    pieces = gather_pieces(grad_down[:, -last_cols:])
    grad_downs = [join(pieces)]
    down_terms = [unit_term(hidden, grad_downs[0])]
    others = [array for array, _, _ in pieces[1:3]]
    pieces = gather_pieces(after(grad_down[:, :-last_cols], *others))
    pieces[0] = (after(pieces[0][0], down_terms[0]), *pieces[0][1:])
    grad_downs.append(join(pieces))
    down_terms.append(unit_term(hidden, grad_downs[1]))
    grad_downs, down_terms[1] = lax.optimization_barrier((grad_downs, down_terms[1]))
    down_sums = [fsdp_sum(term) for term in down_terms]
    grad_gate, grad_up = units_back(grad_downs, full_downs[::-1], gate_slope, up_slope)
    grad_normed_mlp = product_last([grad_gate, grad_up], full_units)
    grad_normed_mlp, grad_gate = lax.optimization_barrier((grad_normed_mlp, grad_gate))
    gate_term = weight_term(normed_mlp_apart, after(grad_gate, down_sums[0]))
    gate_sum = fsdp_sum(gate_term)
    up_term = weight_term(normed_mlp_apart, after(grad_up, gate_term))
    up_sum = fsdp_sum(up_term)
    grad_normed_mlp = scatter_sum(halved(token_blocks(grad_normed_mlp)))
    down_pieces = [gather_pieces(after(down_sums[0], grad_gate))]
    arrived = [piece[0] for piece in down_pieces[0]]
    grad_normed_mlp = after(grad_normed_mlp, up_term, down_sums[1], *arrived)
    down_pieces.append(gather_pieces(after(down_sums[1], grad_normed_mlp)))
    grad_middle_mlp, grad_gain_c = norm_back(middle, inverse_c, gain_c, grad_normed_mlp)
    grad_middle = grad_result + grad_middle_mlp
    grad_branch, grad_gain_b = norm_back(branch, inverse_b, gain_b, grad_middle)

    arrived = [piece[0] for piece in down_pieces[1][1:3]]
    grad_branch_cols = to_columns(after(grad_branch.astype(low), *arrived))
    out_term = chip_term(contract_first(attn_all, grad_branch_cols))
    grad_attn_all = contract_last(grad_branch_cols, full_out).astype(low)
    if tiled:
        parts = split_columns(grad_attn_all, c, n_ctx, cut_at(query_cols))
        grad_attn = scatter_sum(list(zip(parts[::2], parts[1::2]))).astype(low)
    else:
        parts = [
            lax.dynamic_slice_in_dim(grad_attn_all, (c ^ k) * query_cols, query_cols, 1)
            for k in range(n_ctx)
        ]
        parts = [block_order(part_, k) for k, part_ in enumerate(parts)]
        grad_attn = scatter_sum(halved(parts)).astype(low)
    grad_attn = after(grad_attn, gate_sum, *[piece[0] for piece in down_pieces[1]])
    grad_projected = attention_back(
        grad_attn,
        queries.reshape(length, query_cols),
        keys.reshape(length, kv_cols),
        values.reshape(length, kv_cols),
        places,
        cosine,
        sine,
        scale,
    )
    qkv_term = weight_term(normed_apart, grad_projected)
    pad = (qkv_term.shape[0] - out_term.shape[0]) // chips
    out_term = jnp.pad(out_term.reshape(chips, -1, out_cols), ((0, 0), (0, pad), (0, 0)))
    out_term = out_term.reshape(qkv_term.shape[0], out_cols)
    attn_sum = fsdp_sum(jnp.concatenate([qkv_term, out_term], axis=1))
    qkv_sum = attn_sum[:, : qkv_term.shape[1]]
    out_sum = attn_sum[: attn_sum.shape[0] - pad, qkv_term.shape[1] :]
    grad_normed = contract_last(grad_projected, full_qkv).astype(low)
    grad_normed = scatter_sum(halved(token_blocks(grad_normed)))
    grad_normed = after(grad_normed, up_sum)
    grad_rows, grad_gain_a = norm_back(rows, inverse_a, gain_a, grad_normed)
    input_grad = (grad_middle + grad_rows).astype(low)[None]

    gain_terms = jnp.stack([grad_gain_a, grad_gain_b, grad_gain_c, grad_gain_d])
    for bit in range(n_ctx.bit_length() - 1):
        gain_terms = gain_terms + swap(gain_terms, "ctx", 1 << bit)
    gain_terms = jnp.transpose(gain_terms.reshape(4, n_fsdp, width // n_fsdp), (1, 0, 2))
    gain_terms = jnp.take(gain_terms, jnp.arange(n_fsdp) ^ f, axis=0)
    gain_sums = gain_terms[0]
    for k in range(1, n_fsdp):
        gain_sums = gain_sums + swap(gain_terms[k], "fsdp", k)

    if share == 1:
        qkv_pieces = gather_pieces(qkv_sum)

        def columns_of(first, size, shape):
            pieces = []
            for array, k, start in qkv_pieces:
                begin, end = max(first, start), min(first + size, start + array.shape[1])
                if begin < end:
                    pieces.append((array, k, [(begin - start, size, 0, size)]))
            return place(pieces, c, shape, 1, wide)

        query_grad = columns_of(0, query_cols, query_weight.shape)
        key_grad = columns_of(query_cols, kv_cols, key_weight.shape)
        value_grad = columns_of(query_cols + kv_cols, kv_cols, value_weight.shape)
    else:
        qkv_blocks = gather_blocks(qkv_sum)
        query_grad = jnp.zeros(query_weight.shape, wide)
        key_grad = jnp.zeros(key_weight.shape, wide)
        value_grad = jnp.zeros(value_weight.shape, wide)
        for k, block in enumerate(qkv_blocks):
            query_grad = lax.dynamic_update_slice_in_dim(
                query_grad, block[:, :query_cols].astype(wide), (c ^ k) * query_cols, 1
            )
        for k in range(0, n_ctx, share):
            block = sum(qkv_blocks[k + s][:, query_cols:].astype(wide) for s in range(share))
            start = ((c ^ k) // share) * kv_cols
            key_grad = lax.dynamic_update_slice_in_dim(key_grad, block[:, :kv_cols], start, 1)
            value_grad = lax.dynamic_update_slice_in_dim(value_grad, block[:, kv_cols:], start, 1)

    out_grad = jnp.concatenate(in_order(gather_blocks(out_sum)), axis=1).astype(wide)

    def all_units(total):
        if not tiled:
            blocks = gather_blocks(total)
            blocks = [b.reshape(b.shape[0], n_fsdp, part) for b in in_order(blocks)]
            return jnp.stack(blocks, axis=2).reshape(gate_weight.shape).astype(wide)
        pieces, tails = [], []
        for array, k, start in gather_pieces(total):
            moves = []
            for b in range(n_fsdp):
                begin = unit_place(b, n_fsdp, main, rest) - start
                if 0 <= begin < array.shape[1]:
                    moves.append((begin, main, b * ff_rows, main))
            pieces.append((array, k, moves))
            for core in (0, 1):
                begin = rest_place(core, n_fsdp, main, rest) - start
                if 0 <= begin < array.shape[1]:
                    tails.append((k, core, array[:, begin : begin + chips * rest]))
        tails = [tail for _, _, tail in sorted(tails, key=lambda item: item[:2])]
        source = jnp.arange(n_ctx * n_fsdp * rest)[:, None]
        index, unit = source // (n_fsdp * rest), source % (n_fsdp * rest)
        block = unit // rest % chips * 2 + unit // (chips * rest)
        target = block * 128 + (c ^ index) * rest + unit % rest
        spread_to = (target == jnp.arange(n_fsdp * 128)[None, :]).astype(low)
        return place(
            pieces,
            c,
            gate_weight.shape,
            1,
            wide,
            dot(jnp.concatenate(tails, axis=1), spread_to),
            [(b * 128, 128, (b + 1) * ff_rows - 128) for b in range(n_fsdp)],
        )

    gate_grad = all_units(after(gate_sum, qkv_term))
    up_grad = all_units(up_sum)
    down_halves = zip(*[as_blocks(pieces) for pieces in down_pieces[::-1]])
    down_blocks = [jnp.concatenate(block, axis=1) for block in down_halves]
    down_blocks[0] = after(down_blocks[0], qkv_term)
    if tiled:
        moves = [(0, main, 0, main), (main, rest, n_ctx * main, rest)]
        pieces = [(block, k, moves) for k, block in enumerate(down_blocks)]
        down_grad = place(pieces, c, down_weight.shape, 0, wide)
    else:
        down_grad = jnp.concatenate(in_order(down_blocks), axis=0).astype(wide)
    return (
        output,
        input_grad,
        gain_sums[0],
        gain_sums[1],
        gain_sums[2],
        gain_sums[3],
        query_grad,
        key_grad,
        value_grad,
        out_grad,
        gate_grad,
        up_grad,
        down_grad,
    )


def solution(mesh):
    return jax.shard_map(
        per_device,
        mesh=mesh,
        in_specs=(
            P("fsdp", "ctx", None),
            P("fsdp", "ctx"),
            P("fsdp"),
            P("fsdp"),
            P("fsdp"),
            P("fsdp"),
            P("fsdp", None),
            P("fsdp", None),
            P("fsdp", None),
            P("fsdp", None),
            P("fsdp", None),
            P("fsdp", None),
            P("fsdp", None),
            P("fsdp", "ctx", None),
        ),
        out_specs=(
            P("fsdp", "ctx", None),
            P("fsdp", "ctx", None),
            P("fsdp"),
            P("fsdp"),
            P("fsdp"),
            P("fsdp"),
            P("fsdp", None),
            P("fsdp", None),
            P("fsdp", None),
            P("fsdp", None),
            P("fsdp", None),
            P("fsdp", None),
            P("fsdp", None),
        ),
        check_vma=False,
    )
```

time: 3630 us -> 1020 us (0.28)
  waiting for transfers between devices: 3030 us -> 386 us
  matrix products: 330 us -> 129 us
  Pallas kernels: 0 us -> 148 us
  starting transfers between devices: 22.1 us -> 104 us
  blocking collectives: 77.7 us -> 0 us
  local copies, waits for them, and re-layouts: 80.6 us -> 145 us
    all_gather x9 -> x5, waiting for transfers between devices: 1270 us -> 79.9 us  [gathered(): return lax.all_gather(shard, 'fsdp', axis=0, tiled=True)]
    unnamed x15 -> x10, waiting for transfers between devices: 813 us -> 0.17 us
    reduce_scatter x3 -> x5, waiting for transfers between devices: 536 us -> 0.03 us  [fsdp_sum(): lax.psum_scatter(arr, 'fsdp', scatter_dimension=0, tiled=True, axis_index...]
    psum x1 -> x0, waiting for transfers between devices: 285 us -> none  [per_device(): lax.psum(projection_sums, 'ctx').astype(jnp.float32)]
    ppermute x20 -> x102, waiting for transfers between devices: 127 us -> 306 us  [swap(): return lax.ppermute(shard, axis, [(i, i ^ mask) for i in range(size)])]
    pallas_call x0 -> x24, Pallas kernels: none -> 148 us  [the longest x1 34.1 us: units_forward(): pl.pallas_call(units_kernel, out_shape=[out] * 3, grid=(steps,), in_specs...]
    dot_general x29 -> x8, matrix products: 163 us -> 36.9 us  [the longest x6 30 us: dot(): return jnp.dot(left, right, preferred_element_type=wide)]
    dot_general x7 -> x2, matrix products: 94.4 us -> 11.9 us  [contract_last(): lax.dot_general(left, right, (((1,), (1,)), ((), ())), preferred_element_...]
  transfers between devices with their start and end apart: 34 -> 112, of which waited for: 25 -> 57; matrix products, arithmetic and copies ran while one was open for 9% -> 28% of each run, Pallas kernels for 0% -> 14%
where the time goes in v1:
time: 1020 us; the launch traced here: 1010 us
  waiting for transfers between devices  386 us (38%)
  Pallas kernels  148 us (15%)
  local copies, waits for them, and re-layouts  145 us (14%)
  matrix products  129 us (13%)
  starting transfers between devices  104 us (10%)
  other arithmetic  80.1 us (8%)
  between operations  16.4 us (2%)
    ppermute x102, waiting for transfers between devices, swap(): return lax.ppermute(shard, axis, [(i, i ^ mask) for i in range(size)])  306 us
    ppermute x102, starting transfers between devices, swap(): return lax.ppermute(shard, axis, [(i, i ^ mask) for i in range(size)])  104 us
    dot_general x11, matrix products, contract_first(): lax.dot_general(left, right, (((0,), (0,)), ((), ())), preferred_element_...  80.4 us
    all_gather x5, waiting for transfers between devices, gathered(): return lax.all_gather(shard, 'fsdp', axis=0, tiled=True)  79.9 us
    unnamed x256, local copies, waits for them, and re-layouts  69.8 us
    pallas_call x1, Pallas kernels, units_forward(): pl.pallas_call(units_kernel, out_shape=[out] * 3, grid=(steps,), in_specs...  34.1 us
    pallas_call x1, Pallas kernels, product_last(): pl.pallas_call(product_kernel, out_shape=jax.ShapeDtypeStruct((rows, cols...  30.4 us
    pallas_call x9, Pallas kernels, place(): pl.pallas_call(functools.partial(place_kernel, plan, fixed, axis), out_sh...  30.3 us
  transfers between devices with their start and end apart: 112, of which 57 were waited for; matrix products, arithmetic and copies ran while one was open for 28% of the time, Pallas kernels for 14%

profile of v1, /device:TPU:0, one launch (start us, length us, event | category | flops | bytes accessed | tf_op | source)
XLA Modules:
  0.0 1008.9 jit_solution(12665258743558018668)
XLA Ops:
  21.4 5.1 collective-permute-start.8
  44.5 24.9 %collective-permute-done = s32[256]{0:T(256)S(1)} collective-permute-done((s32[256]{0:T(256)S(1)}, s32[256]{0:T(256)S(1)}, u32[]{:S(2)}, u32[]{:S(2)}) %collective-permute-start) | collective-permute-done | bytes 1056 | tf_op jit(solution)/shard_map/ppermute | solution.py:23
  77.2 7.1 collective-permute-done.12.refs_3_
  88.0 8.4 fusion.131
  127.9 19.5 %collective-permute-done.15.refs_2_ = bf16[1024,512]{1,0:T(8,128)(2,1)S(1)} collective-permute-done((bf16[1024,512]{1,0:T(8,128)(2,1)S(1)}, bf16[1024,512]{1,0:T(8,128)(2,1)S(1)}, u32[]{:S(2)}, u32[]{:S(2)}) %collective-permute-start.15) | collective-permute-done | bytes 1048608 | tf_op jit(solution)/shard_map/ppermute | solution.py:23
  150.8 9.0 collective-permute-done.17.refs_4_
  162.5 5.7 convolution_convert_fusion.12
  172.8 7.3 collective-permute-done.20
  198.6 24.2 %collective-permute-done.22.refs_2_ = bf16[256,2304]{1,0:T(8,128)(2,1)S(1)} collective-permute-done((bf16[256,2304]{1,0:T(8,128)(2,1)S(1)}, bf16[256,2304]{1,0:T(8,128)(2,1)S(1)}, u32[]{:S(2)}, u32[]{:S(2)}) %collective-permute-start.22) | collective-permute-done | bytes 1179680 | tf_op jit(solution)/shard_map/ppermute | solution.py:23
  226.9 8.9 collective-permute-done.23.refs_3_
  245.4 43.7 %all-gather.10.cloned.1.call-done.gate_ref.up_ref.refs_2_ = bf16[2304,4608]{1,0:T(8,128)(2,1)} async-done(((bf16[288,4608]{1,0:T(8,128)(2,1)}), bf16[2304,4608]{1,0:T(8,128)(2,1)}) %all-gather.10.cloned.1.call-update) | async-done | bytes 21233680 | tf_op jit(solution)/shard_map/all_gather | solution.py:620
  290.9 34.1 %shard_map.242 = (bf16[1024,2304]{1,0:T(8,128)(2,1)S(1)}, bf16[1024,2304]{1,0:T(8,128)(2,1)}, bf16[1024,2304]{1,0:T(8,128)(2,1)}) custom-call(bf16[1024,2304]{1,0:T(8,128)(2,1)} %bitcast.209, bf16[2304,4608]{1,0:T(8,128)(2,1)} %all-gather.10.cloned.1.call-done.gate_ref.up_ref.refs_2_, bf16[2304,4608]{1,0:T(8,128)(2,1)} %all-gather.10.cloned.1.call-done.gate_ref.up_ref.refs_2_), custom_call_target="tpu_custom_call" | custom-call | flops 21743271936 | bytes 40108032 | tf_op jit(solution)/shard_map/pallas_call | solution.py:432
  327.1 33.6 %all-gather.12.cloned.1.call-done.refs_0_ = bf16[2304,1536]{1,0:T(8,128)(2,1)} async-done(((bf16[288,1536]{1,0:T(8,128)(2,1)}), bf16[2304,1536]{1,0:T(8,128)(2,1)}) %all-gather.12.cloned.1.call-update) | async-done | bytes 7077904 | tf_op jit(solution)/shard_map/all_gather | solution.py:620
  366.4 7.7 convolution_convert_fusion.7
  377.8 8.5 collective-permute-done.26
  388.4 5.5 collective-permute-done.25
  417.0 7.3 collective-permute-done.31
  424.3 8.7 collective-permute-done.33
  440.3 7.8 collective-permute-done.35.refs_2_
  455.1 5.5 convolution_convert_fusion.8
  463.0 17.7 %collective-permute-done.40.refs_2_ = bf16[256,1536]{1,0:T(8,128)(2,1)S(1)} collective-permute-done((bf16[256,1536]{1,0:T(8,128)(2,1)S(1)}, bf16[256,1536]{1,0:T(8,128)(2,1)S(1)}, u32[]{:S(2)}, u32[]{:S(2)}) %collective-permute-start.40) | collective-permute-done | bytes 786464 | tf_op jit(solution)/shard_map/ppermute | solution.py:23
  494.1 8.4 convolution_convert_fusion.2
  502.5 6.5 convolution_convert_fusion.3.first_ref
  514.6 23.4 %shard_map.250 = (bf16[1024,2304]{1,0:T(8,128)(2,1)}, bf16[1024,2304]{1,0:T(8,128)(2,1)}) custom-call(bf16[1024,768]{1,0:T(8,128)(2,1)} %bitcast.219, bf16[1024,1536]{1,0:T(8,128)(2,1)} %bitcast.216, bf16[2304,768]{1,0:T(8,128)(2,1)} %copy-done.20, bf16[2304,1536]{1,0:T(8,128)(2,1)} %copy-done.6, bf16[1024,2304]{1,0:T(8,128)(2,1)} %get-tuple-element.52.refs_4_, ...), custom_call_target="tpu_custom_call" | custom-call | flops 10871635968 | bytes 34209792 | tf_op jit(solution)/shard_map/pallas_call | solution.py:471
  538.0 30.4 %shard_map.251 = bf16[1024,2304]{1,0:T(8,128)(2,1)S(1)} custom-call(bf16[1024,2304]{1,0:T(8,128)(2,1)} %get-tuple-element.58.refs_0_, bf16[1024,2304]{1,0:T(8,128)(2,1)} %get-tuple-element.59.refs_1_, bf16[2304,4608]{1,0:T(8,128)(2,1)} %all-gather.10.cloned.1.call-done.gate_ref.up_ref.refs_2_), custom_call_target="tpu_custom_call" | custom-call | flops 21743271936 | bytes 35389440 | tf_op jit(solution)/shard_map/pallas_call | solution.py:506
  570.6 10.4 %convolution_convert_fusion.1 = bf16[1152,2304]{1,0:T(8,128)(2,1)} fusion(bf16[1024,2304]{1,0:T(8,128)(2,1)} %get-tuple-element.58.refs_0_, bf16[1024,2304]{1,0:T(8,128)(2,1)} %copy-done.13, s32[]{:T(128)S(6)} %select_n.265), kind=kOutput, calls=%fused_computation.9 | convolution fusion | flops 5438472192 | bytes 12386308 | tf_op jit(solution)/shard_map/dot_general | solution.py:578
  581.6 8.6 collective-permute-done.50
  590.3 11.2 %fusion = bf16[1152,2304]{1,0:T(8,128)(2,1)} fusion(bf16[1024,2304]{1,0:T(8,128)(2,1)} %get-tuple-element.58.refs_0_, bf16[1152,2304]{1,0:T(8,128)(2,1)} %collective-permute-done.50, bf16[1024,2304]{1,0:T(8,128)(2,1)} %copy-done.13, s32[]{:T(128)S(6)} %select_n.264), kind=kOutput, calls=%fused_computation.6 | convolution fusion | flops 5443780608 | bytes 17694724 | tf_op jit(solution)/shard_map/dot_general | solution.py:578
  601.6 10.9 %convolution_convert_fusion = bf16[1152,2304]{1,0:T(8,128)(2,1)} fusion(bf16[1024,2304]{1,0:T(8,128)(2,1)} %get-tuple-element.59.refs_1_, bf16[1024,2304]{1,0:T(8,128)(2,1)} %copy-done.13, s32[]{:T(128)S(6)} %select_n.265), kind=kOutput, calls=%fused_computation.8 | convolution fusion | flops 5438472192 | bytes 12386308 | tf_op jit(solution)/shard_map/dot_general | solution.py:578
  638.0 6.3 collective-permute-done.53
  656.9 14.0 %collective-permute-done.46 = bf16[256,1024]{1,0:T(8,128)(2,1)S(1)} collective-permute-done((bf16[256,1024]{1,0:T(8,128)(2,1)S(1)}, bf16[256,1024]{1,0:T(8,128)(2,1)S(1)}, u32[]{:S(2)}, u32[]{:S(2)}) %collective-permute-start.46) | collective-permute-done | bytes 524320 | tf_op jit(solution)/shard_map/ppermute | solution.py:23
  676.8 10.4 %fusion.1 = bf16[1152,2304]{1,0:T(8,128)(2,1)} fusion(bf16[1024,2304]{1,0:T(8,128)(2,1)} %get-tuple-element.59.refs_1_, bf16[1152,2304]{1,0:T(8,128)(2,1)} %collective-permute-done.51, bf16[1024,2304]{1,0:T(8,128)(2,1)S(1)} %bitcast.211, s32[]{:T(128)S(6)} %select_n.264), kind=kOutput, calls=%fused_computation.7 | convolution fusion | flops 5443780608 | bytes 17694724 | tf_op jit(solution)/shard_map/dot_general | solution.py:578
  700.6 6.3 collective-permute-done.57
  743.3 6.6 reshape.787
  756.6 6.3 constant_dynamic-slice_fusion.1
  765.6 8.4 collective-permute-done.63
  776.6 5.6 collective-permute-done.67
  786.8 12.6 %shard_map.253 = bf16[1024,1024]{1,0:T(8,128)(2,1)} custom-call(bf16[1024,512]{1,0:T(8,128)(2,1)S(1)} %pad_maximum_fusion.12.grad_ref, bf16[1024,512]{1,0:T(8,128)(2,1)S(1)} %bitcast.220, bf16[1024,256]{1,0:T(8,128)(2,1)S(1)} %copy-done.34, bf16[1024,256]{1,0:T(8,128)(2,1)S(1)} %copy-done.32, s32[1024,1]{1,0:T(8,128)S(1)} %copy-done.33, ...), custom_call_target="tpu_custom_call" | custom-call | flops 10737418240 | bytes 4194304 | tf_op jit(solution)/shard_map/pallas_call | solution.py:354
  799.4 8.2 convolution_convert_fusion.4
  821.5 6.5 collective-permute-done.72
  836.2 13.4 %collective-permute-done.71 = bf16[256,1024]{1,0:T(8,128)(2,1)} collective-permute-done((bf16[256,1024]{1,0:T(8,128)(2,1)}, bf16[256,1024]{1,0:T(8,128)(2,1)}, u32[]{:S(2)}, u32[]{:S(2)}) %collective-permute-start.71) | collective-permute-done | bytes 524320 | tf_op jit(solution)/shard_map/ppermute | solution.py:23
  853.0 4.9 add_convert_fusion
  874.9 10.8 %collective-permute-done.95.refs_2_ = bf16[288,2304]{1,0:T(8,128)(2,1)} collective-permute-done((bf16[288,2304]{1,0:T(8,128)(2,1)}, bf16[288,2304]{1,0:T(8,128)(2,1)}, u32[]{:S(2)}, u32[]{:S(2)}) %collective-permute-start.95) | collective-permute-done | bytes 1327136 | tf_op jit(solution)/shard_map/ppermute | solution.py:23
  896.3 5.5 collective-permute-done.97.refs_4_
  909.2 7.4 shard_map.258
  938.9 5.8 collective-permute-done.99.refs_2_
  957.0 8.3 collective-permute-done.101.refs_4_
  976.1 6.9 shard_map.259
  (649 shorter events, 428.0 us)
Async XLA Ops:
  7.2 80.8 %all-gather.6.cloned.1.call-start = ((), (), s32[]{:S(2)}) async-start(), calls=%async_computation.5 | async-start | bytes 5308416 | tf_op jit(solution)/shard_map/all_gather | solution.py:620
  10.4 152.1 %all-gather.8.cloned.1.call-start = ((), (), s32[]{:S(2)}) async-start(), calls=%async_computation.6 | async-start | bytes 2949120 | tf_op jit(solution)/shard_map/all_gather | solution.py:620
  12.4 276.7 %all-gather.10.cloned.1.call-start = ((), (), s32[]{:S(2)}) async-start(), calls=%async_computation.7 | async-start | bytes 23887872 | tf_op jit(solution)/shard_map/all_gather | solution.py:620
  20.7 339.9 %all-gather.12.cloned.1.call-start = ((), (), s32[]{:S(2)}) async-start(), calls=%async_computation.8 | async-start | bytes 7962624 | tf_op jit(solution)/shard_map/all_gather | solution.py:620
  40.4 29.5 %collective-permute-start.11 = (bf16[256,2304]{1,0:T(8,128)(2,1)S(1)}, bf16[256,2304]{1,0:T(8,128)(2,1)S(1)}, u32[]{:S(2)}, u32[]{:S(2)}) collective-permute-start(bf16[256,2304]{1,0:T(8,128)(2,1)S(1)} %fusion.22.refs_0_), channel_id=1, source_target_pairs={{0,16},{8,24},{16,0},{24,8},{1,17},{9,25},{17,1},{25,9},{2,18},{10... | collective-permute-start | bytes 3538952 | tf_op jit(solution)/shard_map/ppermute | solution.py:23
  42.0 31.0 %collective-permute-start.10 = (bf16[256,2304]{1,0:T(8,128)(2,1)S(1)}, bf16[256,2304]{1,0:T(8,128)(2,1)S(1)}, u32[]{:S(2)}, u32[]{:S(2)}) collective-permute-start(bf16[256,2304]{1,0:T(8,128)(2,1)S(1)} %fusion.22.refs_0_), channel_id=1, source_target_pairs={{0,8},{8,0},{16,24},{24,16},{1,9},{9,1},{17,25},{25,17},{2,10},{10... | collective-permute-start | bytes 3538952 | tf_op jit(solution)/shard_map/ppermute | solution.py:23
  43.5 25.9 %collective-permute-start = (s32[256]{0:T(256)S(1)}, s32[256]{0:T(256)S(1)}, u32[]{:S(2)}, u32[]{:S(2)}) collective-permute-start(s32[256]{0:T(256)S(1)} %bitcast.237), channel_id=1, source_target_pairs={{0,8},{8,0},{16,24},{24,16},{1,9},{9,1},{17,25},{25,17},{2,10},{10... | collective-permute-start | bytes 3080 | tf_op jit(solution)/shard_map/ppermute | solution.py:23
  44.1 27.5 %collective-permute-start.1 = (s32[256]{0:T(256)S(1)}, s32[256]{0:T(256)S(1)}, u32[]{:S(2)}, u32[]{:S(2)}) collective-permute-start(s32[256]{0:T(256)S(1)} %bitcast.238), channel_id=1, source_target_pairs={{0,16},{8,24},{16,0},{24,8},{1,17},{9,25},{17,1},{25,9},{2,18},{10... | collective-permute-start | bytes 3080 | tf_op jit(solution)/shard_map/ppermute | solution.py:23
  124.8 22.6 %collective-permute-start.15 = (bf16[1024,512]{1,0:T(8,128)(2,1)S(1)}, bf16[1024,512]{1,0:T(8,128)(2,1)S(1)}, u32[]{:S(2)}, u32[]{:S(2)}) collective-permute-start(bf16[1024,512]{1,0:T(8,128)(2,1)S(1)} %copy.91.refs_0_), channel_id=1, source_target_pairs={{0,16},{8,24},{16,0},{24,8},{1,17},{9,25},{17,1},{25,9},{2,18},{10... | collective-permute-start | bytes 3145736 | tf_op jit(solution)/shard_map/ppermute | solution.py:23
  126.5 23.9 %collective-permute-start.14 = (bf16[1024,512]{1,0:T(8,128)(2,1)S(1)}, bf16[1024,512]{1,0:T(8,128)(2,1)S(1)}, u32[]{:S(2)}, u32[]{:S(2)}) collective-permute-start(bf16[1024,512]{1,0:T(8,128)(2,1)S(1)} %copy.91.refs_0_), channel_id=1, source_target_pairs={{0,8},{8,0},{16,24},{24,16},{1,9},{9,1},{17,25},{25,17},{2,10},{10... | collective-permute-start | bytes 3145736 | tf_op jit(solution)/shard_map/ppermute | solution.py:23
  195.2 27.6 %collective-permute-start.22 = (bf16[256,2304]{1,0:T(8,128)(2,1)S(1)}, bf16[256,2304]{1,0:T(8,128)(2,1)S(1)}, u32[]{:S(2)}, u32[]{:S(2)}) collective-permute-start(bf16[256,2304]{1,0:T(8,128)(2,1)S(1)} %multiply_convert_fusion.1.refs_0_), channel_id=1, source_target_pairs={{0,16},{8,24},{16,0},{24,8},{1,17},{9,25},{17,1},{25,9},{2,18},{10... | collective-permute-start | bytes 3538952 | tf_op jit(solution)/shard_map/ppermute | solution.py:23
  195.8 27.2 %collective-permute-start.21 = (bf16[256,2304]{1,0:T(8,128)(2,1)S(1)}, bf16[256,2304]{1,0:T(8,128)(2,1)S(1)}, u32[]{:S(2)}, u32[]{:S(2)}) collective-permute-start(bf16[256,2304]{1,0:T(8,128)(2,1)S(1)} %multiply_convert_fusion.1.refs_0_), channel_id=1, source_target_pairs={{0,8},{8,0},{16,24},{24,16},{1,9},{9,1},{17,25},{25,17},{2,10},{10... | collective-permute-start | bytes 3538952 | tf_op jit(solution)/shard_map/ppermute | solution.py:23
  290.1 112.8 %all-gather.14.cloned.1.call-start = ((), (), s32[]{:S(2)}) async-start(), calls=%async_computation.9 | async-start | bytes 3981312 | tf_op jit(solution)/shard_map/all_gather | solution.py:620
  360.7 209.9 %reduce-scatter.6.cloned.1.call-start = ((), (), s32[]{:S(2)}) async-start(), calls=%async_computation.10 | async-start | bytes 2211840 | tf_op jit(solution)/shard_map/reduce_scatter | solution.py:102
  387.8 27.8 %collective-permute-start.30 = (bf16[256,768]{1,0:T(8,128)(2,1)S(1)}, bf16[256,768]{1,0:T(8,128)(2,1)}, u32[]{:S(2)}, u32[]{:S(2)}) collective-permute-start(bf16[256,768]{1,0:T(8,128)(2,1)S(1)} %get-tuple-element.109), channel_id=1, source_target_pairs={{0,8},{8,0},{16,24},{24,16},{1,9},{9,1},{17,25},{25,17},{2,10},{10... | collective-permute-start | bytes 1179656 | tf_op jit(solution)/shard_map/ppermute | solution.py:23
  413.5 19.5 %collective-permute-start.33 = (bf16[256,768]{1,0:T(8,128)(2,1)}, bf16[256,768]{1,0:T(8,128)(2,1)}, u32[]{:S(2)}, u32[]{:S(2)}) collective-permute-start(bf16[256,768]{1,0:T(8,128)(2,1)} %get-tuple-element.123), channel_id=1, source_target_pairs={{0,24},{8,16},{16,8},{24,0},{1,25},{9,17},{17,9},{25,1},{2,26},{10... | collective-permute-start | bytes 1179656 | tf_op jit(solution)/shard_map/ppermute | solution.py:23
  460.6 27.4 %collective-permute-start.38 = (bf16[1152,768]{1,0:T(8,128)(2,1)}, bf16[1152,768]{1,0:T(8,128)(2,1)}, u32[]{:S(2)}, u32[]{:S(2)}) collective-permute-start(bf16[1152,768]{1,0:T(8,128)(2,1)} %convolution_convert_fusion.8), channel_id=1, source_target_pairs={{0,1},{1,0},{2,3},{3,2},{4,5},{5,4},{6,7},{7,6},{8,9},{9,8},{10,11... | collective-permute-start | bytes 5308424 | tf_op jit(solution)/shard_map/ppermute | solution.py:23
  460.7 20.0 %collective-permute-start.40 = (bf16[256,1536]{1,0:T(8,128)(2,1)S(1)}, bf16[256,1536]{1,0:T(8,128)(2,1)S(1)}, u32[]{:S(2)}, u32[]{:S(2)}) collective-permute-start(bf16[256,1536]{1,0:T(8,128)(2,1)S(1)} %slice.497.refs_0_), channel_id=1, source_target_pairs={{0,16},{8,24},{16,0},{24,8},{1,17},{9,25},{17,1},{25,9},{2,18},{10... | collective-permute-start | bytes 2359304 | tf_op jit(solution)/shard_map/ppermute | solution.py:23
  461.5 20.6 %collective-permute-start.39 = (bf16[256,1536]{1,0:T(8,128)(2,1)S(1)}, bf16[256,1536]{1,0:T(8,128)(2,1)S(1)}, u32[]{:S(2)}, u32[]{:S(2)}) collective-permute-start(bf16[256,1536]{1,0:T(8,128)(2,1)S(1)} %slice.497.refs_0_), channel_id=1, source_target_pairs={{0,8},{8,0},{16,24},{24,16},{1,9},{9,1},{17,25},{25,17},{2,10},{10... | collective-permute-start | bytes 2359304 | tf_op jit(solution)/shard_map/ppermute | solution.py:23
  502.5 184.8 %reduce-scatter.8.cloned.1.call-start = ((), (), s32[]{:S(2)}) async-start(), calls=%async_computation.11 | async-start | bytes 4423680 | tf_op jit(solution)/shard_map/reduce_scatter | solution.py:102
  581.6 200.5 %reduce-scatter.10.cloned.1.call-start = ((), (), s32[]{:S(2)}) async-start(), calls=%async_computation.12 | async-start | bytes 6635520 | tf_op jit(solution)/shard_map/reduce_scatter | solution.py:102
  601.6 301.5 %reduce-scatter.12.cloned.1.call-start = ((), (), s32[]{:S(2)}) async-start(), calls=%async_computation.13 | async-start | bytes 6635520 | tf_op jit(solution)/shard_map/reduce_scatter | solution.py:102
  612.6 64.2 %collective-permute-start.51 = (bf16[1152,2304]{1,0:T(8,128)(2,1)}, bf16[1152,2304]{1,0:T(8,128)(2,1)}, u32[]{:S(2)}, u32[]{:S(2)}) collective-permute-start(bf16[1152,2304]{1,0:T(8,128)(2,1)} %convolution_convert_fusion), channel_id=1, source_target_pairs={{0,1},{1,0},{2,3},{3,2},{4,5},{5,4},{6,7},{7,6},{8,9},{9,8},{10,11... | collective-permute-start | bytes 15925256 | tf_op jit(solution)/shard_map/ppermute | solution.py:23
  633.5 22.1 %collective-permute-start.44 = (bf16[256,1024]{1,0:T(8,128)(2,1)}, bf16[256,1024]{1,0:T(8,128)(2,1)S(1)}, u32[]{:S(2)}, u32[]{:S(2)}) collective-permute-start(bf16[256,1024]{1,0:T(8,128)(2,1)} %get-tuple-element.102), channel_id=1, source_target_pairs={{0,16},{8,24},{16,0},{24,8},{1,17},{9,25},{17,1},{25,9},{2,18},{10... | collective-permute-start | bytes 1572872 | tf_op jit(solution)/shard_map/ppermute | solution.py:23
  636.3 37.5 %collective-permute-start.49 = (bf16[256,1280]{1,0:T(8,128)(2,1)}, bf16[256,1280]{1,0:T(8,128)(2,1)S(1)}, u32[]{:S(2)}, u32[]{:S(2)}) collective-permute-start(bf16[256,1280]{1,0:T(8,128)(2,1)} %get-tuple-element.105), channel_id=1, source_target_pairs={{0,8},{8,0},{16,24},{24,16},{1,9},{9,1},{17,25},{25,17},{2,10},{10... | collective-permute-start | bytes 1966088 | tf_op jit(solution)/shard_map/ppermute | solution.py:23
  644.4 26.5 %collective-permute-start.46 = (bf16[256,1024]{1,0:T(8,128)(2,1)S(1)}, bf16[256,1024]{1,0:T(8,128)(2,1)S(1)}, u32[]{:S(2)}, u32[]{:S(2)}) collective-permute-start(bf16[256,1024]{1,0:T(8,128)(2,1)S(1)} %add_convert_fusion.8), channel_id=1, source_target_pairs={{0,8},{8,0},{16,24},{24,16},{1,9},{9,1},{17,25},{25,17},{2,10},{10... | collective-permute-start | bytes 1572872 | tf_op jit(solution)/shard_map/ppermute | solution.py:23
  645.7 28.0 %collective-permute-start.48 = (bf16[256,1280]{1,0:T(8,128)(2,1)S(1)}, bf16[256,1280]{1,0:T(8,128)(2,1)S(1)}, u32[]{:S(2)}, u32[]{:S(2)}) collective-permute-start(bf16[256,1280]{1,0:T(8,128)(2,1)S(1)} %add_convert_fusion.2), channel_id=1, source_target_pairs={{0,16},{8,24},{16,0},{24,8},{1,17},{9,25},{17,1},{25,9},{2,18},{10... | collective-permute-start | bytes 1966088 | tf_op jit(solution)/shard_map/ppermute | solution.py:23
  655.6 31.6 %collective-permute-start.55 = (bf16[288,512]{1,0:T(8,128)(2,1)}, bf16[288,512]{1,0:T(8,128)(2,1)}, u32[]{:S(2)}, u32[]{:S(2)}) collective-permute-start(bf16[288,512]{1,0:T(8,128)(2,1)} %slice.501), channel_id=1, source_target_pairs={{0,8},{8,0},{16,24},{24,16},{1,9},{9,1},{17,25},{25,17},{2,10},{10... | collective-permute-start | bytes 884744 | tf_op jit(solution)/shard_map/ppermute | solution.py:23
  687.3 19.7 %collective-permute-start.57 = (bf16[288,1536]{1,0:T(8,128)(2,1)}, bf16[288,1536]{1,0:T(8,128)(2,1)}, u32[]{:S(2)}, u32[]{:S(2)}) collective-permute-start(bf16[288,1536]{1,0:T(8,128)(2,1)} %reduce-scatter.8.cloned.1.call-done), channel_id=1, source_target_pairs={{0,16},{8,24},{16,0},{24,8},{1,17},{9,25},{17,1},{25,9},{2,18},{10... | collective-permute-start | bytes 2654216 | tf_op jit(solution)/shard_map/ppermute | solution.py:23
  688.1 21.3 %collective-permute-start.56 = (bf16[288,1536]{1,0:T(8,128)(2,1)}, bf16[288,1536]{1,0:T(8,128)(2,1)S(1)}, u32[]{:S(2)}, u32[]{:S(2)}) collective-permute-start(bf16[288,1536]{1,0:T(8,128)(2,1)} %reduce-scatter.8.cloned.1.call-done), channel_id=1, source_target_pairs={{0,8},{8,0},{16,24},{24,16},{1,9},{9,1},{17,25},{25,17},{2,10},{10... | collective-permute-start | bytes 2654216 | tf_op jit(solution)/shard_map/ppermute | solution.py:23
  692.7 261.2 %reduce-scatter.14.cloned.1.call-start = ((), (), s32[]{:S(2)}) async-start(), calls=%async_computation.14 | async-start | bytes 4792320 | tf_op jit(solution)/shard_map/reduce_scatter | solution.py:102
  708.8 67.8 %collective-permute-start.68 = (bf16[288,768]{1,0:T(8,128)(2,1)}, bf16[288,768]{1,0:T(8,128)(2,1)}, u32[]{:S(2)}, u32[]{:S(2)}) collective-permute-start(bf16[288,768]{1,0:T(8,128)(2,1)} %slice.507), channel_id=1, source_target_pairs={{0,8},{8,0},{16,24},{24,16},{1,9},{9,1},{17,25},{25,17},{2,10},{10... | collective-permute-start | bytes 1327112 | tf_op jit(solution)/shard_map/ppermute | solution.py:23
  750.6 23.7 %collective-permute-start.66 = (bf16[1024,256]{1,0:T(8,128)(2,1)}, bf16[1024,256]{1,0:T(8,128)(2,1)S(1)}, u32[]{:S(2)}, u32[]{:S(2)}) collective-permute-start(bf16[1024,256]{1,0:T(8,128)(2,1)} %copy-done.37), channel_id=1, source_target_pairs={{0,8},{8,0},{16,24},{24,16},{1,9},{9,1},{17,25},{25,17},{2,10},{10... | collective-permute-start | bytes 1572872 | tf_op jit(solution)/shard_map/ppermute | solution.py:23
  753.6 20.4 %collective-permute-start.63 = (bf16[1024,256]{1,0:T(8,128)(2,1)S(1)}, bf16[1024,256]{1,0:T(8,128)(2,1)S(1)}, u32[]{:S(2)}, u32[]{:S(2)}) collective-permute-start(bf16[1024,256]{1,0:T(8,128)(2,1)S(1)} %add_convert_fusion.7), channel_id=1, source_target_pairs={{0,8},{8,0},{16,24},{24,16},{1,9},{9,1},{17,25},{25,17},{2,10},{10... | collective-permute-start | bytes 1572872 | tf_op jit(solution)/shard_map/ppermute | solution.py:23
  755.1 21.1 %collective-permute-start.65 = (bf16[1024,256]{1,0:T(8,128)(2,1)S(1)}, bf16[1024,256]{1,0:T(8,128)(2,1)S(1)}, u32[]{:S(2)}, u32[]{:S(2)}) collective-permute-start(bf16[1024,256]{1,0:T(8,128)(2,1)S(1)} %add_convert_fusion.5), channel_id=1, source_target_pairs={{0,16},{8,24},{16,0},{24,8},{1,17},{9,25},{17,1},{25,9},{2,18},{10... | collective-permute-start | bytes 1572872 | tf_op jit(solution)/shard_map/ppermute | solution.py:23
  774.0 55.1 %collective-permute-start.85 = (bf16[4,256,576]{1,2,0:T(8,128)(2,1)}, bf16[4,256,576]{1,2,0:T(8,128)(2,1)}, u32[]{:S(2)}, u32[]{:S(2)}) collective-permute-start(bf16[4,256,576]{1,2,0:T(8,128)(2,1)} %bitcast.204), channel_id=1, source_target_pairs={{0,1},{1,0},{2,3},{3,2},{4,5},{5,4},{6,7},{7,6},{8,9},{9,8},{10,11... | collective-permute-start | bytes 3538952 | tf_op jit(solution)/shard_map/ppermute | solution.py:23
  815.1 38.0 %collective-permute-start.84 = (bf16[1152,1024]{1,0:T(8,128)(2,1)}, bf16[1152,1024]{1,0:T(8,128)(2,1)}, u32[]{:S(2)}, u32[]{:S(2)}) collective-permute-start(bf16[1152,1024]{1,0:T(8,128)(2,1)} %convolution_convert_fusion.5), channel_id=1, source_target_pairs={{0,1},{1,0},{2,3},{3,2},{4,5},{5,4},{6,7},{7,6},{8,9},{9,8},{10,11... | collective-permute-start | bytes 7077896 | tf_op jit(solution)/shard_map/ppermute | solution.py:23
  816.2 20.0 %collective-permute-start.69 = (bf16[256,1024]{1,0:T(8,128)(2,1)}, bf16[256,1024]{1,0:T(8,128)(2,1)}, u32[]{:S(2)}, u32[]{:S(2)}) collective-permute-start(bf16[256,1024]{1,0:T(8,128)(2,1)} %get-tuple-element.98), channel_id=1, source_target_pairs={{0,16},{8,24},{16,0},{24,8},{1,17},{9,25},{17,1},{25,9},{2,18},{10... | collective-permute-start | bytes 1572872 | tf_op jit(solution)/shard_map/ppermute | solution.py:23
  820.1 31.2 %collective-permute-start.74 = (bf16[256,1280]{1,0:T(8,128)(2,1)S(1)}, bf16[256,1280]{1,0:T(8,128)(2,1)}, u32[]{:S(2)}, u32[]{:S(2)}) collective-permute-start(bf16[256,1280]{1,0:T(8,128)(2,1)S(1)} %get-tuple-element.101), channel_id=1, source_target_pairs={{0,8},{8,0},{16,24},{24,16},{1,9},{9,1},{17,25},{25,17},{2,10},{10... | collective-permute-start | bytes 1966088 | tf_op jit(solution)/shard_map/ppermute | solution.py:23
  828.1 21.6 %collective-permute-start.71 = (bf16[256,1024]{1,0:T(8,128)(2,1)}, bf16[256,1024]{1,0:T(8,128)(2,1)}, u32[]{:S(2)}, u32[]{:S(2)}) collective-permute-start(bf16[256,1024]{1,0:T(8,128)(2,1)} %add_convert_fusion.3), channel_id=1, source_target_pairs={{0,8},{8,0},{16,24},{24,16},{1,9},{9,1},{17,25},{25,17},{2,10},{10... | collective-permute-start | bytes 1572872 | tf_op jit(solution)/shard_map/ppermute | solution.py:23
  829.1 22.2 %collective-permute-start.73 = (bf16[256,1280]{1,0:T(8,128)(2,1)}, bf16[256,1280]{1,0:T(8,128)(2,1)}, u32[]{:S(2)}, u32[]{:S(2)}) collective-permute-start(bf16[256,1280]{1,0:T(8,128)(2,1)} %add_convert_fusion.1), channel_id=1, source_target_pairs={{0,16},{8,24},{16,0},{24,8},{1,17},{9,25},{17,1},{25,9},{2,18},{10... | collective-permute-start | bytes 1966088 | tf_op jit(solution)/shard_map/ppermute | solution.py:23
  858.0 27.7 %collective-permute-start.95 = (bf16[288,2304]{1,0:T(8,128)(2,1)}, bf16[288,2304]{1,0:T(8,128)(2,1)}, u32[]{:S(2)}, u32[]{:S(2)}) collective-permute-start(bf16[288,2304]{1,0:T(8,128)(2,1)} %reduce-scatter.10.cloned.1.call-done.refs_0_), channel_id=1, source_target_pairs={{0,16},{8,24},{16,0},{24,8},{1,17},{9,25},{17,1},{25,9},{2,18},{10... | collective-permute-start | bytes 3981320 | tf_op jit(solution)/shard_map/ppermute | solution.py:23
  858.3 29.3 %collective-permute-start.94 = (bf16[288,2304]{1,0:T(8,128)(2,1)}, bf16[288,2304]{1,0:T(8,128)(2,1)}, u32[]{:S(2)}, u32[]{:S(2)}) collective-permute-start(bf16[288,2304]{1,0:T(8,128)(2,1)} %reduce-scatter.10.cloned.1.call-done.refs_0_), channel_id=1, source_target_pairs={{0,8},{8,0},{16,24},{24,16},{1,9},{9,1},{17,25},{25,17},{2,10},{10... | collective-permute-start | bytes 3981320 | tf_op jit(solution)/shard_map/ppermute | solution.py:23
  888.8 20.4 %collective-permute-start.96 = (bf16[288,1024]{1,0:T(8,128)(2,1)S(1)}, bf16[288,1024]{1,0:T(8,128)(2,1)S(1)}, u32[]{:S(2)}, u32[]{:S(2)}) collective-permute-start(bf16[288,1024]{1,0:T(8,128)(2,1)S(1)} %slice.534), channel_id=1, source_target_pairs={{0,16},{8,24},{16,0},{24,8},{1,17},{9,25},{17,1},{25,9},{2,18},{10... | collective-permute-start | bytes 1769480 | tf_op jit(solution)/shard_map/ppermute | solution.py:23
  917.5 27.2 %collective-permute-start.99 = (bf16[288,2304]{1,0:T(8,128)(2,1)}, bf16[288,2304]{1,0:T(8,128)(2,1)S(1)}, u32[]{:S(2)}, u32[]{:S(2)}) collective-permute-start(bf16[288,2304]{1,0:T(8,128)(2,1)} %reduce-scatter.12.cloned.1.call-done.refs_0_), channel_id=1, source_target_pairs={{0,16},{8,24},{16,0},{24,8},{1,17},{9,25},{17,1},{25,9},{2,18},{10... | collective-permute-start | bytes 3981320 | tf_op jit(solution)/shard_map/ppermute | solution.py:23
  918.8 28.8 %collective-permute-start.98 = (bf16[288,2304]{1,0:T(8,128)(2,1)}, bf16[288,2304]{1,0:T(8,128)(2,1)}, u32[]{:S(2)}, u32[]{:S(2)}) collective-permute-start(bf16[288,2304]{1,0:T(8,128)(2,1)} %reduce-scatter.12.cloned.1.call-done.refs_0_), channel_id=1, source_target_pairs={{0,8},{8,0},{16,24},{24,16},{1,9},{9,1},{17,25},{25,17},{2,10},{10... | collective-permute-start | bytes 3981320 | tf_op jit(solution)/shard_map/ppermute | solution.py:23
  945.7 19.6 %collective-permute-start.101 = (bf16[288,1280]{1,0:T(8,128)(2,1)}, bf16[288,1280]{1,0:T(8,128)(2,1)S(1)}, u32[]{:S(2)}, u32[]{:S(2)}) collective-permute-start(bf16[288,1280]{1,0:T(8,128)(2,1)} %slice.543), channel_id=1, source_target_pairs={{0,8},{8,0},{16,24},{24,16},{1,9},{9,1},{17,25},{25,17},{2,10},{10... | collective-permute-start | bytes 2211848 | tf_op jit(solution)/shard_map/ppermute | solution.py:23
  949.5 26.5 %collective-permute-start.100 = (bf16[288,1024]{1,0:T(8,128)(2,1)}, bf16[288,1024]{1,0:T(8,128)(2,1)S(1)}, u32[]{:S(2)}, u32[]{:S(2)}) collective-permute-start(bf16[288,1024]{1,0:T(8,128)(2,1)} %slice.542), channel_id=1, source_target_pairs={{0,16},{8,24},{16,0},{24,8},{1,17},{9,25},{17,1},{25,9},{2,18},{10... | collective-permute-start | bytes 1769480 | tf_op jit(solution)/shard_map/ppermute | solution.py:23
  (179 other events, 1947.6 us)
Sparse Core Ops, SparseCore 0:
  10.5 54.8 all-gather.5
  67.6 32.5 all-gather.7
  102.4 186.6 all-gather.9
  291.1 69.4 all-gather.11
  362.7 40.0 all-gather.13
  502.6 36.0 reduce-scatter.5
  581.7 63.9 reduce-scatter.7
  648.7 95.0 reduce-scatter.9
  746.7 95.3 reduce-scatter.11
  863.0 70.8 reduce-scatter.13

commit v2 on v1

--- a/solution.py
+++ b/solution.py
@@ -718,7 +718,6 @@
 
     inverse_a = inverse_rms(rows)
     normed = join(gather_pieces((rows * inverse_a * gain_a).astype(low)))
-    normed_apart = cores_apart(normed, n_fsdp) if tiled else normed
     places = jnp.concatenate(gather_blocks(positions[0], halves=False), axis=0)
     angles = places.astype(wide)[:, None] * frequencies(HD // 2, HD)
     cosine, sine = jnp.cos(angles), jnp.sin(angles)
@@ -798,7 +797,7 @@
 
     arrived = [piece[0] for piece in down_pieces[1][1:3]]
     grad_branch_cols = to_columns(after(grad_branch.astype(low), *arrived))
-    out_term = chip_term(contract_first(attn_all, grad_branch_cols))
+    out_term = contract_first(attn_all, grad_branch_cols).astype(low)
     grad_attn_all = contract_last(grad_branch_cols, full_out).astype(low)
     if tiled:
         parts = split_columns(grad_attn_all, c, n_ctx, cut_at(query_cols))
@@ -811,6 +810,7 @@
         parts = [block_order(part_, k) for k, part_ in enumerate(parts)]
         grad_attn = scatter_sum(halved(parts)).astype(low)
     grad_attn = after(grad_attn, gate_sum, *[piece[0] for piece in down_pieces[1]])
+    gate_pieces = gather_pieces(after(gate_sum, grad_attn))
     grad_projected = attention_back(
         grad_attn,
         queries.reshape(length, query_cols),
@@ -821,11 +821,14 @@
         sine,
         scale,
     )
-    qkv_term = weight_term(normed_apart, grad_projected)
-    pad = (qkv_term.shape[0] - out_term.shape[0]) // chips
-    out_term = jnp.pad(out_term.reshape(chips, -1, out_cols), ((0, 0), (0, pad), (0, 0)))
+    grad_projected = after(grad_projected, *[piece[0] for piece in gate_pieces[1:3]])
+    qkv_term = contract_first(normed, grad_projected).astype(low)
+    pad = (qkv_term.shape[0] - out_term.shape[0]) // n_fsdp
+    out_term = jnp.pad(out_term.reshape(n_fsdp, -1, out_cols), ((0, 0), (0, pad), (0, 0)))
     out_term = out_term.reshape(qkv_term.shape[0], out_cols)
-    attn_sum = fsdp_sum(jnp.concatenate([qkv_term, out_term], axis=1))
+    attn_sum = lax.psum_scatter(
+        jnp.concatenate([qkv_term, out_term], axis=1), "fsdp", scatter_dimension=0, tiled=True
+    )
     qkv_sum = attn_sum[:, : qkv_term.shape[1]]
     out_sum = attn_sum[: attn_sum.shape[0] - pad, qkv_term.shape[1] :]
     grad_normed = contract_last(grad_projected, full_qkv).astype(low)
@@ -874,13 +877,13 @@
 
     out_grad = jnp.concatenate(in_order(gather_blocks(out_sum)), axis=1).astype(wide)
 
-    def all_units(total):
+    def all_units(gathered_pieces):
         if not tiled:
-            blocks = gather_blocks(total)
+            blocks = as_blocks(gathered_pieces)
             blocks = [b.reshape(b.shape[0], n_fsdp, part) for b in in_order(blocks)]
             return jnp.stack(blocks, axis=2).reshape(gate_weight.shape).astype(wide)
         pieces, tails = [], []
-        for array, k, start in gather_pieces(total):
+        for array, k, start in gathered_pieces:
             moves = []
             for b in range(n_fsdp):
                 begin = unit_place(b, n_fsdp, main, rest) - start
@@ -907,8 +910,9 @@
             [(b * 128, 128, (b + 1) * ff_rows - 128) for b in range(n_fsdp)],
         )
 
-    gate_grad = all_units(after(gate_sum, qkv_term))
-    up_grad = all_units(up_sum)
+    gate_arrays = lax.optimization_barrier(([piece[0] for piece in gate_pieces], qkv_term))[0]
+    gate_grad = all_units([(a, *piece[1:]) for a, piece in zip(gate_arrays, gate_pieces)])
+    up_grad = all_units(gather_pieces(up_sum))
     down_halves = zip(*[as_blocks(pieces) for pieces in down_pieces[::-1]])
     down_blocks = [jnp.concatenate(block, axis=1) for block in down_halves]
     down_blocks[0] = after(down_blocks[0], qkv_term)

time: 1020 us -> 1000 us (0.980)
  local copies, waits for them, and re-layouts: 145 us -> 109 us
  waiting for transfers between devices: 386 us -> 411 us
    ppermute x102 -> x100, waiting for transfers between devices: 306 us -> 329 us  [swap(): return lax.ppermute(shard, axis, [(i, i ^ mask) for i in range(size)])]
    unnamed x256 -> x247, local copies, waits for them, and re-layouts: 69.8 us -> 54.2 us
    ppermute x102 -> x100, starting transfers between devices: 104 us -> 110 us  [swap(): return lax.ppermute(shard, axis, [(i, i ^ mask) for i in range(size)])]
    dot_general x11 -> x10, matrix products: 80.4 us -> 81.4 us  [contract_first(): lax.dot_general(left, right, (((0,), (0,)), ((), ())), preferred_element_...]
  transfers between devices with their start and end apart: 112 -> 110, of which waited for: 57 -> 53; matrix products, arithmetic and copies ran while one was open for 28% -> 25% of each run, Pallas kernels for 14% -> 14%
where the time goes in v2:
time: 1000 us; the launch traced here: 995 us
  waiting for transfers between devices  411 us (41%)
  Pallas kernels  147 us (15%)
  matrix products  128 us (13%)
  starting transfers between devices  111 us (11%)
  local copies, waits for them, and re-layouts  109 us (11%)
  other arithmetic  73.2 us (7%)
  between operations  16.5 us (2%)
    ppermute x100, waiting for transfers between devices, swap(): return lax.ppermute(shard, axis, [(i, i ^ mask) for i in range(size)])  329 us
    ppermute x100, starting transfers between devices, swap(): return lax.ppermute(shard, axis, [(i, i ^ mask) for i in range(size)])  110 us
    all_gather x5, waiting for transfers between devices, gathered(): return lax.all_gather(shard, 'fsdp', axis=0, tiled=True)  82.6 us
    dot_general x10, matrix products, contract_first(): lax.dot_general(left, right, (((0,), (0,)), ((), ())), preferred_element_...  81.4 us
    unnamed x247, local copies, waits for them, and re-layouts  54.2 us
    pallas_call x1, Pallas kernels, units_forward(): pl.pallas_call(units_kernel, out_shape=[out] * 3, grid=(steps,), in_specs...  34.1 us
    pallas_call x1, Pallas kernels, product_last(): pl.pallas_call(product_kernel, out_shape=jax.ShapeDtypeStruct((rows, cols...  30.4 us
    pallas_call x9, Pallas kernels, place(): pl.pallas_call(functools.partial(place_kernel, plan, fixed, axis), out_sh...  29.2 us
  transfers between devices with their start and end apart: 110, of which 53 were waited for; matrix products, arithmetic and copies ran while one was open for 25% of the time, Pallas kernels for 14%

profile of v2, /device:TPU:0, one launch (start us, length us, event | category | flops | bytes accessed | tf_op | source)
XLA Modules:
  0.0 995.1 jit_solution(11426089370402734521)
XLA Ops:
  44.0 24.8 %collective-permute-done = s32[256]{0:T(256)S(1)} collective-permute-done((s32[256]{0:T(256)S(1)}, s32[256]{0:T(256)S(1)}, u32[]{:S(2)}, u32[]{:S(2)}) %collective-permute-start) | collective-permute-done | bytes 1056 | tf_op jit(solution)/shard_map/ppermute | solution.py:23
  76.7 7.1 collective-permute-done.12.refs_3_
  87.4 8.4 fusion.126
  126.2 19.0 %collective-permute-done.15.refs_2_ = bf16[1024,512]{1,0:T(8,128)(2,1)S(1)} collective-permute-done((bf16[1024,512]{1,0:T(8,128)(2,1)S(1)}, bf16[1024,512]{1,0:T(8,128)(2,1)S(1)}, u32[]{:S(2)}, u32[]{:S(2)}) %collective-permute-start.15) | collective-permute-done | bytes 1048608 | tf_op jit(solution)/shard_map/ppermute | solution.py:23
  149.1 8.5 collective-permute-done.17.refs_4_
  160.2 5.7 convolution_convert_fusion.12
  170.5 7.2 collective-permute-done.20
  196.0 23.7 %collective-permute-done.22.refs_2_ = bf16[256,2304]{1,0:T(8,128)(2,1)S(1)} collective-permute-done((bf16[256,2304]{1,0:T(8,128)(2,1)S(1)}, bf16[256,2304]{1,0:T(8,128)(2,1)S(1)}, u32[]{:S(2)}, u32[]{:S(2)}) %collective-permute-start.22) | collective-permute-done | bytes 1179680 | tf_op jit(solution)/shard_map/ppermute | solution.py:23
  224.5 8.0 collective-permute-done.23.refs_3_
  242.0 47.1 %all-gather.10.cloned.1.call-done.gate_ref.up_ref.refs_2_ = bf16[2304,4608]{1,0:T(8,128)(2,1)} async-done(((bf16[288,4608]{1,0:T(8,128)(2,1)}), bf16[2304,4608]{1,0:T(8,128)(2,1)}) %all-gather.10.cloned.1.call-update) | async-done | bytes 21233680 | tf_op jit(solution)/shard_map/all_gather | solution.py:620
  290.9 34.1 %shard_map.242 = (bf16[1024,2304]{1,0:T(8,128)(2,1)S(1)}, bf16[1024,2304]{1,0:T(8,128)(2,1)}, bf16[1024,2304]{1,0:T(8,128)(2,1)}) custom-call(bf16[1024,2304]{1,0:T(8,128)(2,1)} %bitcast.198, bf16[2304,4608]{1,0:T(8,128)(2,1)} %all-gather.10.cloned.1.call-done.gate_ref.up_ref.refs_2_, bf16[2304,4608]{1,0:T(8,128)(2,1)} %all-gather.10.cloned.1.call-done.gate_ref.up_ref.refs_2_), custom_call_target="tpu_custom_call" | custom-call | flops 21743271936 | bytes 40108032 | tf_op jit(solution)/shard_map/pallas_call | solution.py:432
  327.1 33.5 %all-gather.12.cloned.1.call-done.refs_0_ = bf16[2304,1536]{1,0:T(8,128)(2,1)} async-done(((bf16[288,1536]{1,0:T(8,128)(2,1)}), bf16[2304,1536]{1,0:T(8,128)(2,1)}) %all-gather.12.cloned.1.call-update) | async-done | bytes 7077904 | tf_op jit(solution)/shard_map/all_gather | solution.py:620
  366.3 7.7 convolution_convert_fusion.7
  377.7 8.4 collective-permute-done.26
  388.3 5.5 collective-permute-done.25
  416.5 7.3 collective-permute-done.31
  423.7 8.8 collective-permute-done.33
  439.7 7.8 collective-permute-done.35.refs_2_
  454.6 5.5 convolution_convert_fusion.8
  462.5 17.7 %collective-permute-done.40.refs_2_ = bf16[256,1536]{1,0:T(8,128)(2,1)S(1)} collective-permute-done((bf16[256,1536]{1,0:T(8,128)(2,1)S(1)}, bf16[256,1536]{1,0:T(8,128)(2,1)S(1)}, u32[]{:S(2)}, u32[]{:S(2)}) %collective-permute-start.40) | collective-permute-done | bytes 786464 | tf_op jit(solution)/shard_map/ppermute | solution.py:23
  493.6 8.3 convolution_convert_fusion.2
  501.9 6.5 convolution_convert_fusion.3.first_ref
  513.6 23.6 %shard_map.250 = (bf16[1024,2304]{1,0:T(8,128)(2,1)}, bf16[1024,2304]{1,0:T(8,128)(2,1)}) custom-call(bf16[1024,768]{1,0:T(8,128)(2,1)} %bitcast.208, bf16[1024,1536]{1,0:T(8,128)(2,1)} %bitcast.205, bf16[2304,768]{1,0:T(8,128)(2,1)} %copy-done.13, bf16[2304,1536]{1,0:T(8,128)(2,1)} %copy-done.3, bf16[1024,2304]{1,0:T(8,128)(2,1)} %get-tuple-element.58.refs_4_, ...), custom_call_target="tpu_custom_call" | custom-call | flops 10871635968 | bytes 34209792 | tf_op jit(solution)/shard_map/pallas_call | solution.py:471
  537.1 30.4 %shard_map.251 = bf16[1024,2304]{1,0:T(8,128)(2,1)S(1)} custom-call(bf16[1024,2304]{1,0:T(8,128)(2,1)} %get-tuple-element.64.refs_0_, bf16[1024,2304]{1,0:T(8,128)(2,1)} %get-tuple-element.65.refs_1_, bf16[2304,4608]{1,0:T(8,128)(2,1)} %all-gather.10.cloned.1.call-done.gate_ref.up_ref.refs_2_), custom_call_target="tpu_custom_call" | custom-call | flops 21743271936 | bytes 35389440 | tf_op jit(solution)/shard_map/pallas_call | solution.py:506
  569.6 10.4 %convolution_convert_fusion.1 = bf16[1152,2304]{1,0:T(8,128)(2,1)} fusion(bf16[1024,2304]{1,0:T(8,128)(2,1)} %get-tuple-element.64.refs_0_, bf16[1024,2304]{1,0:T(8,128)(2,1)} %copy-done.8, s32[]{:T(128)S(6)} %select_n.256), kind=kOutput, calls=%fused_computation.9 | convolution fusion | flops 5438472192 | bytes 12386308 | tf_op jit(solution)/shard_map/dot_general | solution.py:578
  580.6 8.6 collective-permute-done.50
  589.2 11.2 %fusion = bf16[1152,2304]{1,0:T(8,128)(2,1)} fusion(bf16[1024,2304]{1,0:T(8,128)(2,1)} %get-tuple-element.64.refs_0_, bf16[1152,2304]{1,0:T(8,128)(2,1)} %collective-permute-done.50, bf16[1024,2304]{1,0:T(8,128)(2,1)} %copy-done.8, s32[]{:T(128)S(6)} %select_n.255), kind=kOutput, calls=%fused_computation.6 | convolution fusion | flops 5443780608 | bytes 17694724 | tf_op jit(solution)/shard_map/dot_general | solution.py:578
  600.6 9.5 convolution_convert_fusion
  626.6 8.2 collective-permute-done.45
  641.7 10.6 %fusion.1 = bf16[1152,2304]{1,0:T(8,128)(2,1)} fusion(bf16[1024,2304]{1,0:T(8,128)(2,1)} %get-tuple-element.65.refs_1_, bf16[1152,2304]{1,0:T(8,128)(2,1)S(1)} %collective-permute-done.51, bf16[1024,2304]{1,0:T(8,128)(2,1)} %copy-done.8, s32[]{:T(128)S(6)} %select_n.255), kind=kOutput, calls=%fused_computation.7 | convolution fusion | flops 5443780608 | bytes 17694724 | tf_op jit(solution)/shard_map/dot_general | solution.py:578
  653.4 15.7 %collective-permute-done.46 = bf16[256,1024]{1,0:T(8,128)(2,1)} collective-permute-done((bf16[256,1024]{1,0:T(8,128)(2,1)}, bf16[256,1024]{1,0:T(8,128)(2,1)}, u32[]{:S(2)}, u32[]{:S(2)}) %collective-permute-start.46) | collective-permute-done | bytes 524320 | tf_op jit(solution)/shard_map/ppermute | solution.py:23
  684.5 10.2 %collective-permute-done.57 = bf16[288,1536]{1,0:T(8,128)(2,1)S(1)} collective-permute-done((bf16[288,1536]{1,0:T(8,128)(2,1)}, bf16[288,1536]{1,0:T(8,128)(2,1)S(1)}, u32[]{:S(2)}, u32[]{:S(2)}) %collective-permute-start.57) | collective-permute-done | bytes 884768 | tf_op jit(solution)/shard_map/ppermute | solution.py:23
  701.0 7.4 collective-permute-done.60
  723.3 9.8 collective-permute-done.62
  745.1 11.3 %collective-permute-done.63 = bf16[1024,256]{1,0:T(8,128)(2,1)S(1)} collective-permute-done((bf16[1024,256]{1,0:T(8,128)(2,1)S(1)}, bf16[1024,256]{1,0:T(8,128)(2,1)S(1)}, u32[]{:S(2)}, u32[]{:S(2)}) %collective-permute-start.63) | collective-permute-done | bytes 524320 | tf_op jit(solution)/shard_map/ppermute | solution.py:23
  756.9 7.4 collective-permute-done.68
  766.9 6.6 convolution_convert_fusion.10
  784.8 12.5 %shard_map.253 = bf16[1024,1024]{1,0:T(8,128)(2,1)} custom-call(bf16[1024,512]{1,0:T(8,128)(2,1)S(1)} %pad_maximum_fusion.12.grad_ref, bf16[1024,512]{1,0:T(8,128)(2,1)S(1)} %bitcast.209, bf16[1024,256]{1,0:T(8,128)(2,1)S(1)} %copy-done.29, bf16[1024,256]{1,0:T(8,128)(2,1)S(1)} %copy-done.27, s32[1024,1]{1,0:T(8,128)S(1)} %copy-done.28, ...), custom_call_target="tpu_custom_call" | custom-call | flops 10737418240 | bytes 4194304 | tf_op jit(solution)/shard_map/pallas_call | solution.py:354
  797.3 8.6 convolution_convert_fusion.4
  805.9 7.1 pad_maximum_fusion
  822.4 7.7 convolution_convert_fusion.5
  850.5 7.3 collective-permute-done.94.refs_3_
  859.3 6.1 collective-permute-done.95.refs_4_
  869.2 18.8 %collective-permute-done.73 = bf16[256,1024]{1,0:T(8,128)(2,1)S(1)} collective-permute-done((bf16[256,1024]{1,0:T(8,128)(2,1)S(1)}, bf16[256,1024]{1,0:T(8,128)(2,1)S(1)}, u32[]{:S(2)}, u32[]{:S(2)}) %collective-permute-start.73) | collective-permute-done | bytes 524320 | tf_op jit(solution)/shard_map/ppermute | solution.py:23
  895.0 6.5 shard_map.257
  924.5 7.2 collective-permute-done.97.refs_2_
  944.0 8.3 collective-permute-done.99.refs_4_
  963.1 6.9 shard_map.258
  (630 shorter events, 390.2 us)
Async XLA Ops:
  7.2 80.2 %all-gather.6.cloned.1.call-start = ((), (), s32[]{:S(2)}) async-start(), calls=%async_computation.5 | async-start | bytes 5308416 | tf_op jit(solution)/shard_map/all_gather | solution.py:620
  10.4 149.8 %all-gather.8.cloned.1.call-start = ((), (), s32[]{:S(2)}) async-start(), calls=%async_computation.6 | async-start | bytes 2949120 | tf_op jit(solution)/shard_map/all_gather | solution.py:620
  12.4 276.7 %all-gather.10.cloned.1.call-start = ((), (), s32[]{:S(2)}) async-start(), calls=%async_computation.7 | async-start | bytes 23887872 | tf_op jit(solution)/shard_map/all_gather | solution.py:620
  20.7 339.8 %all-gather.12.cloned.1.call-start = ((), (), s32[]{:S(2)}) async-start(), calls=%async_computation.8 | async-start | bytes 7962624 | tf_op jit(solution)/shard_map/all_gather | solution.py:620
  39.9 29.5 %collective-permute-start.11 = (bf16[256,2304]{1,0:T(8,128)(2,1)S(1)}, bf16[256,2304]{1,0:T(8,128)(2,1)S(1)}, u32[]{:S(2)}, u32[]{:S(2)}) collective-permute-start(bf16[256,2304]{1,0:T(8,128)(2,1)S(1)} %fusion.22.refs_0_), channel_id=1, source_target_pairs={{0,16},{8,24},{16,0},{24,8},{1,17},{9,25},{17,1},{25,9},{2,18},{10... | collective-permute-start | bytes 3538952 | tf_op jit(solution)/shard_map/ppermute | solution.py:23
  41.5 30.9 %collective-permute-start.10 = (bf16[256,2304]{1,0:T(8,128)(2,1)S(1)}, bf16[256,2304]{1,0:T(8,128)(2,1)S(1)}, u32[]{:S(2)}, u32[]{:S(2)}) collective-permute-start(bf16[256,2304]{1,0:T(8,128)(2,1)S(1)} %fusion.22.refs_0_), channel_id=1, source_target_pairs={{0,8},{8,0},{16,24},{24,16},{1,9},{9,1},{17,25},{25,17},{2,10},{10... | collective-permute-start | bytes 3538952 | tf_op jit(solution)/shard_map/ppermute | solution.py:23
  43.0 25.9 %collective-permute-start = (s32[256]{0:T(256)S(1)}, s32[256]{0:T(256)S(1)}, u32[]{:S(2)}, u32[]{:S(2)}) collective-permute-start(s32[256]{0:T(256)S(1)} %bitcast.227), channel_id=1, source_target_pairs={{0,8},{8,0},{16,24},{24,16},{1,9},{9,1},{17,25},{25,17},{2,10},{10... | collective-permute-start | bytes 3080 | tf_op jit(solution)/shard_map/ppermute | solution.py:23
  43.6 27.5 %collective-permute-start.1 = (s32[256]{0:T(256)S(1)}, s32[256]{0:T(256)S(1)}, u32[]{:S(2)}, u32[]{:S(2)}) collective-permute-start(s32[256]{0:T(256)S(1)} %bitcast.228), channel_id=1, source_target_pairs={{0,16},{8,24},{16,0},{24,8},{1,17},{9,25},{17,1},{25,9},{2,18},{10... | collective-permute-start | bytes 3080 | tf_op jit(solution)/shard_map/ppermute | solution.py:23
  122.8 22.4 %collective-permute-start.15 = (bf16[1024,512]{1,0:T(8,128)(2,1)S(1)}, bf16[1024,512]{1,0:T(8,128)(2,1)S(1)}, u32[]{:S(2)}, u32[]{:S(2)}) collective-permute-start(bf16[1024,512]{1,0:T(8,128)(2,1)S(1)} %copy.71.refs_0_), channel_id=1, source_target_pairs={{0,16},{8,24},{16,0},{24,8},{1,17},{9,25},{17,1},{25,9},{2,18},{10... | collective-permute-start | bytes 3145736 | tf_op jit(solution)/shard_map/ppermute | solution.py:23
  124.7 23.6 %collective-permute-start.14 = (bf16[1024,512]{1,0:T(8,128)(2,1)S(1)}, bf16[1024,512]{1,0:T(8,128)(2,1)S(1)}, u32[]{:S(2)}, u32[]{:S(2)}) collective-permute-start(bf16[1024,512]{1,0:T(8,128)(2,1)S(1)} %copy.71.refs_0_), channel_id=1, source_target_pairs={{0,8},{8,0},{16,24},{24,16},{1,9},{9,1},{17,25},{25,17},{2,10},{10... | collective-permute-start | bytes 3145736 | tf_op jit(solution)/shard_map/ppermute | solution.py:23
  192.5 27.3 %collective-permute-start.22 = (bf16[256,2304]{1,0:T(8,128)(2,1)S(1)}, bf16[256,2304]{1,0:T(8,128)(2,1)S(1)}, u32[]{:S(2)}, u32[]{:S(2)}) collective-permute-start(bf16[256,2304]{1,0:T(8,128)(2,1)S(1)} %multiply_convert_fusion.1.refs_0_), channel_id=1, source_target_pairs={{0,16},{8,24},{16,0},{24,8},{1,17},{9,25},{17,1},{25,9},{2,18},{10... | collective-permute-start | bytes 3538952 | tf_op jit(solution)/shard_map/ppermute | solution.py:23
  193.5 27.1 %collective-permute-start.21 = (bf16[256,2304]{1,0:T(8,128)(2,1)S(1)}, bf16[256,2304]{1,0:T(8,128)(2,1)S(1)}, u32[]{:S(2)}, u32[]{:S(2)}) collective-permute-start(bf16[256,2304]{1,0:T(8,128)(2,1)S(1)} %multiply_convert_fusion.1.refs_0_), channel_id=1, source_target_pairs={{0,8},{8,0},{16,24},{24,16},{1,9},{9,1},{17,25},{25,17},{2,10},{10... | collective-permute-start | bytes 3538952 | tf_op jit(solution)/shard_map/ppermute | solution.py:23
  290.1 112.2 %all-gather.14.cloned.1.call-start = ((), (), s32[]{:S(2)}) async-start(), calls=%async_computation.9 | async-start | bytes 3981312 | tf_op jit(solution)/shard_map/all_gather | solution.py:620
  360.6 209.0 %reduce-scatter.6.cloned.1.call-start = ((), (), s32[]{:S(2)}) async-start(), calls=%async_computation.10 | async-start | bytes 2211840 | tf_op jit(solution)/shard_map/reduce_scatter | solution.py:102
  387.8 27.3 %collective-permute-start.30 = (bf16[256,768]{1,0:T(8,128)(2,1)S(1)}, bf16[256,768]{1,0:T(8,128)(2,1)}, u32[]{:S(2)}, u32[]{:S(2)}) collective-permute-start(bf16[256,768]{1,0:T(8,128)(2,1)S(1)} %get-tuple-element.121), channel_id=1, source_target_pairs={{0,8},{8,0},{16,24},{24,16},{1,9},{9,1},{17,25},{25,17},{2,10},{10... | collective-permute-start | bytes 1179656 | tf_op jit(solution)/shard_map/ppermute | solution.py:23
  460.1 27.4 %collective-permute-start.38 = (bf16[1152,768]{1,0:T(8,128)(2,1)}, bf16[1152,768]{1,0:T(8,128)(2,1)}, u32[]{:S(2)}, u32[]{:S(2)}) collective-permute-start(bf16[1152,768]{1,0:T(8,128)(2,1)} %convolution_convert_fusion.8), channel_id=1, source_target_pairs={{0,1},{1,0},{2,3},{3,2},{4,5},{5,4},{6,7},{7,6},{8,9},{9,8},{10,11... | collective-permute-start | bytes 5308424 | tf_op jit(solution)/shard_map/ppermute | solution.py:23
  461.0 20.6 %collective-permute-start.39 = (bf16[256,1536]{1,0:T(8,128)(2,1)S(1)}, bf16[256,1536]{1,0:T(8,128)(2,1)S(1)}, u32[]{:S(2)}, u32[]{:S(2)}) collective-permute-start(bf16[256,1536]{1,0:T(8,128)(2,1)S(1)} %slice.497.refs_0_), channel_id=1, source_target_pairs={{0,8},{8,0},{16,24},{24,16},{1,9},{9,1},{17,25},{25,17},{2,10},{10... | collective-permute-start | bytes 2359304 | tf_op jit(solution)/shard_map/ppermute | solution.py:23
  501.8 172.1 %reduce-scatter.8.cloned.1.call-start = ((), (), s32[]{:S(2)}) async-start(), calls=%async_computation.11 | async-start | bytes 4423680 | tf_op jit(solution)/shard_map/reduce_scatter | solution.py:102
  580.5 184.5 %reduce-scatter.10.cloned.1.call-start = ((), (), s32[]{:S(2)}) async-start(), calls=%async_computation.12 | async-start | bytes 6635520 | tf_op jit(solution)/shard_map/reduce_scatter | solution.py:102
  600.5 289.6 %reduce-scatter.12.cloned.1.call-start = ((), (), s32[]{:S(2)}) async-start(), calls=%async_computation.13 | async-start | bytes 6635520 | tf_op jit(solution)/shard_map/reduce_scatter | solution.py:102
  610.0 30.5 %collective-permute-start.51 = (bf16[1152,2304]{1,0:T(8,128)(2,1)S(1)}, bf16[1152,2304]{1,0:T(8,128)(2,1)S(1)}, u32[]{:S(2)}, u32[]{:S(2)}) collective-permute-start(bf16[1152,2304]{1,0:T(8,128)(2,1)S(1)} %convolution_convert_fusion), channel_id=1, source_target_pairs={{0,1},{1,0},{2,3},{3,2},{4,5},{5,4},{6,7},{7,6},{8,9},{9,8},{10,11... | collective-permute-start | bytes 15925256 | tf_op jit(solution)/shard_map/ppermute | solution.py:23
  614.2 20.5 %collective-permute-start.45 = (bf16[256,1024]{1,0:T(8,128)(2,1)S(1)}, bf16[256,1024]{1,0:T(8,128)(2,1)S(1)}, u32[]{:S(2)}, u32[]{:S(2)}) collective-permute-start(bf16[256,1024]{1,0:T(8,128)(2,1)S(1)} %get-tuple-element.115), channel_id=1, source_target_pairs={{0,16},{8,24},{16,0},{24,8},{1,17},{9,25},{17,1},{25,9},{2,18},{10... | collective-permute-start | bytes 1572872 | tf_op jit(solution)/shard_map/ppermute | solution.py:23
  616.7 21.8 %collective-permute-start.47 = (bf16[256,1280]{1,0:T(8,128)(2,1)S(1)}, bf16[256,1280]{1,0:T(8,128)(2,1)S(1)}, u32[]{:S(2)}, u32[]{:S(2)}) collective-permute-start(bf16[256,1280]{1,0:T(8,128)(2,1)S(1)} %get-tuple-element.116), channel_id=1, source_target_pairs={{0,8},{8,0},{16,24},{24,16},{1,9},{9,1},{17,25},{25,17},{2,10},{10... | collective-permute-start | bytes 1966088 | tf_op jit(solution)/shard_map/ppermute | solution.py:23
  623.5 28.9 %collective-permute-start.44 = (bf16[256,1024]{1,0:T(8,128)(2,1)}, bf16[256,1024]{1,0:T(8,128)(2,1)}, u32[]{:S(2)}, u32[]{:S(2)}) collective-permute-start(bf16[256,1024]{1,0:T(8,128)(2,1)} %get-tuple-element.114), channel_id=1, source_target_pairs={{0,16},{8,24},{16,0},{24,8},{1,17},{9,25},{17,1},{25,9},{2,18},{10... | collective-permute-start | bytes 1572872 | tf_op jit(solution)/shard_map/ppermute | solution.py:23
  625.2 45.5 %collective-permute-start.49 = (bf16[256,1280]{1,0:T(8,128)(2,1)S(1)}, bf16[256,1280]{1,0:T(8,128)(2,1)S(1)}, u32[]{:S(2)}, u32[]{:S(2)}) collective-permute-start(bf16[256,1280]{1,0:T(8,128)(2,1)S(1)} %get-tuple-element.117), channel_id=1, source_target_pairs={{0,8},{8,0},{16,24},{24,16},{1,9},{9,1},{17,25},{25,17},{2,10},{10... | collective-permute-start | bytes 1966088 | tf_op jit(solution)/shard_map/ppermute | solution.py:23
  634.7 39.2 %collective-permute-start.55 = (bf16[288,512]{1,0:T(8,128)(2,1)}, bf16[288,512]{1,0:T(8,128)(2,1)}, u32[]{:S(2)}, u32[]{:S(2)}) collective-permute-start(bf16[288,512]{1,0:T(8,128)(2,1)} %slice.501), channel_id=1, source_target_pairs={{0,8},{8,0},{16,24},{24,16},{1,9},{9,1},{17,25},{25,17},{2,10},{10... | collective-permute-start | bytes 884744 | tf_op jit(solution)/shard_map/ppermute | solution.py:23
  638.6 30.6 %collective-permute-start.46 = (bf16[256,1024]{1,0:T(8,128)(2,1)}, bf16[256,1024]{1,0:T(8,128)(2,1)}, u32[]{:S(2)}, u32[]{:S(2)}) collective-permute-start(bf16[256,1024]{1,0:T(8,128)(2,1)} %add_convert_fusion.7), channel_id=1, source_target_pairs={{0,8},{8,0},{16,24},{24,16},{1,9},{9,1},{17,25},{25,17},{2,10},{10... | collective-permute-start | bytes 1572872 | tf_op jit(solution)/shard_map/ppermute | solution.py:23
  640.5 30.3 %collective-permute-start.48 = (bf16[256,1280]{1,0:T(8,128)(2,1)S(1)}, bf16[256,1280]{1,0:T(8,128)(2,1)}, u32[]{:S(2)}, u32[]{:S(2)}) collective-permute-start(bf16[256,1280]{1,0:T(8,128)(2,1)S(1)} %add_convert_fusion.1), channel_id=1, source_target_pairs={{0,16},{8,24},{16,0},{24,8},{1,17},{9,25},{17,1},{25,9},{2,18},{10... | collective-permute-start | bytes 1966088 | tf_op jit(solution)/shard_map/ppermute | solution.py:23
  652.4 288.4 %reduce-scatter.14.cloned.1.call-start = ((), (), s32[]{:S(2)}) async-start(), calls=%async_computation.14 | async-start | bytes 8626176 | tf_op jit(solution)/shard_map/reduce_scatter | solution.py:829
  652.4 21.5 %collective-permute-start.54 = (bf16[288,256]{1,0:T(8,128)(2,1)}, bf16[288,256]{1,0:T(8,128)(2,1)}, u32[]{:S(2)}, u32[]{:S(2)}) collective-permute-start(bf16[288,256]{1,0:T(8,128)(2,1)} %slice.500), channel_id=1, source_target_pairs={{0,16},{8,24},{16,0},{24,8},{1,17},{9,25},{17,1},{25,9},{2,18},{10... | collective-permute-start | bytes 442376 | tf_op jit(solution)/shard_map/ppermute | solution.py:23
  673.9 20.8 %collective-permute-start.57 = (bf16[288,1536]{1,0:T(8,128)(2,1)}, bf16[288,1536]{1,0:T(8,128)(2,1)S(1)}, u32[]{:S(2)}, u32[]{:S(2)}) collective-permute-start(bf16[288,1536]{1,0:T(8,128)(2,1)} %reduce-scatter.8.cloned.1.call-done), channel_id=1, source_target_pairs={{0,16},{8,24},{16,0},{24,8},{1,17},{9,25},{17,1},{25,9},{2,18},{10... | collective-permute-start | bytes 2654216 | tf_op jit(solution)/shard_map/ppermute | solution.py:23
  675.0 20.6 %collective-permute-start.56 = (bf16[288,1536]{1,0:T(8,128)(2,1)}, bf16[288,1536]{1,0:T(8,128)(2,1)}, u32[]{:S(2)}, u32[]{:S(2)}) collective-permute-start(bf16[288,1536]{1,0:T(8,128)(2,1)} %reduce-scatter.8.cloned.1.call-done), channel_id=1, source_target_pairs={{0,8},{8,0},{16,24},{24,16},{1,9},{9,1},{17,25},{25,17},{2,10},{10... | collective-permute-start | bytes 2654216 | tf_op jit(solution)/shard_map/ppermute | solution.py:23
  721.0 23.2 %collective-permute-start.61 = (bf16[1024,256]{1,0:T(8,128)(2,1)}, bf16[1024,256]{1,0:T(8,128)(2,1)S(1)}, u32[]{:S(2)}, u32[]{:S(2)}) collective-permute-start(bf16[1024,256]{1,0:T(8,128)(2,1)} %get-tuple-element.72), channel_id=1, source_target_pairs={{0,16},{8,24},{16,0},{24,8},{1,17},{9,25},{17,1},{25,9},{2,18},{10... | collective-permute-start | bytes 1572872 | tf_op jit(solution)/shard_map/ppermute | solution.py:23
  721.8 34.8 %collective-permute-start.66 = (bf16[1024,256]{1,0:T(8,128)(2,1)}, bf16[1024,256]{1,0:T(8,128)(2,1)S(1)}, u32[]{:S(2)}, u32[]{:S(2)}) collective-permute-start(bf16[1024,256]{1,0:T(8,128)(2,1)} %get-tuple-element.78), channel_id=1, source_target_pairs={{0,8},{8,0},{16,24},{24,16},{1,9},{9,1},{17,25},{25,17},{2,10},{10... | collective-permute-start | bytes 1572872 | tf_op jit(solution)/shard_map/ppermute | solution.py:23
  734.3 22.1 %collective-permute-start.63 = (bf16[1024,256]{1,0:T(8,128)(2,1)S(1)}, bf16[1024,256]{1,0:T(8,128)(2,1)S(1)}, u32[]{:S(2)}, u32[]{:S(2)}) collective-permute-start(bf16[1024,256]{1,0:T(8,128)(2,1)S(1)} %add_convert_fusion.6), channel_id=1, source_target_pairs={{0,8},{8,0},{16,24},{24,16},{1,9},{9,1},{17,25},{25,17},{2,10},{10... | collective-permute-start | bytes 1572872 | tf_op jit(solution)/shard_map/ppermute | solution.py:23
  736.2 20.5 %collective-permute-start.65 = (bf16[1024,256]{1,0:T(8,128)(2,1)S(1)}, bf16[1024,256]{1,0:T(8,128)(2,1)S(1)}, u32[]{:S(2)}, u32[]{:S(2)}) collective-permute-start(bf16[1024,256]{1,0:T(8,128)(2,1)S(1)} %add_convert_fusion.4), channel_id=1, source_target_pairs={{0,16},{8,24},{16,0},{24,8},{1,17},{9,25},{17,1},{25,9},{2,18},{10... | collective-permute-start | bytes 1572872 | tf_op jit(solution)/shard_map/ppermute | solution.py:23
  738.6 25.7 %collective-permute-start.68 = (bf16[288,768]{1,0:T(8,128)(2,1)S(1)}, bf16[288,768]{1,0:T(8,128)(2,1)S(1)}, u32[]{:S(2)}, u32[]{:S(2)}) collective-permute-start(bf16[288,768]{1,0:T(8,128)(2,1)S(1)} %slice.507), channel_id=1, source_target_pairs={{0,8},{8,0},{16,24},{24,16},{1,9},{9,1},{17,25},{25,17},{2,10},{10... | collective-permute-start | bytes 1327112 | tf_op jit(solution)/shard_map/ppermute | solution.py:23
  744.2 20.8 %collective-permute-start.67 = (bf16[288,768]{1,0:T(8,128)(2,1)S(1)}, bf16[288,768]{1,0:T(8,128)(2,1)}, u32[]{:S(2)}, u32[]{:S(2)}) collective-permute-start(bf16[288,768]{1,0:T(8,128)(2,1)S(1)} %slice.506), channel_id=1, source_target_pairs={{0,16},{8,24},{16,0},{24,8},{1,17},{9,25},{17,1},{25,9},{2,18},{10... | collective-permute-start | bytes 1327112 | tf_op jit(solution)/shard_map/ppermute | solution.py:23
  765.1 32.2 %collective-permute-start.70 = (bf16[288,2304]{1,0:T(8,128)(2,1)}, bf16[288,2304]{1,0:T(8,128)(2,1)S(1)}, u32[]{:S(2)}, u32[]{:S(2)}) collective-permute-start(bf16[288,2304]{1,0:T(8,128)(2,1)} %reduce-scatter.10.cloned.1.call-done.refs_0_), channel_id=1, source_target_pairs={{0,16},{8,24},{16,0},{24,8},{1,17},{9,25},{17,1},{25,9},{2,18},{10... | collective-permute-start | bytes 3981320 | tf_op jit(solution)/shard_map/ppermute | solution.py:23
  766.6 30.6 %collective-permute-start.69 = (bf16[288,2304]{1,0:T(8,128)(2,1)}, bf16[288,2304]{1,0:T(8,128)(2,1)}, u32[]{:S(2)}, u32[]{:S(2)}) collective-permute-start(bf16[288,2304]{1,0:T(8,128)(2,1)} %reduce-scatter.10.cloned.1.call-done.refs_0_), channel_id=1, source_target_pairs={{0,8},{8,0},{16,24},{24,16},{1,9},{9,1},{17,25},{25,17},{2,10},{10... | collective-permute-start | bytes 3981320 | tf_op jit(solution)/shard_map/ppermute | solution.py:23
  835.3 30.1 %collective-permute-start.95 = (bf16[288,1280]{1,0:T(8,128)(2,1)S(1)}, bf16[288,1280]{1,0:T(8,128)(2,1)S(1)}, u32[]{:S(2)}, u32[]{:S(2)}) collective-permute-start(bf16[288,1280]{1,0:T(8,128)(2,1)S(1)} %slice.535), channel_id=1, source_target_pairs={{0,8},{8,0},{16,24},{24,16},{1,9},{9,1},{17,25},{25,17},{2,10},{10... | collective-permute-start | bytes 2211848 | tf_op jit(solution)/shard_map/ppermute | solution.py:23
  838.4 30.8 %collective-permute-start.71 = (bf16[256,1024]{1,0:T(8,128)(2,1)S(1)}, bf16[256,1024]{1,0:T(8,128)(2,1)S(1)}, u32[]{:S(2)}, u32[]{:S(2)}) collective-permute-start(bf16[256,1024]{1,0:T(8,128)(2,1)S(1)} %get-tuple-element.110), channel_id=1, source_target_pairs={{0,16},{8,24},{16,0},{24,8},{1,17},{9,25},{17,1},{25,9},{2,18},{10... | collective-permute-start | bytes 1572872 | tf_op jit(solution)/shard_map/ppermute | solution.py:23
  845.2 43.0 %collective-permute-start.76 = (bf16[256,1280]{1,0:T(8,128)(2,1)S(1)}, bf16[256,1280]{1,0:T(8,128)(2,1)S(1)}, u32[]{:S(2)}, u32[]{:S(2)}) collective-permute-start(bf16[256,1280]{1,0:T(8,128)(2,1)S(1)} %get-tuple-element.113), channel_id=1, source_target_pairs={{0,8},{8,0},{16,24},{24,16},{1,9},{9,1},{17,25},{25,17},{2,10},{10... | collective-permute-start | bytes 1966088 | tf_op jit(solution)/shard_map/ppermute | solution.py:23
  849.6 38.4 %collective-permute-start.73 = (bf16[256,1024]{1,0:T(8,128)(2,1)S(1)}, bf16[256,1024]{1,0:T(8,128)(2,1)S(1)}, u32[]{:S(2)}, u32[]{:S(2)}) collective-permute-start(bf16[256,1024]{1,0:T(8,128)(2,1)S(1)} %add_convert_fusion.2), channel_id=1, source_target_pairs={{0,8},{8,0},{16,24},{24,16},{1,9},{9,1},{17,25},{25,17},{2,10},{10... | collective-permute-start | bytes 1572872 | tf_op jit(solution)/shard_map/ppermute | solution.py:23
  857.8 30.4 %collective-permute-start.75 = (bf16[256,1280]{1,0:T(8,128)(2,1)S(1)}, bf16[256,1280]{1,0:T(8,128)(2,1)S(1)}, u32[]{:S(2)}, u32[]{:S(2)}) collective-permute-start(bf16[256,1280]{1,0:T(8,128)(2,1)S(1)} %add_convert_fusion), channel_id=1, source_target_pairs={{0,16},{8,24},{16,0},{24,8},{1,17},{9,25},{17,1},{25,9},{2,18},{10... | collective-permute-start | bytes 1966088 | tf_op jit(solution)/shard_map/ppermute | solution.py:23
  903.1 28.6 %collective-permute-start.97 = (bf16[288,2304]{1,0:T(8,128)(2,1)}, bf16[288,2304]{1,0:T(8,128)(2,1)S(1)}, u32[]{:S(2)}, u32[]{:S(2)}) collective-permute-start(bf16[288,2304]{1,0:T(8,128)(2,1)} %reduce-scatter.12.cloned.1.call-done.refs_0_), channel_id=1, source_target_pairs={{0,16},{8,24},{16,0},{24,8},{1,17},{9,25},{17,1},{25,9},{2,18},{10... | collective-permute-start | bytes 3981320 | tf_op jit(solution)/shard_map/ppermute | solution.py:23
  903.6 29.4 %collective-permute-start.96 = (bf16[288,2304]{1,0:T(8,128)(2,1)}, bf16[288,2304]{1,0:T(8,128)(2,1)}, u32[]{:S(2)}, u32[]{:S(2)}) collective-permute-start(bf16[288,2304]{1,0:T(8,128)(2,1)} %reduce-scatter.12.cloned.1.call-done.refs_0_), channel_id=1, source_target_pairs={{0,8},{8,0},{16,24},{24,16},{1,9},{9,1},{17,25},{25,17},{2,10},{10... | collective-permute-start | bytes 3981320 | tf_op jit(solution)/shard_map/ppermute | solution.py:23
  935.0 28.2 %collective-permute-start.98 = (bf16[288,1024]{1,0:T(8,128)(2,1)}, bf16[288,1024]{1,0:T(8,128)(2,1)S(1)}, u32[]{:S(2)}, u32[]{:S(2)}) collective-permute-start(bf16[288,1024]{1,0:T(8,128)(2,1)} %slice.536), channel_id=1, source_target_pairs={{0,16},{8,24},{16,0},{24,8},{1,17},{9,25},{17,1},{25,9},{2,18},{10... | collective-permute-start | bytes 1769480 | tf_op jit(solution)/shard_map/ppermute | solution.py:23
  (173 other events, 1686.1 us)
Sparse Core Ops, SparseCore 0:
  10.5 54.8 all-gather.5
  67.6 32.5 all-gather.7
  102.4 186.6 all-gather.9
  291.1 69.3 all-gather.11
  362.1 40.1 all-gather.13
  502.0 36.0 reduce-scatter.5
  580.7 63.9 reduce-scatter.7
  647.7 95.0 reduce-scatter.9
  745.7 95.3 reduce-scatter.11
  843.9 84.0 reduce-scatter.13

commit v3 on v2

--- a/solution.py
+++ b/solution.py
@@ -838,13 +838,12 @@
     input_grad = (grad_middle + grad_rows).astype(low)[None]
 
     gain_terms = jnp.stack([grad_gain_a, grad_gain_b, grad_gain_c, grad_gain_d])
-    for bit in range(n_ctx.bit_length() - 1):
-        gain_terms = gain_terms + swap(gain_terms, "ctx", 1 << bit)
     gain_terms = jnp.transpose(gain_terms.reshape(4, n_fsdp, width // n_fsdp), (1, 0, 2))
     gain_terms = jnp.take(gain_terms, jnp.arange(n_fsdp) ^ f, axis=0)
     gain_sums = gain_terms[0]
     for k in range(1, n_fsdp):
         gain_sums = gain_sums + swap(gain_terms[k], "fsdp", k)
+    gain_sums = sum(in_order(exchange([gain_sums] * n_ctx)))
 
     if share == 1:
         qkv_pieces = gather_pieces(qkv_sum)

time: 1000 us -> 1000 us (level)
    ppermute x100 -> x101, waiting for transfers between devices: 329 us -> 334 us  [swap(): return lax.ppermute(shard, axis, [(i, i ^ mask) for i in range(size)])]
    unnamed x247 -> x245, local copies, waits for them, and re-layouts: 54.2 us -> 50.1 us
    ppermute x100 -> x101, starting transfers between devices: 110 us -> 111 us  [swap(): return lax.ppermute(shard, axis, [(i, i ^ mask) for i in range(size)])]
  transfers between devices with their start and end apart: 110 -> 111, of which waited for: 53 -> 56; matrix products, arithmetic and copies ran while one was open for 25% -> 24% of each run, Pallas kernels for 14% -> 14%
where the time goes in v3:
time: 1000 us; the launch traced here: 995 us
  waiting for transfers between devices  417 us (42%)
  Pallas kernels  144 us (14%)
  matrix products  128 us (13%)
  starting transfers between devices  112 us (11%)
  local copies, waits for them, and re-layouts  104 us (10%)
  other arithmetic  73.9 us (7%)
  between operations  16.4 us (2%)
    ppermute x101, waiting for transfers between devices, swap(): return lax.ppermute(shard, axis, [(i, i ^ mask) for i in range(size)])  334 us
    ppermute x101, starting transfers between devices, swap(): return lax.ppermute(shard, axis, [(i, i ^ mask) for i in range(size)])  111 us
    all_gather x5, waiting for transfers between devices, gathered(): return lax.all_gather(shard, 'fsdp', axis=0, tiled=True)  82.6 us
    dot_general x10, matrix products, contract_first(): lax.dot_general(left, right, (((0,), (0,)), ((), ())), preferred_element_...  81.3 us
    unnamed x245, local copies, waits for them, and re-layouts  50.1 us
    pallas_call x1, Pallas kernels, units_forward(): pl.pallas_call(units_kernel, out_shape=[out] * 3, grid=(steps,), in_specs...  34.1 us
    pallas_call x1, Pallas kernels, product_last(): pl.pallas_call(product_kernel, out_shape=jax.ShapeDtypeStruct((rows, cols...  30.4 us
    dot_general x6, matrix products, dot(): return jnp.dot(left, right, preferred_element_type=wide)  28.9 us
  transfers between devices with their start and end apart: 111, of which 56 were waited for; matrix products, arithmetic and copies ran while one was open for 24% of the time, Pallas kernels for 14%

profile of v3, /device:TPU:0, one launch (start us, length us, event | category | flops | bytes accessed | tf_op | source)
XLA Modules:
  0.0 995.1 jit_solution(10045434303162233353)
XLA Ops:
  44.0 24.8 %collective-permute-done = s32[256]{0:T(256)S(1)} collective-permute-done((s32[256]{0:T(256)S(1)}, s32[256]{0:T(256)S(1)}, u32[]{:S(2)}, u32[]{:S(2)}) %collective-permute-start) | collective-permute-done | bytes 1056 | tf_op jit(solution)/shard_map/ppermute | solution.py:23
  76.7 7.1 collective-permute-done.12.refs_3_
  87.4 8.4 fusion.125
  126.2 19.0 %collective-permute-done.15.refs_2_ = bf16[1024,512]{1,0:T(8,128)(2,1)S(1)} collective-permute-done((bf16[1024,512]{1,0:T(8,128)(2,1)S(1)}, bf16[1024,512]{1,0:T(8,128)(2,1)S(1)}, u32[]{:S(2)}, u32[]{:S(2)}) %collective-permute-start.15) | collective-permute-done | bytes 1048608 | tf_op jit(solution)/shard_map/ppermute | solution.py:23
  149.1 8.5 collective-permute-done.17.refs_4_
  160.2 5.7 convolution_convert_fusion.12
  170.5 7.2 collective-permute-done.20
  196.0 23.7 %collective-permute-done.22.refs_2_ = bf16[256,2304]{1,0:T(8,128)(2,1)S(1)} collective-permute-done((bf16[256,2304]{1,0:T(8,128)(2,1)S(1)}, bf16[256,2304]{1,0:T(8,128)(2,1)S(1)}, u32[]{:S(2)}, u32[]{:S(2)}) %collective-permute-start.22) | collective-permute-done | bytes 1179680 | tf_op jit(solution)/shard_map/ppermute | solution.py:23
  224.7 7.9 collective-permute-done.23.refs_3_
  242.0 47.1 %all-gather.10.cloned.1.call-done.gate_ref.up_ref.refs_2_ = bf16[2304,4608]{1,0:T(8,128)(2,1)} async-done(((bf16[288,4608]{1,0:T(8,128)(2,1)}), bf16[2304,4608]{1,0:T(8,128)(2,1)}) %all-gather.10.cloned.1.call-update) | async-done | bytes 21233680 | tf_op jit(solution)/shard_map/all_gather | solution.py:620
  290.9 34.1 %shard_map.242 = (bf16[1024,2304]{1,0:T(8,128)(2,1)S(1)}, bf16[1024,2304]{1,0:T(8,128)(2,1)}, bf16[1024,2304]{1,0:T(8,128)(2,1)}) custom-call(bf16[1024,2304]{1,0:T(8,128)(2,1)} %bitcast.197, bf16[2304,4608]{1,0:T(8,128)(2,1)} %all-gather.10.cloned.1.call-done.gate_ref.up_ref.refs_2_, bf16[2304,4608]{1,0:T(8,128)(2,1)} %all-gather.10.cloned.1.call-done.gate_ref.up_ref.refs_2_), custom_call_target="tpu_custom_call" | custom-call | flops 21743271936 | bytes 40108032 | tf_op jit(solution)/shard_map/pallas_call | solution.py:432
  327.1 33.5 %all-gather.12.cloned.1.call-done.refs_0_ = bf16[2304,1536]{1,0:T(8,128)(2,1)} async-done(((bf16[288,1536]{1,0:T(8,128)(2,1)}), bf16[2304,1536]{1,0:T(8,128)(2,1)}) %all-gather.12.cloned.1.call-update) | async-done | bytes 7077904 | tf_op jit(solution)/shard_map/all_gather | solution.py:620
  366.3 7.7 convolution_convert_fusion.7
  377.7 8.4 collective-permute-done.26
  388.3 5.5 collective-permute-done.25
  416.5 7.3 collective-permute-done.31
  423.7 8.8 collective-permute-done.33
  439.7 7.8 collective-permute-done.35.refs_2_
  454.6 5.5 convolution_convert_fusion.8
  462.5 17.7 %collective-permute-done.40.refs_2_ = bf16[256,1536]{1,0:T(8,128)(2,1)S(1)} collective-permute-done((bf16[256,1536]{1,0:T(8,128)(2,1)S(1)}, bf16[256,1536]{1,0:T(8,128)(2,1)S(1)}, u32[]{:S(2)}, u32[]{:S(2)}) %collective-permute-start.40) | collective-permute-done | bytes 786464 | tf_op jit(solution)/shard_map/ppermute | solution.py:23
  493.5 8.2 convolution_convert_fusion.2
  501.9 6.5 convolution_convert_fusion.3.first_ref
  513.6 23.5 %shard_map.250 = (bf16[1024,2304]{1,0:T(8,128)(2,1)}, bf16[1024,2304]{1,0:T(8,128)(2,1)}) custom-call(bf16[1024,768]{1,0:T(8,128)(2,1)} %bitcast.207, bf16[1024,1536]{1,0:T(8,128)(2,1)} %bitcast.204, bf16[2304,768]{1,0:T(8,128)(2,1)} %copy-done.13, bf16[2304,1536]{1,0:T(8,128)(2,1)} %copy-done.3, bf16[1024,2304]{1,0:T(8,128)(2,1)} %get-tuple-element.58.refs_4_, ...), custom_call_target="tpu_custom_call" | custom-call | flops 10871635968 | bytes 34209792 | tf_op jit(solution)/shard_map/pallas_call | solution.py:471
  537.1 30.4 %shard_map.251 = bf16[1024,2304]{1,0:T(8,128)(2,1)S(1)} custom-call(bf16[1024,2304]{1,0:T(8,128)(2,1)} %get-tuple-element.64.refs_0_, bf16[1024,2304]{1,0:T(8,128)(2,1)} %get-tuple-element.65.refs_1_, bf16[2304,4608]{1,0:T(8,128)(2,1)} %all-gather.10.cloned.1.call-done.gate_ref.up_ref.refs_2_), custom_call_target="tpu_custom_call" | custom-call | flops 21743271936 | bytes 35389440 | tf_op jit(solution)/shard_map/pallas_call | solution.py:506
  569.7 10.4 %convolution_convert_fusion.1 = bf16[1152,2304]{1,0:T(8,128)(2,1)} fusion(bf16[1024,2304]{1,0:T(8,128)(2,1)} %get-tuple-element.64.refs_0_, bf16[1024,2304]{1,0:T(8,128)(2,1)} %copy-done.8, s32[]{:T(128)S(6)} %select_n.294), kind=kOutput, calls=%fused_computation.9 | convolution fusion | flops 5438472192 | bytes 12386308 | tf_op jit(solution)/shard_map/dot_general | solution.py:578
  580.6 8.6 collective-permute-done.50
  589.3 11.2 %fusion = bf16[1152,2304]{1,0:T(8,128)(2,1)} fusion(bf16[1024,2304]{1,0:T(8,128)(2,1)} %get-tuple-element.64.refs_0_, bf16[1152,2304]{1,0:T(8,128)(2,1)} %collective-permute-done.50, bf16[1024,2304]{1,0:T(8,128)(2,1)} %copy-done.8, s32[]{:T(128)S(6)} %select_n.293), kind=kOutput, calls=%fused_computation.6 | convolution fusion | flops 5443780608 | bytes 17694724 | tf_op jit(solution)/shard_map/dot_general | solution.py:578
  600.6 9.5 convolution_convert_fusion
  618.0 5.5 collective-permute-done.53
  626.6 8.1 collective-permute-done.45
  641.7 10.6 %fusion.1 = bf16[1152,2304]{1,0:T(8,128)(2,1)} fusion(bf16[1024,2304]{1,0:T(8,128)(2,1)} %get-tuple-element.65.refs_1_, bf16[1152,2304]{1,0:T(8,128)(2,1)S(1)} %collective-permute-done.51, bf16[1024,2304]{1,0:T(8,128)(2,1)} %copy-done.8, s32[]{:T(128)S(6)} %select_n.293), kind=kOutput, calls=%fused_computation.7 | convolution fusion | flops 5443780608 | bytes 17694724 | tf_op jit(solution)/shard_map/dot_general | solution.py:578
  653.5 15.7 %collective-permute-done.46 = bf16[256,1024]{1,0:T(8,128)(2,1)} collective-permute-done((bf16[256,1024]{1,0:T(8,128)(2,1)}, bf16[256,1024]{1,0:T(8,128)(2,1)}, u32[]{:S(2)}, u32[]{:S(2)}) %collective-permute-start.46) | collective-permute-done | bytes 524320 | tf_op jit(solution)/shard_map/ppermute | solution.py:23
  684.5 10.3 %collective-permute-done.57 = bf16[288,1536]{1,0:T(8,128)(2,1)S(1)} collective-permute-done((bf16[288,1536]{1,0:T(8,128)(2,1)}, bf16[288,1536]{1,0:T(8,128)(2,1)S(1)}, u32[]{:S(2)}, u32[]{:S(2)}) %collective-permute-start.57) | collective-permute-done | bytes 884768 | tf_op jit(solution)/shard_map/ppermute | solution.py:23
  701.1 7.4 collective-permute-done.60
  723.4 9.8 collective-permute-done.62
  745.2 11.3 %collective-permute-done.63 = bf16[1024,256]{1,0:T(8,128)(2,1)S(1)} collective-permute-done((bf16[1024,256]{1,0:T(8,128)(2,1)S(1)}, bf16[1024,256]{1,0:T(8,128)(2,1)S(1)}, u32[]{:S(2)}, u32[]{:S(2)}) %collective-permute-start.63) | collective-permute-done | bytes 524320 | tf_op jit(solution)/shard_map/ppermute | solution.py:23
  757.0 7.4 collective-permute-done.68
  767.1 6.6 convolution_convert_fusion.10
  784.9 12.5 %shard_map.253 = bf16[1024,1024]{1,0:T(8,128)(2,1)} custom-call(bf16[1024,512]{1,0:T(8,128)(2,1)S(1)} %pad_maximum_fusion.12.grad_ref, bf16[1024,512]{1,0:T(8,128)(2,1)S(1)} %bitcast.208, bf16[1024,256]{1,0:T(8,128)(2,1)S(1)} %copy-done.31, bf16[1024,256]{1,0:T(8,128)(2,1)S(1)} %copy-done.29, s32[1024,1]{1,0:T(8,128)S(1)} %copy-done.30, ...), custom_call_target="tpu_custom_call" | custom-call | flops 10737418240 | bytes 4194304 | tf_op jit(solution)/shard_map/pallas_call | solution.py:354
  797.5 8.6 convolution_convert_fusion.4
  806.0 7.1 pad_maximum_fusion
  823.0 7.7 convolution_convert_fusion.5
  851.0 7.4 collective-permute-done.95.refs_3_
  859.7 6.1 collective-permute-done.96.refs_4_
  868.9 6.5 shard_map.257
  875.4 12.8 %collective-permute-done.73 = bf16[256,1024]{1,0:T(8,128)(2,1)S(1)} collective-permute-done((bf16[256,1024]{1,0:T(8,128)(2,1)S(1)}, bf16[256,1024]{1,0:T(8,128)(2,1)S(1)}, u32[]{:S(2)}, u32[]{:S(2)}) %collective-permute-start.73) | collective-permute-done | bytes 524320 | tf_op jit(solution)/shard_map/ppermute | solution.py:23
  915.1 14.5 %collective-permute-done.86 = f32[4,288]{1,0:T(4,128)S(1)} collective-permute-done((f32[4,288]{1,0:T(4,128)S(1)}, f32[4,288]{1,0:T(4,128)S(1)}, u32[]{:S(2)}, u32[]{:S(2)}) %collective-permute-start.86) | collective-permute-done | bytes 4640 | tf_op jit(solution)/shard_map/ppermute | solution.py:23
  941.6 9.9 collective-permute-done.100.refs_4_
  (627 shorter events, 388.7 us)
Async XLA Ops:
  7.2 80.2 %all-gather.6.cloned.1.call-start = ((), (), s32[]{:S(2)}) async-start(), calls=%async_computation.5 | async-start | bytes 5308416 | tf_op jit(solution)/shard_map/all_gather | solution.py:620
  10.4 149.8 %all-gather.8.cloned.1.call-start = ((), (), s32[]{:S(2)}) async-start(), calls=%async_computation.6 | async-start | bytes 2949120 | tf_op jit(solution)/shard_map/all_gather | solution.py:620
  12.4 276.7 %all-gather.10.cloned.1.call-start = ((), (), s32[]{:S(2)}) async-start(), calls=%async_computation.7 | async-start | bytes 23887872 | tf_op jit(solution)/shard_map/all_gather | solution.py:620
  20.7 339.9 %all-gather.12.cloned.1.call-start = ((), (), s32[]{:S(2)}) async-start(), calls=%async_computation.8 | async-start | bytes 7962624 | tf_op jit(solution)/shard_map/all_gather | solution.py:620
  39.9 29.5 %collective-permute-start.11 = (bf16[256,2304]{1,0:T(8,128)(2,1)S(1)}, bf16[256,2304]{1,0:T(8,128)(2,1)S(1)}, u32[]{:S(2)}, u32[]{:S(2)}) collective-permute-start(bf16[256,2304]{1,0:T(8,128)(2,1)S(1)} %fusion.22.refs_0_), channel_id=1, source_target_pairs={{0,16},{8,24},{16,0},{24,8},{1,17},{9,25},{17,1},{25,9},{2,18},{10... | collective-permute-start | bytes 3538952 | tf_op jit(solution)/shard_map/ppermute | solution.py:23
  41.5 30.9 %collective-permute-start.10 = (bf16[256,2304]{1,0:T(8,128)(2,1)S(1)}, bf16[256,2304]{1,0:T(8,128)(2,1)S(1)}, u32[]{:S(2)}, u32[]{:S(2)}) collective-permute-start(bf16[256,2304]{1,0:T(8,128)(2,1)S(1)} %fusion.22.refs_0_), channel_id=1, source_target_pairs={{0,8},{8,0},{16,24},{24,16},{1,9},{9,1},{17,25},{25,17},{2,10},{10... | collective-permute-start | bytes 3538952 | tf_op jit(solution)/shard_map/ppermute | solution.py:23
  43.0 25.9 %collective-permute-start = (s32[256]{0:T(256)S(1)}, s32[256]{0:T(256)S(1)}, u32[]{:S(2)}, u32[]{:S(2)}) collective-permute-start(s32[256]{0:T(256)S(1)} %bitcast.225), channel_id=1, source_target_pairs={{0,8},{8,0},{16,24},{24,16},{1,9},{9,1},{17,25},{25,17},{2,10},{10... | collective-permute-start | bytes 3080 | tf_op jit(solution)/shard_map/ppermute | solution.py:23
  43.6 27.5 %collective-permute-start.1 = (s32[256]{0:T(256)S(1)}, s32[256]{0:T(256)S(1)}, u32[]{:S(2)}, u32[]{:S(2)}) collective-permute-start(s32[256]{0:T(256)S(1)} %bitcast.226), channel_id=1, source_target_pairs={{0,16},{8,24},{16,0},{24,8},{1,17},{9,25},{17,1},{25,9},{2,18},{10... | collective-permute-start | bytes 3080 | tf_op jit(solution)/shard_map/ppermute | solution.py:23
  122.8 22.4 %collective-permute-start.15 = (bf16[1024,512]{1,0:T(8,128)(2,1)S(1)}, bf16[1024,512]{1,0:T(8,128)(2,1)S(1)}, u32[]{:S(2)}, u32[]{:S(2)}) collective-permute-start(bf16[1024,512]{1,0:T(8,128)(2,1)S(1)} %copy.56.refs_0_), channel_id=1, source_target_pairs={{0,16},{8,24},{16,0},{24,8},{1,17},{9,25},{17,1},{25,9},{2,18},{10... | collective-permute-start | bytes 3145736 | tf_op jit(solution)/shard_map/ppermute | solution.py:23
  124.7 23.6 %collective-permute-start.14 = (bf16[1024,512]{1,0:T(8,128)(2,1)S(1)}, bf16[1024,512]{1,0:T(8,128)(2,1)S(1)}, u32[]{:S(2)}, u32[]{:S(2)}) collective-permute-start(bf16[1024,512]{1,0:T(8,128)(2,1)S(1)} %copy.56.refs_0_), channel_id=1, source_target_pairs={{0,8},{8,0},{16,24},{24,16},{1,9},{9,1},{17,25},{25,17},{2,10},{10... | collective-permute-start | bytes 3145736 | tf_op jit(solution)/shard_map/ppermute | solution.py:23
  192.5 27.3 %collective-permute-start.22 = (bf16[256,2304]{1,0:T(8,128)(2,1)S(1)}, bf16[256,2304]{1,0:T(8,128)(2,1)S(1)}, u32[]{:S(2)}, u32[]{:S(2)}) collective-permute-start(bf16[256,2304]{1,0:T(8,128)(2,1)S(1)} %multiply_convert_fusion.1.refs_0_), channel_id=1, source_target_pairs={{0,16},{8,24},{16,0},{24,8},{1,17},{9,25},{17,1},{25,9},{2,18},{10... | collective-permute-start | bytes 3538952 | tf_op jit(solution)/shard_map/ppermute | solution.py:23
  193.5 27.1 %collective-permute-start.21 = (bf16[256,2304]{1,0:T(8,128)(2,1)S(1)}, bf16[256,2304]{1,0:T(8,128)(2,1)S(1)}, u32[]{:S(2)}, u32[]{:S(2)}) collective-permute-start(bf16[256,2304]{1,0:T(8,128)(2,1)S(1)} %multiply_convert_fusion.1.refs_0_), channel_id=1, source_target_pairs={{0,8},{8,0},{16,24},{24,16},{1,9},{9,1},{17,25},{25,17},{2,10},{10... | collective-permute-start | bytes 3538952 | tf_op jit(solution)/shard_map/ppermute | solution.py:23
  290.1 112.2 %all-gather.14.cloned.1.call-start = ((), (), s32[]{:S(2)}) async-start(), calls=%async_computation.9 | async-start | bytes 3981312 | tf_op jit(solution)/shard_map/all_gather | solution.py:620
  360.7 209.1 %reduce-scatter.6.cloned.1.call-start = ((), (), s32[]{:S(2)}) async-start(), calls=%async_computation.10 | async-start | bytes 2211840 | tf_op jit(solution)/shard_map/reduce_scatter | solution.py:102
  387.8 27.2 %collective-permute-start.30 = (bf16[256,768]{1,0:T(8,128)(2,1)S(1)}, bf16[256,768]{1,0:T(8,128)(2,1)}, u32[]{:S(2)}, u32[]{:S(2)}) collective-permute-start(bf16[256,768]{1,0:T(8,128)(2,1)S(1)} %get-tuple-element.121), channel_id=1, source_target_pairs={{0,8},{8,0},{16,24},{24,16},{1,9},{9,1},{17,25},{25,17},{2,10},{10... | collective-permute-start | bytes 1179656 | tf_op jit(solution)/shard_map/ppermute | solution.py:23
  460.1 27.4 %collective-permute-start.38 = (bf16[1152,768]{1,0:T(8,128)(2,1)}, bf16[1152,768]{1,0:T(8,128)(2,1)}, u32[]{:S(2)}, u32[]{:S(2)}) collective-permute-start(bf16[1152,768]{1,0:T(8,128)(2,1)} %convolution_convert_fusion.8), channel_id=1, source_target_pairs={{0,1},{1,0},{2,3},{3,2},{4,5},{5,4},{6,7},{7,6},{8,9},{9,8},{10,11... | collective-permute-start | bytes 5308424 | tf_op jit(solution)/shard_map/ppermute | solution.py:23
  461.0 20.6 %collective-permute-start.39 = (bf16[256,1536]{1,0:T(8,128)(2,1)S(1)}, bf16[256,1536]{1,0:T(8,128)(2,1)S(1)}, u32[]{:S(2)}, u32[]{:S(2)}) collective-permute-start(bf16[256,1536]{1,0:T(8,128)(2,1)S(1)} %slice.497.refs_0_), channel_id=1, source_target_pairs={{0,8},{8,0},{16,24},{24,16},{1,9},{9,1},{17,25},{25,17},{2,10},{10... | collective-permute-start | bytes 2359304 | tf_op jit(solution)/shard_map/ppermute | solution.py:23
  501.8 172.1 %reduce-scatter.8.cloned.1.call-start = ((), (), s32[]{:S(2)}) async-start(), calls=%async_computation.11 | async-start | bytes 4423680 | tf_op jit(solution)/shard_map/reduce_scatter | solution.py:102
  580.6 184.6 %reduce-scatter.10.cloned.1.call-start = ((), (), s32[]{:S(2)}) async-start(), calls=%async_computation.12 | async-start | bytes 6635520 | tf_op jit(solution)/shard_map/reduce_scatter | solution.py:102
  600.5 289.9 %reduce-scatter.12.cloned.1.call-start = ((), (), s32[]{:S(2)}) async-start(), calls=%async_computation.13 | async-start | bytes 6635520 | tf_op jit(solution)/shard_map/reduce_scatter | solution.py:102
  610.1 30.5 %collective-permute-start.51 = (bf16[1152,2304]{1,0:T(8,128)(2,1)S(1)}, bf16[1152,2304]{1,0:T(8,128)(2,1)S(1)}, u32[]{:S(2)}, u32[]{:S(2)}) collective-permute-start(bf16[1152,2304]{1,0:T(8,128)(2,1)S(1)} %convolution_convert_fusion), channel_id=1, source_target_pairs={{0,1},{1,0},{2,3},{3,2},{4,5},{5,4},{6,7},{7,6},{8,9},{9,8},{10,11... | collective-permute-start | bytes 15925256 | tf_op jit(solution)/shard_map/ppermute | solution.py:23
  614.2 20.5 %collective-permute-start.45 = (bf16[256,1024]{1,0:T(8,128)(2,1)S(1)}, bf16[256,1024]{1,0:T(8,128)(2,1)S(1)}, u32[]{:S(2)}, u32[]{:S(2)}) collective-permute-start(bf16[256,1024]{1,0:T(8,128)(2,1)S(1)} %get-tuple-element.115), channel_id=1, source_target_pairs={{0,16},{8,24},{16,0},{24,8},{1,17},{9,25},{17,1},{25,9},{2,18},{10... | collective-permute-start | bytes 1572872 | tf_op jit(solution)/shard_map/ppermute | solution.py:23
  616.7 21.9 %collective-permute-start.47 = (bf16[256,1280]{1,0:T(8,128)(2,1)S(1)}, bf16[256,1280]{1,0:T(8,128)(2,1)S(1)}, u32[]{:S(2)}, u32[]{:S(2)}) collective-permute-start(bf16[256,1280]{1,0:T(8,128)(2,1)S(1)} %get-tuple-element.116), channel_id=1, source_target_pairs={{0,8},{8,0},{16,24},{24,16},{1,9},{9,1},{17,25},{25,17},{2,10},{10... | collective-permute-start | bytes 1966088 | tf_op jit(solution)/shard_map/ppermute | solution.py:23
  623.5 28.9 %collective-permute-start.44 = (bf16[256,1024]{1,0:T(8,128)(2,1)}, bf16[256,1024]{1,0:T(8,128)(2,1)}, u32[]{:S(2)}, u32[]{:S(2)}) collective-permute-start(bf16[256,1024]{1,0:T(8,128)(2,1)} %get-tuple-element.114), channel_id=1, source_target_pairs={{0,16},{8,24},{16,0},{24,8},{1,17},{9,25},{17,1},{25,9},{2,18},{10... | collective-permute-start | bytes 1572872 | tf_op jit(solution)/shard_map/ppermute | solution.py:23
  625.3 45.5 %collective-permute-start.49 = (bf16[256,1280]{1,0:T(8,128)(2,1)S(1)}, bf16[256,1280]{1,0:T(8,128)(2,1)S(1)}, u32[]{:S(2)}, u32[]{:S(2)}) collective-permute-start(bf16[256,1280]{1,0:T(8,128)(2,1)S(1)} %get-tuple-element.117), channel_id=1, source_target_pairs={{0,8},{8,0},{16,24},{24,16},{1,9},{9,1},{17,25},{25,17},{2,10},{10... | collective-permute-start | bytes 1966088 | tf_op jit(solution)/shard_map/ppermute | solution.py:23
  634.7 39.2 %collective-permute-start.55 = (bf16[288,512]{1,0:T(8,128)(2,1)}, bf16[288,512]{1,0:T(8,128)(2,1)}, u32[]{:S(2)}, u32[]{:S(2)}) collective-permute-start(bf16[288,512]{1,0:T(8,128)(2,1)} %slice.501), channel_id=1, source_target_pairs={{0,8},{8,0},{16,24},{24,16},{1,9},{9,1},{17,25},{25,17},{2,10},{10... | collective-permute-start | bytes 884744 | tf_op jit(solution)/shard_map/ppermute | solution.py:23
  638.6 30.6 %collective-permute-start.46 = (bf16[256,1024]{1,0:T(8,128)(2,1)}, bf16[256,1024]{1,0:T(8,128)(2,1)}, u32[]{:S(2)}, u32[]{:S(2)}) collective-permute-start(bf16[256,1024]{1,0:T(8,128)(2,1)} %add_convert_fusion.7), channel_id=1, source_target_pairs={{0,8},{8,0},{16,24},{24,16},{1,9},{9,1},{17,25},{25,17},{2,10},{10... | collective-permute-start | bytes 1572872 | tf_op jit(solution)/shard_map/ppermute | solution.py:23
  640.6 30.2 %collective-permute-start.48 = (bf16[256,1280]{1,0:T(8,128)(2,1)S(1)}, bf16[256,1280]{1,0:T(8,128)(2,1)}, u32[]{:S(2)}, u32[]{:S(2)}) collective-permute-start(bf16[256,1280]{1,0:T(8,128)(2,1)S(1)} %add_convert_fusion.1), channel_id=1, source_target_pairs={{0,16},{8,24},{16,0},{24,8},{1,17},{9,25},{17,1},{25,9},{2,18},{10... | collective-permute-start | bytes 1966088 | tf_op jit(solution)/shard_map/ppermute | solution.py:23
  652.4 286.4 %reduce-scatter.14.cloned.1.call-start = ((), (), s32[]{:S(2)}) async-start(), calls=%async_computation.14 | async-start | bytes 8626176 | tf_op jit(solution)/shard_map/reduce_scatter | solution.py:829
  652.4 21.5 %collective-permute-start.54 = (bf16[288,256]{1,0:T(8,128)(2,1)}, bf16[288,256]{1,0:T(8,128)(2,1)}, u32[]{:S(2)}, u32[]{:S(2)}) collective-permute-start(bf16[288,256]{1,0:T(8,128)(2,1)} %slice.500), channel_id=1, source_target_pairs={{0,16},{8,24},{16,0},{24,8},{1,17},{9,25},{17,1},{25,9},{2,18},{10... | collective-permute-start | bytes 442376 | tf_op jit(solution)/shard_map/ppermute | solution.py:23
  674.0 20.8 %collective-permute-start.57 = (bf16[288,1536]{1,0:T(8,128)(2,1)}, bf16[288,1536]{1,0:T(8,128)(2,1)S(1)}, u32[]{:S(2)}, u32[]{:S(2)}) collective-permute-start(bf16[288,1536]{1,0:T(8,128)(2,1)} %reduce-scatter.8.cloned.1.call-done), channel_id=1, source_target_pairs={{0,16},{8,24},{16,0},{24,8},{1,17},{9,25},{17,1},{25,9},{2,18},{10... | collective-permute-start | bytes 2654216 | tf_op jit(solution)/shard_map/ppermute | solution.py:23
  675.1 20.6 %collective-permute-start.56 = (bf16[288,1536]{1,0:T(8,128)(2,1)}, bf16[288,1536]{1,0:T(8,128)(2,1)}, u32[]{:S(2)}, u32[]{:S(2)}) collective-permute-start(bf16[288,1536]{1,0:T(8,128)(2,1)} %reduce-scatter.8.cloned.1.call-done), channel_id=1, source_target_pairs={{0,8},{8,0},{16,24},{24,16},{1,9},{9,1},{17,25},{25,17},{2,10},{10... | collective-permute-start | bytes 2654216 | tf_op jit(solution)/shard_map/ppermute | solution.py:23
  721.1 23.2 %collective-permute-start.61 = (bf16[1024,256]{1,0:T(8,128)(2,1)}, bf16[1024,256]{1,0:T(8,128)(2,1)S(1)}, u32[]{:S(2)}, u32[]{:S(2)}) collective-permute-start(bf16[1024,256]{1,0:T(8,128)(2,1)} %get-tuple-element.72), channel_id=1, source_target_pairs={{0,16},{8,24},{16,0},{24,8},{1,17},{9,25},{17,1},{25,9},{2,18},{10... | collective-permute-start | bytes 1572872 | tf_op jit(solution)/shard_map/ppermute | solution.py:23
  721.9 34.8 %collective-permute-start.66 = (bf16[1024,256]{1,0:T(8,128)(2,1)}, bf16[1024,256]{1,0:T(8,128)(2,1)S(1)}, u32[]{:S(2)}, u32[]{:S(2)}) collective-permute-start(bf16[1024,256]{1,0:T(8,128)(2,1)} %get-tuple-element.78), channel_id=1, source_target_pairs={{0,8},{8,0},{16,24},{24,16},{1,9},{9,1},{17,25},{25,17},{2,10},{10... | collective-permute-start | bytes 1572872 | tf_op jit(solution)/shard_map/ppermute | solution.py:23
  734.4 22.1 %collective-permute-start.63 = (bf16[1024,256]{1,0:T(8,128)(2,1)S(1)}, bf16[1024,256]{1,0:T(8,128)(2,1)S(1)}, u32[]{:S(2)}, u32[]{:S(2)}) collective-permute-start(bf16[1024,256]{1,0:T(8,128)(2,1)S(1)} %add_convert_fusion.6), channel_id=1, source_target_pairs={{0,8},{8,0},{16,24},{24,16},{1,9},{9,1},{17,25},{25,17},{2,10},{10... | collective-permute-start | bytes 1572872 | tf_op jit(solution)/shard_map/ppermute | solution.py:23
  736.2 20.5 %collective-permute-start.65 = (bf16[1024,256]{1,0:T(8,128)(2,1)S(1)}, bf16[1024,256]{1,0:T(8,128)(2,1)S(1)}, u32[]{:S(2)}, u32[]{:S(2)}) collective-permute-start(bf16[1024,256]{1,0:T(8,128)(2,1)S(1)} %add_convert_fusion.4), channel_id=1, source_target_pairs={{0,16},{8,24},{16,0},{24,8},{1,17},{9,25},{17,1},{25,9},{2,18},{10... | collective-permute-start | bytes 1572872 | tf_op jit(solution)/shard_map/ppermute | solution.py:23
  738.6 25.8 %collective-permute-start.68 = (bf16[288,768]{1,0:T(8,128)(2,1)S(1)}, bf16[288,768]{1,0:T(8,128)(2,1)S(1)}, u32[]{:S(2)}, u32[]{:S(2)}) collective-permute-start(bf16[288,768]{1,0:T(8,128)(2,1)S(1)} %slice.507), channel_id=1, source_target_pairs={{0,8},{8,0},{16,24},{24,16},{1,9},{9,1},{17,25},{25,17},{2,10},{10... | collective-permute-start | bytes 1327112 | tf_op jit(solution)/shard_map/ppermute | solution.py:23
  744.3 20.9 %collective-permute-start.67 = (bf16[288,768]{1,0:T(8,128)(2,1)S(1)}, bf16[288,768]{1,0:T(8,128)(2,1)}, u32[]{:S(2)}, u32[]{:S(2)}) collective-permute-start(bf16[288,768]{1,0:T(8,128)(2,1)S(1)} %slice.506), channel_id=1, source_target_pairs={{0,16},{8,24},{16,0},{24,8},{1,17},{9,25},{17,1},{25,9},{2,18},{10... | collective-permute-start | bytes 1327112 | tf_op jit(solution)/shard_map/ppermute | solution.py:23
  765.2 32.2 %collective-permute-start.70 = (bf16[288,2304]{1,0:T(8,128)(2,1)}, bf16[288,2304]{1,0:T(8,128)(2,1)S(1)}, u32[]{:S(2)}, u32[]{:S(2)}) collective-permute-start(bf16[288,2304]{1,0:T(8,128)(2,1)} %reduce-scatter.10.cloned.1.call-done.refs_0_), channel_id=1, source_target_pairs={{0,16},{8,24},{16,0},{24,8},{1,17},{9,25},{17,1},{25,9},{2,18},{10... | collective-permute-start | bytes 3981320 | tf_op jit(solution)/shard_map/ppermute | solution.py:23
  766.7 30.7 %collective-permute-start.69 = (bf16[288,2304]{1,0:T(8,128)(2,1)}, bf16[288,2304]{1,0:T(8,128)(2,1)}, u32[]{:S(2)}, u32[]{:S(2)}) collective-permute-start(bf16[288,2304]{1,0:T(8,128)(2,1)} %reduce-scatter.10.cloned.1.call-done.refs_0_), channel_id=1, source_target_pairs={{0,8},{8,0},{16,24},{24,16},{1,9},{9,1},{17,25},{25,17},{2,10},{10... | collective-permute-start | bytes 3981320 | tf_op jit(solution)/shard_map/ppermute | solution.py:23
  835.8 30.0 %collective-permute-start.96 = (bf16[288,1280]{1,0:T(8,128)(2,1)S(1)}, bf16[288,1280]{1,0:T(8,128)(2,1)S(1)}, u32[]{:S(2)}, u32[]{:S(2)}) collective-permute-start(bf16[288,1280]{1,0:T(8,128)(2,1)S(1)} %slice.535), channel_id=1, source_target_pairs={{0,8},{8,0},{16,24},{24,16},{1,9},{9,1},{17,25},{25,17},{2,10},{10... | collective-permute-start | bytes 2211848 | tf_op jit(solution)/shard_map/ppermute | solution.py:23
  838.9 36.5 %collective-permute-start.71 = (bf16[256,1024]{1,0:T(8,128)(2,1)S(1)}, bf16[256,1024]{1,0:T(8,128)(2,1)S(1)}, u32[]{:S(2)}, u32[]{:S(2)}) collective-permute-start(bf16[256,1024]{1,0:T(8,128)(2,1)S(1)} %get-tuple-element.110), channel_id=1, source_target_pairs={{0,16},{8,24},{16,0},{24,8},{1,17},{9,25},{17,1},{25,9},{2,18},{10... | collective-permute-start | bytes 1572872 | tf_op jit(solution)/shard_map/ppermute | solution.py:23
  845.7 42.7 %collective-permute-start.76 = (bf16[256,1280]{1,0:T(8,128)(2,1)S(1)}, bf16[256,1280]{1,0:T(8,128)(2,1)S(1)}, u32[]{:S(2)}, u32[]{:S(2)}) collective-permute-start(bf16[256,1280]{1,0:T(8,128)(2,1)S(1)} %get-tuple-element.113), channel_id=1, source_target_pairs={{0,8},{8,0},{16,24},{24,16},{1,9},{9,1},{17,25},{25,17},{2,10},{10... | collective-permute-start | bytes 1966088 | tf_op jit(solution)/shard_map/ppermute | solution.py:23
  850.0 38.2 %collective-permute-start.73 = (bf16[256,1024]{1,0:T(8,128)(2,1)S(1)}, bf16[256,1024]{1,0:T(8,128)(2,1)S(1)}, u32[]{:S(2)}, u32[]{:S(2)}) collective-permute-start(bf16[256,1024]{1,0:T(8,128)(2,1)S(1)} %add_convert_fusion.2), channel_id=1, source_target_pairs={{0,8},{8,0},{16,24},{24,16},{1,9},{9,1},{17,25},{25,17},{2,10},{10... | collective-permute-start | bytes 1572872 | tf_op jit(solution)/shard_map/ppermute | solution.py:23
  858.4 30.1 %collective-permute-start.75 = (bf16[256,1280]{1,0:T(8,128)(2,1)S(1)}, bf16[256,1280]{1,0:T(8,128)(2,1)S(1)}, u32[]{:S(2)}, u32[]{:S(2)}) collective-permute-start(bf16[256,1280]{1,0:T(8,128)(2,1)S(1)} %add_convert_fusion), channel_id=1, source_target_pairs={{0,16},{8,24},{16,0},{24,8},{1,17},{9,25},{17,1},{25,9},{2,18},{10... | collective-permute-start | bytes 1966088 | tf_op jit(solution)/shard_map/ppermute | solution.py:23
  897.9 33.0 %collective-permute-start.98 = (bf16[288,2304]{1,0:T(8,128)(2,1)S(1)}, bf16[288,2304]{1,0:T(8,128)(2,1)S(1)}, u32[]{:S(2)}, u32[]{:S(2)}) collective-permute-start(bf16[288,2304]{1,0:T(8,128)(2,1)S(1)} %copy-done.22), channel_id=1, source_target_pairs={{0,16},{8,24},{16,0},{24,8},{1,17},{9,25},{17,1},{25,9},{2,18},{10... | collective-permute-start | bytes 3981320 | tf_op jit(solution)/shard_map/ppermute | solution.py:23
  898.7 34.3 %collective-permute-start.97 = (bf16[288,2304]{1,0:T(8,128)(2,1)S(1)}, bf16[288,2304]{1,0:T(8,128)(2,1)S(1)}, u32[]{:S(2)}, u32[]{:S(2)}) collective-permute-start(bf16[288,2304]{1,0:T(8,128)(2,1)S(1)} %copy-done.22), channel_id=1, source_target_pairs={{0,8},{8,0},{16,24},{24,16},{1,9},{9,1},{17,25},{25,17},{2,10},{10... | collective-permute-start | bytes 3981320 | tf_op jit(solution)/shard_map/ppermute | solution.py:23
  933.8 27.8 %collective-permute-start.99 = (bf16[288,1024]{1,0:T(8,128)(2,1)}, bf16[288,1024]{1,0:T(8,128)(2,1)S(1)}, u32[]{:S(2)}, u32[]{:S(2)}) collective-permute-start(bf16[288,1024]{1,0:T(8,128)(2,1)} %slice.536), channel_id=1, source_target_pairs={{0,16},{8,24},{16,0},{24,8},{1,17},{9,25},{17,1},{25,9},{2,18},{10... | collective-permute-start | bytes 1769480 | tf_op jit(solution)/shard_map/ppermute | solution.py:23
  (173 other events, 1701.2 us)
Sparse Core Ops, SparseCore 0:
  10.5 54.8 all-gather.5
  67.6 32.5 all-gather.7
  102.4 186.6 all-gather.9
  291.1 69.4 all-gather.11
  362.1 40.0 all-gather.13
  501.9 36.0 reduce-scatter.5
  580.7 64.0 reduce-scatter.7
  647.7 95.0 reduce-scatter.9
  745.2 95.3 reduce-scatter.11
  843.4 84.0 reduce-scatter.13
